TPU v7x, 256 devices: a whole 4x4x8 slice. The times are simulated.
256 devices in a mesh: section: 2 (over x_hi), tensor: 2 (over core), dp: 64 (over z, y, x_lo).
Axes of the slice: x: 4 (x_hi: 2, x_lo: 2; x = x_hi * 2 + x_lo), y: 4, z: 8, core: 2. Of those that a mesh axis runs over, the one named last changes fastest.
Arguments:
- layer_input: bfloat16 [2, 16384, 4096], P('section', 'dp', 'tensor')
- other_grad: bfloat16 [2, 16384, 4096], P('section', 'dp', 'tensor'), may hold values from -3 to 3
- head_grad: bfloat16 [2, 16384, 2048], P('section', 'dp', 'tensor')
- lengths: int32 [256], P('dp'), may hold values from 1 to 64, 10922 in all
- proj_weight: bfloat16 [2, 4096, 2048], P('section', None, 'tensor'), may hold values from -0.09375 to 0.09375
- old_momentum: bfloat16 [2, 4096, 2048], P('section', None, 'tensor'), may hold values from -5 to 5
Outputs:
- upstream_grad: bfloat16 [2, 16384, 4096], P('section', 'dp', 'tensor')
- momentum: bfloat16 [2, 4096, 2048], P('section', None, 'tensor')
- worker_error: bfloat16 [2, 64, 4096, 2048], P('section', 'dp', None, 'tensor')
- server_error: float32 [2, 4096, 2048], P('section', 'dp', 'tensor')
Inputs may be any that keep to these rules, and one draw needn't show every extreme that they name: `lengths`: each sequence's length; some sequence has all 64 slots used.
All inputs are finite; a program needn't handle non-finite values. Where the computation divides by a largest or mean magnitude, that divisor is 1e-20 or more. No bound on the sum of `lengths` on one device may be relied on, other than what follows from the above.
Results may differ from a plain program's by a relative error of at most 0.02.
Values may be sent and summed in bfloat16 or wider, within the bound.
No kernel may reach another device: no remote copies, remote signals or barrier semaphores. Data moves between devices by JAX's collectives and lax.ppermute only.
A program may use at most 192 MiB of HBM per device.

v0:
```python
import functools

import jax
import jax.numpy as jnp
from jax import lax
from jax.experimental import pallas as pl
from jax.experimental.pallas import tpu as pltpu
from jax.sharding import Mesh, PartitionSpec as P

momentum_decay = 0.9
saturation = 0.5
epsilon_term = 1e-06

Z, Y, X = 8, 4, 2
SPAN = 64
COLS_Y, COLS_X = 256, 256
F32, BF16 = jnp.float32, jnp.bfloat16
PARAMS = pltpu.CompilerParams(vmem_limit_bytes=32 * 1024 * 1024)
WIDE = pltpu.CompilerParams(vmem_limit_bytes=56 * 1024 * 1024)
ANY = pl.BlockSpec(memory_space=pl.ANY)
VMEM = pl.BlockSpec(memory_space=pltpu.VMEM)


def local_block(x, g, m):
    grad = lax.dot_general(x, g, (((0,), (0,)), ((), ())), preferred_element_type=F32)
    return momentum_decay * m.astype(F32) + (1.0 - momentum_decay) * grad


def local_kernel(where_ref, x_ref, g_ref, m_ref, out_ref, sums_ref):
    local = local_block(x_ref[...], g_ref[...], m_ref[...])
    out_ref[...] = local.astype(BF16)
    rows, cols = local.shape
    per_span = jnp.sum(jnp.abs(local).reshape(rows // SPAN, SPAN, cols), axis=1)
    total = per_span[:, :128]
    for lane in range(128, cols, 128):
        total = total + per_span[:, lane : lane + 128]
    sums_ref[...] = total


def masked_kernel(seqs, where_ref, x_ref, g_ref, m_ref, out_ref, sums_ref, used_ref):
    @pl.when(pl.program_id(0) == 0)
    def _():
        slots = used_ref.shape[0] // seqs
        for seq in range(seqs):
            rows = slice(seq * slots, (seq + 1) * slots)
            grads = g_ref[rows, :].astype(F32)
            slot = lax.broadcasted_iota(jnp.int32, grads.shape, 0)
            used_ref[rows, :] = jnp.where(slot < where_ref[1 + seq], grads, 0.0).astype(BF16)

    local_kernel(where_ref, x_ref, used_ref, m_ref, out_ref, sums_ref)


def local_momentum(x, g, m, first, lengths=None):
    tokens, feats = x.shape
    cols = m.shape[1]
    rows = Y * X * SPAN
    where, kernel = first.reshape(1), local_kernel
    if lengths is not None:
        where = jnp.concatenate([where, lengths])
        kernel = functools.partial(masked_kernel, lengths.shape[0])
    return pl.pallas_call(
        kernel,
        grid_spec=pltpu.PrefetchScalarGridSpec(
            num_scalar_prefetch=1,
            grid=(feats // rows,),
            in_specs=[
                pl.BlockSpec((tokens, rows), lambda i, w: (0, i)),
                pl.BlockSpec((tokens, cols), lambda i, w: (0, 0)),
                pl.BlockSpec((rows, cols), lambda i, w: (w[0] + i, 0)),
            ],
            out_specs=[
                pl.BlockSpec((rows, cols), lambda i, w: (i, 0)),
                pl.BlockSpec((rows // SPAN, 128), lambda i, w: (i, 0)),
            ]
            + ([] if lengths is None else [pl.BlockSpec((tokens, cols), lambda i, w: (0, 0))]),
        ),
        out_shape=[
            pltpu.HBM((feats, cols), BF16),
            jax.ShapeDtypeStruct((feats // SPAN, 128), F32),
        ]
        + ([] if lengths is None else [jax.ShapeDtypeStruct((tokens, cols), BF16)]),
        compiler_params=WIDE,
        cost_estimate=pl.CostEstimate(
            flops=2 * tokens * feats * cols, bytes_accessed=4 * feats * cols, transcendentals=0
        ),
    )(where, x, g, m)


def squash(local, scale):
    slope = scale / (saturation * scale + epsilon_term)
    return jnp.clip(local * slope, -scale, scale).astype(BF16)


def halves(run, own_ref, other_ref):
    half = pl.num_programs(0) // 2
    pl.when(pl.program_id(0) < half)(lambda: run(own_ref))
    pl.when(pl.program_id(0) >= half)(lambda: run(other_ref))


def compress_kernel(where_ref, own_ref, other_ref, s_ref, z_ref, *outs):
    my_y, my_x = where_ref[1], where_ref[2]
    cut = z_ref.shape[1]

    def run(local_ref):
        for k in range(Y * X):
            dy, dx = k // X, k % X
            j = lax.rem(my_y + dy, Y) * X + lax.rem(my_x + dx, X)
            rows = pl.ds(pl.multiple_of(j * SPAN, SPAN), SPAN)
            packed = squash(local_ref[rows, :].astype(F32), s_ref[pl.ds(j, 1), 0:1])
            z_ref[k * SPAN : (k + 1) * SPAN] = packed[:, :cut]
            outs[dy][dx, 0] = packed[:, cut : cut + COLS_Y]
            outs[Y + dx][dy, 0] = packed[:, cut + COLS_Y :]

    halves(run, own_ref, other_ref)


def error_kernel(where_ref, own_ref, other_ref, s_ref, after_ref, err_ref):
    def run(local_ref):
        for j in range(Y * X):
            rows = pl.ds(j * SPAN, SPAN)
            local = local_ref[rows, :].astype(F32)
            packed = squash(local, s_ref[j : j + 1, 0:1])
            err_ref[rows, :] = (local - packed.astype(F32)).astype(BF16)

    halves(run, own_ref, other_ref)


def local_specs(own):
    feats, cols = own.shape
    rows = Y * X * SPAN
    half = feats // rows

    def whole(i, w):
        return lax.rem(w[0] + i, 2 * half)

    in_specs = [
        pl.BlockSpec((rows, cols), lambda i, w: (jnp.minimum(i, half - 1), 0)),
        pl.BlockSpec((rows, cols), lambda i, w: (jnp.maximum(i - half, 0), 0)),
        pl.BlockSpec((rows // SPAN, 128), lambda i, w: (whole(i, w), 0)),
    ]
    return (2 * half,), in_specs, whole


def compress(own, other, scales, where):
    feats, cols = own.shape
    width = 2 * feats
    grid, in_specs, whole = local_specs(own)
    rows, cut = Y * X * SPAN, cols // 2
    return pl.pallas_call(
        compress_kernel,
        grid_spec=pltpu.PrefetchScalarGridSpec(
            num_scalar_prefetch=1,
            grid=grid,
            in_specs=in_specs,
            out_specs=[pl.BlockSpec((rows, cut), lambda i, w: (whole(i, w), 0))]
            + [pl.BlockSpec((X, 1, SPAN, COLS_Y), lambda i, w: (0, whole(i, w), 0, 0))] * Y
            + [pl.BlockSpec((Y, 1, SPAN, COLS_X), lambda i, w: (0, whole(i, w), 0, 0))] * X,
        ),
        out_shape=[pltpu.HBM((width, cut), BF16)]
        + [pltpu.HBM((X, Z, SPAN, COLS_Y), BF16)] * Y
        + [pltpu.HBM((Y, Z, SPAN, COLS_X), BF16)] * X,
        compiler_params=WIDE,
        cost_estimate=pl.CostEstimate(
            flops=8 * width * cols, bytes_accessed=4 * width * cols, transcendentals=0
        ),
    )(where, own, other, scales)


def compression_error(own, other, scales, where, after):
    feats, cols = own.shape
    width = 2 * feats
    grid, in_specs, whole = local_specs(own)
    return pl.pallas_call(
        error_kernel,
        grid_spec=pltpu.PrefetchScalarGridSpec(
            num_scalar_prefetch=1,
            grid=grid,
            in_specs=in_specs + [ANY],
            out_specs=pl.BlockSpec((Y * X * SPAN, cols), lambda i, w: (whole(i, w), 0)),
        ),
        out_shape=pltpu.HBM((width, cols), BF16),
        compiler_params=PARAMS,
        cost_estimate=pl.CostEstimate(
            flops=8 * width * cols, bytes_accessed=4 * width * cols, transcendentals=0
        ),
    )(where, own, other, scales, after)


def first_sums_kernel(*refs):
    kept_ref, given_ref = refs[Y + X + 1 : Y + X + 3]
    kept_ref[...] = added([ref.at[0] for ref in refs[:Y]])
    given_ref[...] = added([ref.at[1] for ref in refs[:Y]]).astype(BF16)
    for k, out_ref in enumerate(refs[Y + X + 3 : -1]):
        out_ref[...] = added([ref.at[k] for ref in refs[Y : Y + X]]).astype(BF16)


def first_sums(y_parts, x_parts, through):
    _, _, span, share_y = y_parts[0].shape
    share_x = x_parts[0].shape[3]
    return pl.pallas_call(
        first_sums_kernel,
        in_specs=[VMEM] * (Y + X) + [ANY],
        out_specs=[VMEM] * (2 + Y) + [ANY],
        out_shape=[
            jax.ShapeDtypeStruct((Z, span, share_y), F32),
            jax.ShapeDtypeStruct((Z, span, share_y), BF16),
        ]
        + [jax.ShapeDtypeStruct((Z, span, share_x), BF16)] * Y
        + [jax.ShapeDtypeStruct(through.shape, through.dtype)],
        input_output_aliases={Y + X: 2 + Y},
        compiler_params=PARAMS,
        cost_estimate=pl.CostEstimate(
            flops=16 * y_parts[0].size, bytes_accessed=20 * y_parts[0].size, transcendentals=0
        ),
    )(*y_parts, *x_parts, through)


def gathered_kernel(all_ref, swapped_ref, *refs):
    pair_ref, ring_ref = refs[-2:]
    pair_ref[0] = all_ref[:, :, :COLS_Y]
    pair_ref[1] = swapped_ref[...]
    ring_ref[0] = all_ref[:, :, COLS_Y:]
    for k in range(1, Y):
        ring_ref[k] = refs[k - 1][...]


def first_gathered(all_z, swapped, others):
    span = all_z.shape[1]
    return pl.pallas_call(
        gathered_kernel,
        in_specs=[VMEM] * (1 + Y),
        out_specs=[VMEM] * 2,
        out_shape=[
            jax.ShapeDtypeStruct((X, Z, span, COLS_Y), BF16),
            jax.ShapeDtypeStruct((Y, Z, span, COLS_X), BF16),
        ],
        compiler_params=PARAMS,
        cost_estimate=pl.CostEstimate(flops=0, bytes_accessed=8 * all_z.size, transcendentals=0),
    )(all_z, swapped, *others)


def added(refs):
    total = refs[0][...].astype(F32)
    for ref in refs[1:]:
        total = total + ref[...].astype(F32)
    return total


def plane_sum_kernel(kept_ref, other_ref, *refs):
    out_ref = refs[-1]
    out_ref[:, :, :COLS_Y] = added([kept_ref, other_ref]).astype(BF16)
    out_ref[:, :, COLS_Y:] = added(refs[:Y]).astype(BF16)


def plane_sum(kept, other, x_parts, after):
    return pl.pallas_call(
        plane_sum_kernel,
        in_specs=[VMEM] * (2 + Y) + [ANY],
        out_specs=VMEM,
        out_shape=jax.ShapeDtypeStruct((Z, SPAN, COLS_Y + COLS_X), BF16),
        compiler_params=PARAMS,
        cost_estimate=pl.CostEstimate(
            flops=8 * kept.size, bytes_accessed=12 * kept.size, transcendentals=0
        ),
    )(kept, other, *x_parts, after)


def y_sum_kernel(own_ref, *refs):
    kept_ref, given_ref = refs[-2:]
    kept_ref[...] = added([own_ref.at[0, 0]] + [ref.at[0] for ref in refs[: Y - 1]])
    given_ref[...] = added([own_ref.at[0, 1]] + [ref.at[1] for ref in refs[: Y - 1]]).astype(BF16)


def y_sum(own, parts, after):
    shape = own.shape[2:]
    return pl.pallas_call(
        y_sum_kernel,
        in_specs=[VMEM] * (1 + len(parts)) + [ANY],
        out_specs=[VMEM] * 2,
        out_shape=[jax.ShapeDtypeStruct(shape, F32), jax.ShapeDtypeStruct(shape, BF16)],
        compiler_params=PARAMS,
        cost_estimate=pl.CostEstimate(flops=own.size, bytes_accessed=3 * own.size, transcendentals=0),
    )(own, *parts, after)


def server_kernel(kept_ref, other_ref, b_ref, out_ref, sums_ref):
    cut = b_ref.shape[2]
    out_ref[:, :cut] = added([kept_ref, other_ref]) / (Z * Y * X)
    out_ref[:, cut:] = added([b_ref.at[k] for k in range(Z)]) / (Z * Y * X)
    sums_ref[...] = jnp.sum(jnp.abs(out_ref[...]), axis=0, keepdims=True)


def server_sum(kept, other, b):
    _, span, cut = b.shape
    return pl.pallas_call(
        server_kernel,
        in_specs=[VMEM] * 3,
        out_specs=[VMEM] * 2,
        out_shape=[jax.ShapeDtypeStruct((span, 2 * cut), F32), jax.ShapeDtypeStruct((1, 2 * cut), F32)],
        compiler_params=PARAMS,
        cost_estimate=pl.CostEstimate(flops=2 * b.size, bytes_accessed=5 * b.size, transcendentals=0),
    )(kept, other, b)


def owned_kernel(averaged_ref, scale_ref, error_ref, a_ref, b_ref):
    averaged = averaged_ref[...]
    owned = squash(averaged, scale_ref[...])
    error_ref[...] = averaged - owned.astype(F32)
    cut = a_ref.shape[1]
    a_ref[...] = owned[:, :cut]
    b_ref[...] = jnp.broadcast_to(owned[None, :, cut:], b_ref.shape)


def owned_momentum(averaged, scale):
    span, cols = averaged.shape
    cut = cols // 2
    return pl.pallas_call(
        owned_kernel,
        in_specs=[VMEM] * 2,
        out_specs=[VMEM] * 3,
        out_shape=[
            jax.ShapeDtypeStruct((span, cols), F32),
            jax.ShapeDtypeStruct((span, cut), BF16),
            jax.ShapeDtypeStruct((Z, span, cut), BF16),
        ],
        compiler_params=PARAMS,
        cost_estimate=pl.CostEstimate(
            flops=8 * averaged.size, bytes_accessed=24 * averaged.size, transcendentals=0
        ),
    )(averaged, scale)


def input_grad_kernel(half, where_ref, g_ref, w_ref, after_ref, own_ref, other_ref):
    step = pl.program_id(0)
    term = lax.dot_general(g_ref[...], w_ref[...], (((1,), (1,)), ((), ())), preferred_element_type=F32)

    @pl.when(step < half)
    def _():
        other_ref[...] = term.astype(BF16)

    @pl.when(step >= half)
    def _():
        own_ref[...] = term


def input_grad(g, weight, first_other, after):
    tokens, cols = g.shape
    width = weight.shape[0]
    rows = min(512, width // 2)
    half = width // 2 // rows
    return pl.pallas_call(
        functools.partial(input_grad_kernel, half),
        grid_spec=pltpu.PrefetchScalarGridSpec(
            num_scalar_prefetch=1,
            grid=(2 * half,),
            in_specs=[
                pl.BlockSpec((tokens, cols), lambda i, w: (0, 0)),
                pl.BlockSpec((rows, cols), lambda i, w: (lax.rem(w[0] * half + i, 2 * half), 0)),
                ANY,
            ],
            out_specs=[
                pl.BlockSpec((tokens, rows), lambda i, w: (0, jnp.maximum(i - half, 0))),
                pl.BlockSpec((tokens, rows), lambda i, w: (0, jnp.minimum(i, half - 1))),
            ],
        ),
        out_shape=[jax.ShapeDtypeStruct((tokens, width // 2), t) for t in (F32, BF16)],
        compiler_params=PARAMS,
        cost_estimate=pl.CostEstimate(
            flops=2 * tokens * width * cols,
            bytes_accessed=2 * width * cols + 4 * tokens * width,
            transcendentals=0,
        ),
    )(first_other.reshape(1), g, weight, after)


def copy_all(pairs, sems):
    copies = [pltpu.make_async_copy(*pair, sems.at[k]) for k, pair in enumerate(pairs)]
    for copy in copies:
        copy.start()
    for copy in copies:
        copy.wait()


def rows_of(where_ref, z, dy, dx):
    j = lax.rem(where_ref[1] + dy, Y) * X + lax.rem(where_ref[2] + dx, X)
    return pl.ds(pl.multiple_of((z * Y * X + j) * SPAN, SPAN), SPAN)


def assemble_a_kernel(where_ref, a_ref, out_ref, sems):
    cut = a_ref.shape[1]
    pairs = []
    for k in range(Z * X * Y):
        rows = rows_of(where_ref, k // (X * Y), k % Y, k // Y % X)
        pairs.append((a_ref.at[pl.ds(k * SPAN, SPAN)], out_ref.at[rows, pl.ds(0, cut)]))
    copy_all(pairs, sems)


def assemble_b_kernel(where_ref, *refs):
    out_ref, sems = refs[-2:]
    cut = out_ref.shape[1] // 2
    pairs = []
    for z in range(Z):
        for dy in range(Y):
            for dx in range(X):
                rows = rows_of(where_ref, z, dy, dx)
                pairs.append((refs[dy].at[dx, z], out_ref.at[rows, pl.ds(cut, COLS_Y)]))
                pairs.append((refs[Y + dx].at[dy, z], out_ref.at[rows, pl.ds(cut + COLS_Y, COLS_X)]))
    copy_all(pairs, sems)


def assemble(where, a, y_parts, x_parts, after):
    width, cut = a.shape

    def call(kernel, count, operands, sources, aliases):
        return pl.pallas_call(
            kernel,
            grid_spec=pltpu.PrefetchScalarGridSpec(
                num_scalar_prefetch=1,
                grid=(1,),
                in_specs=[VMEM] * sources + [ANY] * (len(operands) - sources),
                out_specs=ANY,
                scratch_shapes=[pltpu.SemaphoreType.DMA((count,))],
            ),
            out_shape=pltpu.HBM((width, 2 * cut), BF16),
            input_output_aliases=aliases,
            compiler_params=PARAMS,
            cost_estimate=pl.CostEstimate(flops=0, bytes_accessed=4 * width * cut, transcendentals=0),
        )(where, *operands)

    half = call(assemble_a_kernel, Z * Y * X, [a], 1, {})
    return call(
        assemble_b_kernel, 2 * Z * Y * X, [*y_parts, *x_parts, half, *after], Y + X, {1 + Y + X: 0}
    )


def over_tensor(value):
    return lax.ppermute(value, "tensor", [(0, 1), (1, 0)])


def along(value, axis, steps):
    count = lax.axis_size(axis)
    return lax.ppermute(value, axis, [(i, (i + steps) % count) for i in range(count)])


def exchanged(value, axes):
    return lax.all_to_all(value, axes, split_axis=0, concat_axis=0, tiled=True)


def shards(layer_input, other_grad, head_grad, lengths, proj_weight, old_momentum):
    tensor, my_y, my_x = (lax.axis_index(a).astype(jnp.int32) for a in ("tensor", "y", "x"))
    own, momentum, weight = layer_input[0], old_momentum[0], proj_weight[0]
    width, cols = momentum.shape
    cut = cols // 2
    other = over_tensor(own)

    half = width // 2 // (Y * X * SPAN)
    local_own, own_sums, used_grad = local_momentum(own, head_grad[0], momentum, tensor * half, lengths)
    local_other, other_sums = local_momentum(other, used_grad, momentum, (1 - tensor) * half)
    stacked = jnp.stack([own_sums, other_sums])
    both = jnp.where(tensor == 0, stacked, stacked[::-1]).sum(axis=2).reshape(-1)
    scales = lax.psum(both, "tensor") / (SPAN * cols * 2)
    scales = jnp.broadcast_to(scales[:, None], (scales.shape[0], 128))

    where = jnp.stack([tensor * half, my_y, my_x])
    by_z, *rest = compress(local_own, local_other, scales, where)
    part_z = lax.psum_scatter(by_z, "z", scatter_dimension=0, tiled=True)
    by_y, by_x = rest[:Y], rest[Y:]
    from_y = [by_y[0]] + [along(by_y[k], "y", k) for k in range(1, Y)]
    from_x = [by_x[0], along(by_x[1], "x", 1)]

    share, share_other = input_grad(used_grad, weight, 1 - tensor, from_y[1][0, 0, :16, :128])
    kept, given, *sum_x, share_other = first_sums(from_y, from_x, share_other)
    other_x = along(given, "x", 1)
    from_xy = [sum_x[0]] + [along(sum_x[k], "y", k) for k in range(1, Y)]
    term = other_grad[0].astype(F32) + share + over_tensor(share_other).astype(F32)
    rounded = term.astype(BF16)
    sum_plane = plane_sum(kept, other_x, from_xy, rounded)
    nearer = lax.ppermute(rounded, ("section", "x"), [(2, 1), (3, 0)])
    passed = lax.ppermute(nearer, ("section", "x"), [(0, 1), (1, 0)])
    upstream = (term + passed.astype(F32)).astype(BF16)

    arrived_b = exchanged(sum_plane, "z")
    own_a = part_z.reshape(Y, X, SPAN, cut)
    kept_a, given_a = y_sum(own_a, [along(own_a[k], "y", k) for k in range(1, Y)], nearer)
    averaged, magnitudes = server_sum(kept_a, along(given_a, "x", 1), arrived_b)

    server_scale = lax.psum(jnp.sum(magnitudes), "tensor") / (SPAN * cols * 2)
    server_error, owned_a, owned_b = owned_momentum(averaged, server_scale.reshape(1, 1))

    ring_a = jnp.concatenate([owned_a] + [along(owned_a, "y", -k) for k in range(1, Y)])
    plane_a = jnp.concatenate([ring_a, along(ring_a, "x", 1)])
    all_a = lax.all_gather(plane_a, "z", axis=0, tiled=True)
    all_z = exchanged(owned_b, "z")
    first_y, first_x = all_z[:, :, :COLS_Y], all_z[:, :, COLS_Y:]
    pair_y, ring_x = first_gathered(
        all_z, along(first_y, "x", 1), [along(first_x, "y", -k) for k in range(1, Y)]
    )
    y_parts = [pair_y] + [along(pair_y, "y", -k) for k in range(1, Y)]
    x_parts = [ring_x, along(ring_x, "x", 1)]
    err = compression_error(local_own, local_other, scales, where, pair_y)
    gathered = assemble(where, all_a, y_parts, x_parts, [upstream])
    return (upstream[None], gathered[None], err[None, None], server_error[None])


def solution(mesh):
    sections, groups, _ = mesh.devices.shape
    fine = Mesh(mesh.devices.reshape(sections, groups, Z, Y, X), ("section", "tensor", "z", "y", "x"))
    dp = ("z", "y", "x")
    placed = (
        P("section", dp, "tensor"),
        P("section", dp, "tensor"),
        P("section", dp, "tensor"),
        P(dp),
        P("section", None, "tensor"),
        P("section", None, "tensor"),
    )
    return jax.shard_map(
        shards,
        mesh=fine,
        in_specs=placed,
        out_specs=(
            P("section", dp, "tensor"),
            P("section", None, "tensor"),
            P("section", dp, None, "tensor"),
            P("section", dp, "tensor"),
        ),
        check_vma=False,
    )
```

profile of v0, /device:TPU:4, one launch (start us, length us, event | category | flops | bytes accessed | tf_op | source)
XLA Modules:
  0.0 221.1 jit_solution(9761821485099817983)
XLA Ops:
  8.6 7.1 %shard_map.93 = (bf16[2048,1024]{1,0:T(8,128)(2,1)}, f32[32,128]{1,0:T(8,128)}, bf16[256,1024]{1,0:T(8,128)(2,1)}) custom-call(s32[5]{0:T(128)} %pad_add_fusion.where_ref, bf16[256,2048]{1,0:T(8,128)(2,1)} %bitcast.37, bf16[256,1024]{1,0:T(8,128)(2,1)} %bitcast.38, bf16[4096,1024]{1,0:T(8,128)(2,1)} %bitcast.33), custom_call_target="tpu_custom_call" | custom-call | flops 1073741824 | bytes 8388608 | tf_op jit(solution)/shard_map/pallas_call | solution.py:61
  17.4 6.4 %shard_map.94 = (bf16[2048,1024]{1,0:T(8,128)(2,1)}, f32[32,128]{1,0:T(8,128)}) custom-call(s32[1]{0:T(128)} %bitcast.9.where_ref, bf16[256,2048]{1,0:T(8,128)(2,1)} %copy-done.14, bf16[256,1024]{1,0:T(8,128)(2,1)} %get-tuple-element.34.g_ref, bf16[4096,1024]{1,0:T(8,128)(2,1)} %bitcast.34), custom_call_target="tpu_custom_call" | custom-call | flops 1073741824 | bytes 8388608 | tf_op jit(solution)/shard_map/pallas_call | solution.py:61
  24.6 2.6 %psum.14 = f32[64]{0:T(128)S(1)} all-reduce(f32[64]{0:T(128)S(1)} %reshape.38), channel_id=1, replica_groups=mesh['section'=2,'tensor'=2,'z'=8,'y'=4,'x'=2] {'tensor'}, use_global_device_ids=true, to_apply=%region_1.2 | all-reduce | flops 64 | bytes 512 | tf_op jit(solution)/shard_map/psum | solution.py:461
  27.9 10.7 %shard_map.95 = (bf16[4096,512]{1,0:T(8,128)(2,1)}, bf16[2,8,64,256]{3,2,1,0:T(8,128)(2,1)}, bf16[2,8,64,256]{3,2,1,0:T(8,128)(2,1)}, bf16[2,8,64,256]{3,2,1,0:T...) custom-call(s32[3]{0:T(128)} %pad_add_fusion.1.where_ref, ...), custom_call_target="tpu_custom_call" | custom-call | flops 33554432 | bytes 16777216 | tf_op jit(solution)/shard_map/pallas_call | solution.py:149
  41.5 2.9 %collective-permute-start.2 = (bf16[2,8,64,256]{3,2,1,0:T(8,128)(2,1)}, bf16[2,8,64,256]{3,2,1,0:T(8,128)(2,1)S(1)}, u32[]{:S(2)}, u32[]{:S(2)}) collective-permute-start(bf16[2,8,64,256]{3,2,1,0:T(8,128)(2,1)} %get-tuple-element.42), channel_id=1, source_target_pairs={{0,4},{2,6},{4,0},{6,2},{1,5},{3,7},{5,1},{7,3},{8,12},{10,14},{12... | collective-permute-start | bytes 1572872 | tf_op jit(solution)/shard_map/ppermute | solution.py:442
  45.7 9.4 %collective-permute-done.1.refs_1_ = bf16[2,8,64,256]{3,2,1,0:T(8,128)(2,1)S(1)} collective-permute-done((bf16[2,8,64,256]{3,2,1,0:T(8,128)(2,1)S(1)}, bf16[2,8,64,256]{3,2,1,0:T(8,128)(2,1)S(1)}, u32[]{:S(2)}, u32[]{:S(2)}) %collective-permute-start.1) | collective-permute-done | bytes 524320 | tf_op jit(solution)/shard_map/ppermute | solution.py:442
  55.1 3.4 %copy-done.2 = bf16[1,4096,1024]{2,1,0:T(8,128)(2,1)S(1)} copy-done((bf16[1,4096,1024]{2,1,0:T(8,128)(2,1)S(1)}, bf16[1,4096,1024]{2,1,0:T(8,128)(2,1)}, u32[]{:S(2)}) %copy-start.2) | copy-done | bytes 8388632
  58.5 4.5 %shard_map.96 = (f32[256,2048]{1,0:T(8,128)S(1)}, bf16[256,2048]{1,0:T(8,128)(2,1)S(1)}) custom-call(s32[1]{0:T(128)} %bitcast.1.where_ref, bf16[256,1024]{1,0:T(8,128)(2,1)S(1)} %copy-done.5, bf16[4096,1024]{1,0:T(8,128)(2,1)S(1)} %bitcast.29, bf16[16,128]{1,0:T(8,128)(2,1)S(1)} %slice_bitcast_fusion.after_ref), custom_call_target="tpu_custom_call" | custom-call | flops 2147483648 | bytes 12582912 | tf_op jit(solution)/shard_map/pallas_call | solution.py:351
  62.9 4.6 %collective-permute-done.2.refs_2_ = bf16[2,8,64,256]{3,2,1,0:T(8,128)(2,1)S(1)} collective-permute-done((bf16[2,8,64,256]{3,2,1,0:T(8,128)(2,1)}, bf16[2,8,64,256]{3,2,1,0:T(8,128)(2,1)S(1)}, u32[]{:S(2)}, u32[]{:S(2)}) %collective-permute-start.2) | collective-permute-done | bytes 524320 | tf_op jit(solution)/shard_map/ppermute | solution.py:442
  70.5 6.6 %collective-permute-start.14 = (bf16[8,64,256]{2,1,0:T(8,128)(2,1)S(1)}, bf16[8,64,256]{2,1,0:T(8,128)(2,1)S(1)}, u32[]{:S(2)}, u32[]{:S(2)}) collective-permute-start(bf16[8,64,256]{2,1,0:T(8,128)(2,1)S(1)} %get-tuple-element.55), channel_id=1, source_target_pairs={{0,4},{2,6},{4,0},{6,2},{1,5},{3,7},{5,1},{7,3},{8,12},{10,14},{12... | collective-permute-start | bytes 786440 | tf_op jit(solution)/shard_map/ppermute | solution.py:442
  77.1 2.5 %collective-permute-start.15 = (bf16[8,64,256]{2,1,0:T(8,128)(2,1)S(1)}, bf16[8,64,256]{2,1,0:T(8,128)(2,1)S(1)}, u32[]{:S(2)}, u32[]{:S(2)}) collective-permute-start(bf16[8,64,256]{2,1,0:T(8,128)(2,1)S(1)} %get-tuple-element.56), channel_id=1, source_target_pairs={{0,6},{2,0},{4,2},{6,4},{1,7},{3,1},{5,3},{7,5},{8,14},{10,8},{12,... | collective-permute-start | bytes 786440 | tf_op jit(solution)/shard_map/ppermute | solution.py:442
  80.6 4.2 %collective-permute-start.6 = (bf16[256,2048]{1,0:T(8,128)(2,1)S(1)}, bf16[256,2048]{1,0:T(8,128)(2,1)}, u32[]{:S(2)}, u32[]{:S(2)}) collective-permute-start(bf16[256,2048]{1,0:T(8,128)(2,1)S(1)} %fusion.1.refs_4_), channel_id=1, source_target_pairs={{128,1},{129,0},{130,3},{131,2},{132,5},{133,4},{134,7},{135,6},{1... | collective-permute-start | bytes 3145736 | tf_op jit(solution)/shard_map/ppermute | solution.py:478
  84.8 4.6 %collective-permute-done.14.refs_2_ = bf16[8,64,256]{2,1,0:T(8,128)(2,1)S(1)} collective-permute-done((bf16[8,64,256]{2,1,0:T(8,128)(2,1)S(1)}, bf16[8,64,256]{2,1,0:T(8,128)(2,1)S(1)}, u32[]{:S(2)}, u32[]{:S(2)}) %collective-permute-start.14) | collective-permute-done | bytes 262176 | tf_op jit(solution)/shard_map/ppermute | solution.py:442
  90.4 9.4 %all-to-all-start = ((bf16[8,64,512]{2,1,0:T(8,128)(2,1)}), bf16[8,64,512]{2,1,0:T(8,128)(2,1)}, u32[]{:S(2)}, u32[]{:S(2)}) async-start(bf16[8,64,512]{2,1,0:T(8,128)(2,1)} %copy-done.6), calls=%async_computation.1 | async-start | bytes 1048576 | tf_op jit(solution)/shard_map/all_to_all | solution.py:446
  100.9 3.7 %collective-permute-start.9 = (bf16[2,64,512]{2,1,0:T(8,128)(2,1)S(1)}, bf16[2,64,512]{2,1,0:T(8,128)(2,1)S(1)}, u32[]{:S(2)}, u32[]{:S(2)}) collective-permute-start(bf16[2,64,512]{2,1,0:T(8,128)(2,1)S(1)} %bitcast.41), channel_id=1, source_target_pairs={{0,4},{2,6},{4,0},{6,2},{1,5},{3,7},{5,1},{7,3},{8,12},{10,14},{12... | collective-permute-start | bytes 393224 | tf_op jit(solution)/shard_map/ppermute | solution.py:442
  113.3 3.9 %all-to-all-done.b_ref = bf16[8,64,512]{2,1,0:T(8,128)(2,1)} async-done(((bf16[8,64,512]{2,1,0:T(8,128)(2,1)}), bf16[8,64,512]{2,1,0:T(8,128)(2,1)}, u32[]{:S(2)}, u32[]{:S(2)}) %all-to-all-start) | async-done | bytes 524320 | tf_op jit(solution)/shard_map/all_to_all | solution.py:446
  119.0 3.1 %psum.15 = f32[]{:T(128)} all-reduce(f32[]{:T(128)} %reduce_sum.19), channel_id=1, replica_groups=mesh['section'=2,'tensor'=2,'z'=8,'y'=4,'x'=2] {'tensor'}, use_global_device_ids=true, to_apply=%region_4.5 | all-reduce | flops 1 | bytes 8 | tf_op jit(solution)/shard_map/psum | solution.py:487
  124.6 3.4 %collective-permute-start.25 = (bf16[64,512]{1,0:T(8,128)(2,1)S(1)}, bf16[64,512]{1,0:T(8,128)(2,1)S(1)}, u32[]{:S(2)}, u32[]{:S(2)}) collective-permute-start(bf16[64,512]{1,0:T(8,128)(2,1)S(1)} %get-tuple-element.62), channel_id=1, source_target_pairs={{0,4},{2,6},{4,0},{6,2},{1,5},{3,7},{5,1},{7,3},{8,12},{10,14},{12... | collective-permute-start | bytes 196616 | tf_op jit(solution)/shard_map/ppermute | solution.py:442
  129.5 2.1 collective-permute-done.25
  133.3 6.1 %collective-permute-done.27 = bf16[256,512]{1,0:T(8,128)(2,1)S(1)} collective-permute-done((bf16[256,512]{1,0:T(8,128)(2,1)S(1)}, bf16[256,512]{1,0:T(8,128)(2,1)S(1)}, u32[]{:S(2)}, u32[]{:S(2)}) %collective-permute-start.27) | collective-permute-done | bytes 262176 | tf_op jit(solution)/shard_map/ppermute | solution.py:442
  140.3 5.8 %all-to-all-start.1 = ((bf16[8,64,512]{2,1,0:T(8,128)(2,1)}), bf16[8,64,512]{2,1,0:T(8,128)(2,1)S(1)}, u32[]{:S(2)}, u32[]{:S(2)}) async-start(bf16[8,64,512]{2,1,0:T(8,128)(2,1)} %get-tuple-element.59), calls=%async_computation.2 | async-start | bytes 1048576 | tf_op jit(solution)/shard_map/all_to_all | solution.py:446
  147.7 18.5 %all-to-all-done.1.all_ref = bf16[8,64,512]{2,1,0:T(8,128)(2,1)S(1)} async-done(((bf16[8,64,512]{2,1,0:T(8,128)(2,1)}), bf16[8,64,512]{2,1,0:T(8,128)(2,1)S(1)}, u32[]{:S(2)}, u32[]{:S(2)}) %all-to-all-start.1) | async-done | bytes 524320 | tf_op jit(solution)/shard_map/all_to_all | solution.py:446
  167.9 3.2 %collective-permute-start.18 = (bf16[8,64,256]{2,1,0:T(8,128)(2,1)S(1)}, bf16[8,64,256]{2,1,0:T(8,128)(2,1)S(1)}, u32[]{:S(2)}, u32[]{:S(2)}) collective-permute-start(bf16[8,64,256]{2,1,0:T(8,128)(2,1)S(1)} %get-tuple-element.64), channel_id=1, source_target_pairs={{0,4},{2,6},{4,0},{6,2},{1,5},{3,7},{5,1},{7,3},{8,12},{10,14},{12... | collective-permute-start | bytes 786440 | tf_op jit(solution)/shard_map/ppermute | solution.py:442
  174.6 4.7 %collective-permute-done.18.refs_1_ = bf16[8,64,256]{2,1,0:T(8,128)(2,1)S(1)} collective-permute-done((bf16[8,64,256]{2,1,0:T(8,128)(2,1)S(1)}, bf16[8,64,256]{2,1,0:T(8,128)(2,1)S(1)}, u32[]{:S(2)}, u32[]{:S(2)}) %collective-permute-start.18) | collective-permute-done | bytes 262176 | tf_op jit(solution)/shard_map/ppermute | solution.py:442
  179.3 4.4 %collective-permute-done.17.refs_0_ = bf16[8,64,256]{2,1,0:T(8,128)(2,1)S(1)} collective-permute-done((bf16[8,64,256]{2,1,0:T(8,128)(2,1)S(1)}, bf16[8,64,256]{2,1,0:T(8,128)(2,1)S(1)}, u32[]{:S(2)}, u32[]{:S(2)}) %collective-permute-start.17) | collective-permute-done | bytes 262176 | tf_op jit(solution)/shard_map/ppermute | solution.py:442
  185.0 2.4 %collective-permute-start.23 = (bf16[4,8,64,256]{3,2,1,0:T(8,128)(2,1)}, bf16[4,8,64,256]{3,2,1,0:T(8,128)(2,1)}, u32[]{:S(2)}, u32[]{:S(2)}) collective-permute-start(bf16[4,8,64,256]{3,2,1,0:T(8,128)(2,1)} %get-tuple-element.61.refs_4_), channel_id=1, source_target_pairs={{0,1},{1,0},{2,3},{3,2},{4,5},{5,4},{6,7},{7,6},{8,9},{9,8},{10,11... | collective-permute-start | bytes 3145736 | tf_op jit(solution)/shard_map/ppermute | solution.py:442
  188.0 4.5 %collective-permute-start.21 = (bf16[2,8,64,256]{3,2,1,0:T(8,128)(2,1)}, bf16[2,8,64,256]{3,2,1,0:T(8,128)(2,1)}, u32[]{:S(2)}, u32[]{:S(2)}) collective-permute-start(bf16[2,8,64,256]{3,2,1,0:T(8,128)(2,1)} %get-tuple-element.60.refs_0_.after_ref), channel_id=1, source_target_pairs={{0,4},{2,6},{4,0},{6,2},{1,5},{3,7},{5,1},{7,3},{8,12},{10,14},{12... | collective-permute-start | bytes 1572872 | tf_op jit(solution)/shard_map/ppermute | solution.py:442
  192.5 2.5 %add_convert_fusion.refs_7_ = bf16[256,2048]{1,0:T(8,128)(2,1)S(1)} fusion(bf16[256,2048]{1,0:T(8,128)(2,1)} %collective-permute-done.7, bf16[256,2048]{1,0:T(8,128)(2,1)} %copy-done.13, f32[256,2048]{1,0:T(8,128)S(1)} %get-tuple-element.40, bf16[1,256,2048]{2,1,0:T(8,128)(2,1)} %param.7), kind=kLoop, calls=%fused_computation.2 | loop fusion | flops 3670016 | bytes 6291456 | tf_op jit(solution)/shard_map/convert_element_type | solution.py:480
  195.0 8.1 %shard_map.105 = bf16[4096,1024]{1,0:T(8,128)(2,1)} custom-call(s32[3]{0:T(128)S(1)} %copy-done.11, bf16[2048,1024]{1,0:T(8,128)(2,1)S(1)} %copy-done, bf16[2048,1024]{1,0:T(8,128)(2,1)S(1)} %copy-done.1, f32[64,128]{1,0:T(8,128)S(1)} %copy-done.10, bf16[2,8,64,256]{3,2,1,0:T(8,128)(2,1)} %get-tuple-element.60.refs_0_.after_ref), custom_call_target="tpu_custom_call" | custom-call | flops 33554432 | bytes 16777216 | tf_op jit(solution)/shard_map/pallas_call | solution.py:173
  203.1 2.2 copy-done.3
  205.3 3.1 %shard_map.103.refs_6_ = bf16[4096,1024]{1,0:T(8,128)(2,1)} custom-call(s32[3]{0:T(128)S(1)} %copy-done.11, bf16[4096,512]{1,0:T(8,128)(2,1)S(1)} %copy-done.3), custom_call_target="tpu_custom_call" | custom-call | bytes 8388608 | tf_op jit(solution)/shard_map/pallas_call | solution.py:415
  208.4 5.8 %shard_map.104 = bf16[4096,1024]{1,0:T(8,128)(2,1)} custom-call(s32[3]{0:T(128)S(1)} %copy-done.11, bf16[2,8,64,256]{3,2,1,0:T(8,128)(2,1)} %get-tuple-element.60.refs_0_.after_ref, bf16[2,8,64,256]{3,2,1,0:T(8,128)(2,1)} %collective-permute-done.20.refs_1_, bf16[2,8,64,256]{3,2,1,0:T(8,128)(2,1)} %collective-permute-done.21.refs_2_, ...), custom_call_target="tpu_custom_call", output_to_operand_aliasing={{}: (7, {})} | custom-call | bytes 8388608 | tf_op jit(solution)/shard_map/pallas_call | solution.py:415
  (106 shorter events, 40.1 us)
Async XLA Ops:
  7.2 92.7 %reduce-scatter.2.cloned.1.call-start = ((), (), s32[]{:S(2)}) async-start(), calls=%async_computation.3 | async-start | bytes 4718592 | tf_op jit(solution)/shard_map/reduce_scatter | solution.py:466
  7.2 9.2 %collective-permute-start = (bf16[256,2048]{1,0:T(8,128)(2,1)}, bf16[256,2048]{1,0:T(8,128)(2,1)S(1)}, u32[]{:S(2)}, u32[]{:S(2)}) collective-permute-start(bf16[256,2048]{1,0:T(8,128)(2,1)} %bitcast.36), channel_id=1, source_target_pairs={{0,64},{64,0},{1,65},{65,1},{2,66},{66,2},{3,67},{67,3},{4,68},{68... | collective-permute-start | bytes 3145736 | tf_op jit(solution)/shard_map/ppermute | solution.py:437
  38.6 28.9 %collective-permute-start.4 = (bf16[4,8,64,256]{3,2,1,0:T(8,128)(2,1)}, bf16[4,8,64,256]{3,2,1,0:T(8,128)(2,1)S(1)}, u32[]{:S(2)}, u32[]{:S(2)}) collective-permute-start(bf16[4,8,64,256]{3,2,1,0:T(8,128)(2,1)} %get-tuple-element.45), channel_id=1, source_target_pairs={{0,1},{1,0},{2,3},{3,2},{4,5},{5,4},{6,7},{7,6},{8,9},{9,8},{10,11... | collective-permute-start | bytes 3145736 | tf_op jit(solution)/shard_map/ppermute | solution.py:442
  39.9 15.2 %collective-permute-start.1 = (bf16[2,8,64,256]{3,2,1,0:T(8,128)(2,1)S(1)}, bf16[2,8,64,256]{3,2,1,0:T(8,128)(2,1)S(1)}, u32[]{:S(2)}, u32[]{:S(2)}) collective-permute-start(bf16[2,8,64,256]{3,2,1,0:T(8,128)(2,1)S(1)} %copy-done.18), channel_id=1, source_target_pairs={{0,2},{2,4},{4,6},{6,0},{1,3},{3,5},{5,7},{7,1},{8,10},{10,12},{12... | collective-permute-start | bytes 1572872 | tf_op jit(solution)/shard_map/ppermute | solution.py:442
  41.5 26.0 %collective-permute-start.2 = (bf16[2,8,64,256]{3,2,1,0:T(8,128)(2,1)}, bf16[2,8,64,256]{3,2,1,0:T(8,128)(2,1)S(1)}, u32[]{:S(2)}, u32[]{:S(2)}) collective-permute-start(bf16[2,8,64,256]{3,2,1,0:T(8,128)(2,1)} %get-tuple-element.42), channel_id=1, source_target_pairs={{0,4},{2,6},{4,0},{6,2},{1,5},{3,7},{5,1},{7,3},{8,12},{10,14},{12... | collective-permute-start | bytes 1572872 | tf_op jit(solution)/shard_map/ppermute | solution.py:442
  44.4 23.1 %collective-permute-start.3 = (bf16[2,8,64,256]{3,2,1,0:T(8,128)(2,1)S(1)}, bf16[2,8,64,256]{3,2,1,0:T(8,128)(2,1)S(1)}, u32[]{:S(2)}, u32[]{:S(2)}) collective-permute-start(bf16[2,8,64,256]{3,2,1,0:T(8,128)(2,1)S(1)} %copy-done.17), channel_id=1, source_target_pairs={{0,6},{2,0},{4,2},{6,4},{1,7},{3,1},{5,3},{7,5},{8,14},{10,8},{12,... | collective-permute-start | bytes 1572872 | tf_op jit(solution)/shard_map/ppermute | solution.py:442
  68.0 11.6 %collective-permute-start.5 = (bf16[256,2048]{1,0:T(8,128)(2,1)S(1)}, bf16[256,2048]{1,0:T(8,128)(2,1)S(1)}, u32[]{:S(2)}, u32[]{:S(2)}) collective-permute-start(bf16[256,2048]{1,0:T(8,128)(2,1)S(1)} %get-tuple-element.47), channel_id=1, source_target_pairs={{0,64},{64,0},{1,65},{65,1},{2,66},{66,2},{3,67},{67,3},{4,68},{68... | collective-permute-start | bytes 3145736 | tf_op jit(solution)/shard_map/ppermute | solution.py:437
  68.1 16.7 %collective-permute-start.12 = (bf16[8,64,256]{2,1,0:T(8,128)(2,1)S(1)}, bf16[8,64,256]{2,1,0:T(8,128)(2,1)S(1)}, u32[]{:S(2)}, u32[]{:S(2)}) collective-permute-start(bf16[8,64,256]{2,1,0:T(8,128)(2,1)S(1)} %get-tuple-element.52), channel_id=1, source_target_pairs={{0,1},{1,0},{2,3},{3,2},{4,5},{5,4},{6,7},{7,6},{8,9},{9,8},{10,11... | collective-permute-start | bytes 786440 | tf_op jit(solution)/shard_map/ppermute | solution.py:442
  69.4 15.5 %collective-permute-start.13 = (bf16[8,64,256]{2,1,0:T(8,128)(2,1)S(1)}, bf16[8,64,256]{2,1,0:T(8,128)(2,1)S(1)}, u32[]{:S(2)}, u32[]{:S(2)}) collective-permute-start(bf16[8,64,256]{2,1,0:T(8,128)(2,1)S(1)} %get-tuple-element.54), channel_id=1, source_target_pairs={{0,2},{2,4},{4,6},{6,0},{1,3},{3,5},{5,7},{7,1},{8,10},{10,12},{12... | collective-permute-start | bytes 786440 | tf_op jit(solution)/shard_map/ppermute | solution.py:442
  70.5 18.9 %collective-permute-start.14 = (bf16[8,64,256]{2,1,0:T(8,128)(2,1)S(1)}, bf16[8,64,256]{2,1,0:T(8,128)(2,1)S(1)}, u32[]{:S(2)}, u32[]{:S(2)}) collective-permute-start(bf16[8,64,256]{2,1,0:T(8,128)(2,1)S(1)} %get-tuple-element.55), channel_id=1, source_target_pairs={{0,4},{2,6},{4,0},{6,2},{1,5},{3,7},{5,1},{7,3},{8,12},{10,14},{12... | collective-permute-start | bytes 786440 | tf_op jit(solution)/shard_map/ppermute | solution.py:442
  77.1 12.3 %collective-permute-start.15 = (bf16[8,64,256]{2,1,0:T(8,128)(2,1)S(1)}, bf16[8,64,256]{2,1,0:T(8,128)(2,1)S(1)}, u32[]{:S(2)}, u32[]{:S(2)}) collective-permute-start(bf16[8,64,256]{2,1,0:T(8,128)(2,1)S(1)} %get-tuple-element.56), channel_id=1, source_target_pairs={{0,6},{2,0},{4,2},{6,4},{1,7},{3,1},{5,3},{7,5},{8,14},{10,8},{12,... | collective-permute-start | bytes 786440 | tf_op jit(solution)/shard_map/ppermute | solution.py:442
  80.6 26.0 %collective-permute-start.6 = (bf16[256,2048]{1,0:T(8,128)(2,1)S(1)}, bf16[256,2048]{1,0:T(8,128)(2,1)}, u32[]{:S(2)}, u32[]{:S(2)}) collective-permute-start(bf16[256,2048]{1,0:T(8,128)(2,1)S(1)} %fusion.1.refs_4_), channel_id=1, source_target_pairs={{128,1},{129,0},{130,3},{131,2},{132,5},{133,4},{134,7},{135,6},{1... | collective-permute-start | bytes 3145736 | tf_op jit(solution)/shard_map/ppermute | solution.py:478
  90.4 26.8 %all-to-all-start = ((bf16[8,64,512]{2,1,0:T(8,128)(2,1)}), bf16[8,64,512]{2,1,0:T(8,128)(2,1)}, u32[]{:S(2)}, u32[]{:S(2)}) async-start(bf16[8,64,512]{2,1,0:T(8,128)(2,1)} %copy-done.6), calls=%async_computation.1 | async-start | bytes 1048576 | tf_op jit(solution)/shard_map/all_to_all | solution.py:446
  99.8 103.3 %all-gather.2.cloned.1.call-start = ((), (), s32[]{:S(2)}) async-start(), calls=%async_computation.4 | async-start | bytes 4718592 | tf_op jit(solution)/shard_map/all_gather | solution.py:492
  100.9 7.7 %collective-permute-start.9 = (bf16[2,64,512]{2,1,0:T(8,128)(2,1)S(1)}, bf16[2,64,512]{2,1,0:T(8,128)(2,1)S(1)}, u32[]{:S(2)}, u32[]{:S(2)}) collective-permute-start(bf16[2,64,512]{2,1,0:T(8,128)(2,1)S(1)} %bitcast.41), channel_id=1, source_target_pairs={{0,4},{2,6},{4,0},{6,2},{1,5},{3,7},{5,1},{7,3},{8,12},{10,14},{12... | collective-permute-start | bytes 393224 | tf_op jit(solution)/shard_map/ppermute | solution.py:442
  104.6 5.7 %collective-permute-start.10 = (bf16[2,64,512]{2,1,0:T(8,128)(2,1)S(1)}, bf16[2,64,512]{2,1,0:T(8,128)(2,1)S(1)}, u32[]{:S(2)}, u32[]{:S(2)}) collective-permute-start(bf16[2,64,512]{2,1,0:T(8,128)(2,1)S(1)} %bitcast.40), channel_id=1, source_target_pairs={{0,6},{2,0},{4,2},{6,4},{1,7},{3,1},{5,3},{7,5},{8,14},{10,8},{12,... | collective-permute-start | bytes 393224 | tf_op jit(solution)/shard_map/ppermute | solution.py:442
  105.1 6.2 %collective-permute-start.8 = (bf16[2,64,512]{2,1,0:T(8,128)(2,1)S(1)}, bf16[2,64,512]{2,1,0:T(8,128)(2,1)S(1)}, u32[]{:S(2)}, u32[]{:S(2)}) collective-permute-start(bf16[2,64,512]{2,1,0:T(8,128)(2,1)S(1)} %bitcast.39), channel_id=1, source_target_pairs={{0,2},{2,4},{4,6},{6,0},{1,3},{3,5},{5,7},{7,1},{8,10},{10,12},{12... | collective-permute-start | bytes 393224 | tf_op jit(solution)/shard_map/ppermute | solution.py:442
  112.4 4.8 %collective-permute-start.11 = (bf16[64,512]{1,0:T(8,128)(2,1)S(1)}, bf16[64,512]{1,0:T(8,128)(2,1)S(1)}, u32[]{:S(2)}, u32[]{:S(2)}) collective-permute-start(bf16[64,512]{1,0:T(8,128)(2,1)S(1)} %get-tuple-element.50), channel_id=1, source_target_pairs={{0,1},{1,0},{2,3},{3,2},{4,5},{5,4},{6,7},{7,6},{8,9},{9,8},{10,11... | collective-permute-start | bytes 196616 | tf_op jit(solution)/shard_map/ppermute | solution.py:442
  123.8 5.7 %collective-permute-start.26 = (bf16[64,512]{1,0:T(8,128)(2,1)S(1)}, bf16[64,512]{1,0:T(8,128)(2,1)S(1)}, u32[]{:S(2)}, u32[]{:S(2)}) collective-permute-start(bf16[64,512]{1,0:T(8,128)(2,1)S(1)} %get-tuple-element.62), channel_id=1, source_target_pairs={{0,2},{2,4},{4,6},{6,0},{1,3},{3,5},{5,7},{7,1},{8,10},{10,12},{12... | collective-permute-start | bytes 196616 | tf_op jit(solution)/shard_map/ppermute | solution.py:442
  124.6 6.9 %collective-permute-start.25 = (bf16[64,512]{1,0:T(8,128)(2,1)S(1)}, bf16[64,512]{1,0:T(8,128)(2,1)S(1)}, u32[]{:S(2)}, u32[]{:S(2)}) collective-permute-start(bf16[64,512]{1,0:T(8,128)(2,1)S(1)} %get-tuple-element.62), channel_id=1, source_target_pairs={{0,4},{2,6},{4,0},{6,2},{1,5},{3,7},{5,1},{7,3},{8,12},{10,14},{12... | collective-permute-start | bytes 196616 | tf_op jit(solution)/shard_map/ppermute | solution.py:442
  128.0 4.3 %collective-permute-start.24 = (bf16[64,512]{1,0:T(8,128)(2,1)S(1)}, bf16[64,512]{1,0:T(8,128)(2,1)S(1)}, u32[]{:S(2)}, u32[]{:S(2)}) collective-permute-start(bf16[64,512]{1,0:T(8,128)(2,1)S(1)} %get-tuple-element.62), channel_id=1, source_target_pairs={{0,6},{2,0},{4,2},{6,4},{1,7},{3,1},{5,3},{7,5},{8,14},{10,8},{12,... | collective-permute-start | bytes 196616 | tf_op jit(solution)/shard_map/ppermute | solution.py:442
  132.3 7.0 %collective-permute-start.27 = (bf16[256,512]{1,0:T(8,128)(2,1)S(1)}, bf16[256,512]{1,0:T(8,128)(2,1)S(1)}, u32[]{:S(2)}, u32[]{:S(2)}) collective-permute-start(bf16[256,512]{1,0:T(8,128)(2,1)S(1)} %pad_maximum_fusion), channel_id=1, source_target_pairs={{0,1},{1,0},{2,3},{3,2},{4,5},{5,4},{6,7},{7,6},{8,9},{9,8},{10,11... | collective-permute-start | bytes 786440 | tf_op jit(solution)/shard_map/ppermute | solution.py:442
  140.3 26.0 %all-to-all-start.1 = ((bf16[8,64,512]{2,1,0:T(8,128)(2,1)}), bf16[8,64,512]{2,1,0:T(8,128)(2,1)S(1)}, u32[]{:S(2)}, u32[]{:S(2)}) async-start(bf16[8,64,512]{2,1,0:T(8,128)(2,1)} %get-tuple-element.59), calls=%async_computation.2 | async-start | bytes 1048576 | tf_op jit(solution)/shard_map/all_to_all | solution.py:446
  146.0 46.5 %collective-permute-start.7 = (bf16[256,2048]{1,0:T(8,128)(2,1)}, bf16[256,2048]{1,0:T(8,128)(2,1)}, u32[]{:S(2)}, u32[]{:S(2)}) collective-permute-start(bf16[256,2048]{1,0:T(8,128)(2,1)} %collective-permute-done.6.refs_3_), channel_id=1, source_target_pairs={{0,1},{1,0},{2,3},{3,2},{4,5},{5,4},{6,7},{7,6},{8,9},{9,8},{10,11... | collective-permute-start | bytes 3145736 | tf_op jit(solution)/shard_map/ppermute | solution.py:479
  166.3 6.5 %collective-permute-start.16 = (bf16[8,64,256]{2,1,0:T(8,128)(2,1)S(1)}, bf16[8,64,256]{2,1,0:T(8,128)(2,1)S(1)}, u32[]{:S(2)}, u32[]{:S(2)}) collective-permute-start(bf16[8,64,256]{2,1,0:T(8,128)(2,1)S(1)} %get-tuple-element.65), channel_id=1, source_target_pairs={{0,1},{1,0},{2,3},{3,2},{4,5},{5,4},{6,7},{7,6},{8,9},{9,8},{10,11... | collective-permute-start | bytes 786440 | tf_op jit(solution)/shard_map/ppermute | solution.py:442
  167.0 7.6 %collective-permute-start.19 = (bf16[8,64,256]{2,1,0:T(8,128)(2,1)S(1)}, bf16[8,64,256]{2,1,0:T(8,128)(2,1)S(1)}, u32[]{:S(2)}, u32[]{:S(2)}) collective-permute-start(bf16[8,64,256]{2,1,0:T(8,128)(2,1)S(1)} %get-tuple-element.64), channel_id=1, source_target_pairs={{0,2},{2,4},{4,6},{6,0},{1,3},{3,5},{5,7},{7,1},{8,10},{10,12},{12... | collective-permute-start | bytes 786440 | tf_op jit(solution)/shard_map/ppermute | solution.py:442
  167.9 11.4 %collective-permute-start.18 = (bf16[8,64,256]{2,1,0:T(8,128)(2,1)S(1)}, bf16[8,64,256]{2,1,0:T(8,128)(2,1)S(1)}, u32[]{:S(2)}, u32[]{:S(2)}) collective-permute-start(bf16[8,64,256]{2,1,0:T(8,128)(2,1)S(1)} %get-tuple-element.64), channel_id=1, source_target_pairs={{0,4},{2,6},{4,0},{6,2},{1,5},{3,7},{5,1},{7,3},{8,12},{10,14},{12... | collective-permute-start | bytes 786440 | tf_op jit(solution)/shard_map/ppermute | solution.py:442
  171.1 12.6 %collective-permute-start.17 = (bf16[8,64,256]{2,1,0:T(8,128)(2,1)S(1)}, bf16[8,64,256]{2,1,0:T(8,128)(2,1)S(1)}, u32[]{:S(2)}, u32[]{:S(2)}) collective-permute-start(bf16[8,64,256]{2,1,0:T(8,128)(2,1)S(1)} %get-tuple-element.64), channel_id=1, source_target_pairs={{0,6},{2,0},{4,2},{6,4},{1,7},{3,1},{5,3},{7,5},{8,14},{10,8},{12,... | collective-permute-start | bytes 786440 | tf_op jit(solution)/shard_map/ppermute | solution.py:442
  185.0 23.5 %collective-permute-start.23 = (bf16[4,8,64,256]{3,2,1,0:T(8,128)(2,1)}, bf16[4,8,64,256]{3,2,1,0:T(8,128)(2,1)}, u32[]{:S(2)}, u32[]{:S(2)}) collective-permute-start(bf16[4,8,64,256]{3,2,1,0:T(8,128)(2,1)} %get-tuple-element.61.refs_4_), channel_id=1, source_target_pairs={{0,1},{1,0},{2,3},{3,2},{4,5},{5,4},{6,7},{7,6},{8,9},{9,8},{10,11... | collective-permute-start | bytes 3145736 | tf_op jit(solution)/shard_map/ppermute | solution.py:442
  187.3 21.0 %collective-permute-start.22 = (bf16[2,8,64,256]{3,2,1,0:T(8,128)(2,1)}, bf16[2,8,64,256]{3,2,1,0:T(8,128)(2,1)}, u32[]{:S(2)}, u32[]{:S(2)}) collective-permute-start(bf16[2,8,64,256]{3,2,1,0:T(8,128)(2,1)} %get-tuple-element.60.refs_0_.after_ref), channel_id=1, source_target_pairs={{0,2},{2,4},{4,6},{6,0},{1,3},{3,5},{5,7},{7,1},{8,10},{10,12},{12... | collective-permute-start | bytes 1572872 | tf_op jit(solution)/shard_map/ppermute | solution.py:442
  188.0 20.4 %collective-permute-start.21 = (bf16[2,8,64,256]{3,2,1,0:T(8,128)(2,1)}, bf16[2,8,64,256]{3,2,1,0:T(8,128)(2,1)}, u32[]{:S(2)}, u32[]{:S(2)}) collective-permute-start(bf16[2,8,64,256]{3,2,1,0:T(8,128)(2,1)} %get-tuple-element.60.refs_0_.after_ref), channel_id=1, source_target_pairs={{0,4},{2,6},{4,0},{6,2},{1,5},{3,7},{5,1},{7,3},{8,12},{10,14},{12... | collective-permute-start | bytes 1572872 | tf_op jit(solution)/shard_map/ppermute | solution.py:442
  192.5 15.9 %collective-permute-start.20 = (bf16[2,8,64,256]{3,2,1,0:T(8,128)(2,1)}, bf16[2,8,64,256]{3,2,1,0:T(8,128)(2,1)}, u32[]{:S(2)}, u32[]{:S(2)}) collective-permute-start(bf16[2,8,64,256]{3,2,1,0:T(8,128)(2,1)} %get-tuple-element.60.refs_0_.after_ref), channel_id=1, source_target_pairs={{0,6},{2,0},{4,2},{6,4},{1,7},{3,1},{5,3},{7,5},{8,14},{10,8},{12,... | collective-permute-start | bytes 1572872 | tf_op jit(solution)/shard_map/ppermute | solution.py:442
  (19 other events, 135.5 us)
Sparse Core Ops, SparseCore 0:
  38.7 58.2 reduce-scatter.1
  140.4 58.6 all-gather.1
where the time goes:
time: 223 us; the launch traced here: 221 us
  waiting for transfers between devices  67.1 us (30%)
  starting transfers between devices  65.6 us (29%)
  Pallas kernels  49.8 us (22%)
  between operations  15 us (7%)
  local copies, waits for them, and re-layouts  11.6 us (5%)
  other arithmetic  6.37 us (3%)
  blocking collectives  5.67 us (3%)
    ppermute x24, waiting for transfers between devices, along(): lax.ppermute(value, axis, [(i, (i + steps) % count) for i in range(count)])  44.7 us
    ppermute x24, starting transfers between devices, along(): lax.ppermute(value, axis, [(i, (i + steps) % count) for i in range(count)])  44.2 us
    all_to_all x2, waiting for transfers between devices, exchanged(): return lax.all_to_all(value, axes, split_axis=0, concat_axis=0, tiled=True)  22.4 us
    all_to_all x2, starting transfers between devices, exchanged(): return lax.all_to_all(value, axes, split_axis=0, concat_axis=0, tiled=True)  15.2 us
    pallas_call x2, Pallas kernels, local_momentum(): pl.pallas_call(kernel, grid_spec=pltpu.PrefetchScalarGridSpec(num_scalar_...  13.5 us
    pallas_call x1, Pallas kernels, compress(): pl.pallas_call(compress_kernel, grid_spec=pltpu.PrefetchScalarGridSpec(nu...  10.7 us
    unnamed x42, local copies, waits for them, and re-layouts  9.73 us
    pallas_call x2, Pallas kernels, call(): pl.pallas_call(kernel, grid_spec=pltpu.PrefetchScalarGridSpec(num_scalar_...  8.9 us
  transfers between devices with their start and end apart: 32, of which 15 were waited for; matrix products, arithmetic and copies ran while one was open for 3% of the time, Pallas kernels for 11%

commit v1 on v0

v1 whole, which is shorter than its diff:
```python
import functools

import jax
import jax.numpy as jnp
from jax import lax
from jax.experimental import pallas as pl
from jax.experimental.pallas import tpu as pltpu
from jax.sharding import Mesh, PartitionSpec as P

momentum_decay = 0.9
saturation = 0.5
epsilon_term = 1e-06

Z, Y, X = 8, 4, 2
SPAN = 64
COLS_Y, COLS_X = 256, 256
WIDE_Y, WIDE_X = 256, 256
F32, BF16 = jnp.float32, jnp.bfloat16
PARAMS = pltpu.CompilerParams(vmem_limit_bytes=32 * 1024 * 1024)
WIDE = pltpu.CompilerParams(vmem_limit_bytes=56 * 1024 * 1024)
ANY = pl.BlockSpec(memory_space=pl.ANY)
VMEM = pl.BlockSpec(memory_space=pltpu.VMEM)


def local_block(x, g, m):
    grad = lax.dot_general(x, g, (((0,), (0,)), ((), ())), preferred_element_type=F32)
    return momentum_decay * m.astype(F32) + (1.0 - momentum_decay) * grad


def local_part(x_ref, g_ref, m_ref, out_ref, sums_ref):
    local = local_block(x_ref[...], g_ref[...], m_ref[...])
    out_ref[...] = local.astype(BF16)
    rows, cols = local.shape
    per_span = jnp.sum(jnp.abs(local).reshape(rows // SPAN, SPAN, cols), axis=1)
    sums_ref[...] = in_lanes(per_span)


def in_lanes(values):
    total = values[:, :128]
    for lane in range(128, values.shape[1], 128):
        total = total + values[:, lane : lane + 128]
    return total


def own_kernel(seqs, where_ref, x_ref, g_ref, m_ref, out_ref, sums_ref, used_ref):
    @pl.when(pl.program_id(0) == 0)
    def _():
        slots = used_ref.shape[0] // seqs
        for seq in range(seqs):
            rows = slice(seq * slots, (seq + 1) * slots)
            grads = g_ref[rows, :].astype(F32)
            slot = lax.broadcasted_iota(jnp.int32, grads.shape, 0)
            used_ref[rows, :] = jnp.where(slot < where_ref[1 + seq], grads, 0.0).astype(BF16)

    local_part(x_ref, used_ref, m_ref, out_ref, sums_ref)


def other_kernel(where_ref, x_ref, g_ref, m_ref, all_sums_ref, out_ref, sums_ref):
    local_part(x_ref, g_ref, m_ref, out_ref, sums_ref)


def local_momentum(x, g, m, first, lengths=None, sums=None):
    tokens, feats = x.shape
    width, cols = m.shape
    rows = Y * X * SPAN
    where, kernel, more, used = first.reshape(1), other_kernel, [sums], []
    if lengths is not None:
        where = jnp.concatenate([where, lengths])
        kernel = functools.partial(own_kernel, lengths.shape[0])
        more, used = [], [pl.BlockSpec((tokens, cols), lambda i, w: (0, 0))]
    return pl.pallas_call(
        kernel,
        grid_spec=pltpu.PrefetchScalarGridSpec(
            num_scalar_prefetch=1,
            grid=(feats // rows,),
            in_specs=[
                pl.BlockSpec((tokens, rows), lambda i, w: (0, i)),
                pl.BlockSpec((tokens, cols), lambda i, w: (0, 0)),
                pl.BlockSpec((rows, cols), lambda i, w: (w[0] + i, 0)),
            ]
            + [ANY] * len(more),
            out_specs=[
                pl.BlockSpec((rows, cols), lambda i, w: (i, 0)),
                pl.BlockSpec((rows // SPAN, 128), lambda i, w: (w[0] + i, 0)),
            ]
            + used,
        ),
        out_shape=[
            pltpu.HBM((feats, cols), BF16),
            jax.ShapeDtypeStruct((width // SPAN, 128), F32),
        ]
        + [jax.ShapeDtypeStruct((tokens, cols), BF16)] * len(used),
        input_output_aliases={4: 1} if more else {},
        compiler_params=WIDE,
        cost_estimate=pl.CostEstimate(
            flops=2 * tokens * feats * cols, bytes_accessed=4 * feats * cols, transcendentals=0
        ),
    )(where, x, g, m, *more)


def squash(local, scale):
    slope = scale / (saturation * scale + epsilon_term)
    return jnp.clip(local * slope, -scale, scale).astype(BF16)


def halves(run, own_ref, other_ref):
    half = pl.num_programs(0) // 2
    pl.when(pl.program_id(0) < half)(lambda: run(own_ref))
    pl.when(pl.program_id(0) >= half)(lambda: run(other_ref))


def scale_of(s_ref, t_ref, rows, count):
    return jnp.sum(s_ref[rows, :] + t_ref[rows, :], axis=1, keepdims=True) / count


def compress_kernel(where_ref, own_ref, other_ref, s_ref, t_ref, z_ref, *outs):
    my_y, my_x = where_ref[1], where_ref[2]
    cut = z_ref.shape[1]

    def run(local_ref):
        for k in range(Y * X):
            dy, dx = k // X, k % X
            j = lax.rem(my_y + dy, Y) * X + lax.rem(my_x + dx, X)
            rows = pl.ds(pl.multiple_of(j * SPAN, SPAN), SPAN)
            scale = scale_of(s_ref, t_ref, pl.ds(j, 1), SPAN * local_ref.shape[1] * 2)
            packed = squash(local_ref[rows, :].astype(F32), scale)
            z_ref[k * SPAN : (k + 1) * SPAN] = packed[:, :cut]
            outs[dy][dx, 0] = packed[:, cut : cut + COLS_Y]
            outs[Y + dx][dy, 0] = packed[:, cut + COLS_Y :]

    halves(run, own_ref, other_ref)


def error_kernel(where_ref, own_ref, other_ref, s_ref, t_ref, err_ref):
    def run(local_ref):
        for j in range(Y * X):
            rows = pl.ds(j * SPAN, SPAN)
            local = local_ref[rows, :].astype(F32)
            packed = squash(local, scale_of(s_ref, t_ref, pl.ds(j, 1), SPAN * local.shape[1] * 2))
            err_ref[rows, :] = (local - packed.astype(F32)).astype(BF16)

    halves(run, own_ref, other_ref)


def local_specs(own):
    feats, cols = own.shape
    rows = Y * X * SPAN
    half = feats // rows

    def whole(i, w):
        return lax.rem(w[0] + i, 2 * half)

    in_specs = [
        pl.BlockSpec((rows, cols), lambda i, w: (jnp.minimum(i, half - 1), 0)),
        pl.BlockSpec((rows, cols), lambda i, w: (jnp.maximum(i - half, 0), 0)),
        pl.BlockSpec((rows // SPAN, 128), lambda i, w: (whole(i, w), 0)),
        pl.BlockSpec((rows // SPAN, 128), lambda i, w: (whole(i, w), 0)),
    ]
    return (2 * half,), in_specs, whole


def compress(own, other, sums, where):
    feats, cols = own.shape
    width = 2 * feats
    grid, in_specs, whole = local_specs(own)
    rows, cut = Y * X * SPAN, cols // 2
    return pl.pallas_call(
        compress_kernel,
        grid_spec=pltpu.PrefetchScalarGridSpec(
            num_scalar_prefetch=1,
            grid=grid,
            in_specs=in_specs,
            out_specs=[pl.BlockSpec((rows, cut), lambda i, w: (whole(i, w), 0))]
            + [pl.BlockSpec((X, 1, SPAN, COLS_Y), lambda i, w: (0, whole(i, w), 0, 0))] * Y
            + [pl.BlockSpec((Y, 1, SPAN, COLS_X), lambda i, w: (0, whole(i, w), 0, 0))] * X,
        ),
        out_shape=[pltpu.HBM((width, cut), BF16)]
        + [pltpu.HBM((X, Z, SPAN, COLS_Y), BF16)] * Y
        + [pltpu.HBM((Y, Z, SPAN, COLS_X), BF16)] * X,
        compiler_params=WIDE,
        cost_estimate=pl.CostEstimate(
            flops=8 * width * cols, bytes_accessed=4 * width * cols, transcendentals=0
        ),
    )(where, own, other, *sums)


def compression_error(own, other, sums, where):
    feats, cols = own.shape
    width = 2 * feats
    grid, in_specs, whole = local_specs(own)
    return pl.pallas_call(
        error_kernel,
        grid_spec=pltpu.PrefetchScalarGridSpec(
            num_scalar_prefetch=1,
            grid=grid,
            in_specs=in_specs,
            out_specs=pl.BlockSpec((Y * X * SPAN, cols), lambda i, w: (whole(i, w), 0)),
        ),
        out_shape=pltpu.HBM((width, cols), BF16),
        compiler_params=PARAMS,
        cost_estimate=pl.CostEstimate(
            flops=width, bytes_accessed=width, transcendentals=0
        ),
    )(where, own, other, *sums)


def first_sums_kernel(*refs):
    kept_ref, given_ref = refs[Y + X + 2 : Y + X + 4]
    kept_ref[...] = added([ref.at[0] for ref in refs[:Y]])
    given_ref[...] = added([ref.at[1] for ref in refs[:Y]]).astype(BF16)
    for k, out_ref in enumerate(refs[Y + X + 4 : -2]):
        out_ref[...] = added([ref.at[k] for ref in refs[Y : Y + X]]).astype(BF16)


def first_sums(y_parts, x_parts, through):
    _, _, span, share_y = y_parts[0].shape
    share_x = x_parts[0].shape[3]
    return pl.pallas_call(
        first_sums_kernel,
        in_specs=[VMEM] * (Y + X) + [ANY] * 2,
        out_specs=[VMEM] * (2 + Y) + [ANY] * 2,
        out_shape=[
            jax.ShapeDtypeStruct((Z, span, share_y), F32),
            jax.ShapeDtypeStruct((Z, span, share_y), BF16),
        ]
        + [jax.ShapeDtypeStruct((Z, span, share_x), BF16)] * Y
        + [jax.ShapeDtypeStruct(through[0].shape, through[0].dtype), pltpu.HBM(through[1].shape, through[1].dtype)],
        input_output_aliases={Y + X: 2 + Y, Y + X + 1: 3 + Y},
        compiler_params=PARAMS,
        cost_estimate=pl.CostEstimate(
            flops=16 * y_parts[0].size, bytes_accessed=20 * y_parts[0].size, transcendentals=0
        ),
    )(*y_parts, *x_parts, *through)


def pair_kernel(all_ref, swapped_ref, pair_ref):
    pair_ref[0] = all_ref[:, :, :WIDE_Y]
    pair_ref[1] = swapped_ref[...]


def ring_kernel(all_ref, *refs):
    ring_ref = refs[-1]
    ring_ref[0] = all_ref[:, :, WIDE_Y:]
    for k in range(1, Y):
        ring_ref[k] = refs[k - 1][...]


def gathered(kernel, all_z, others, share, after):
    span = all_z.shape[1]
    return pl.pallas_call(
        kernel,
        in_specs=[VMEM] * (1 + len(others)) + [ANY] * len(after),
        out_specs=VMEM,
        out_shape=jax.ShapeDtypeStruct((1 + len(others), Z, span, share), BF16),
        compiler_params=PARAMS,
        cost_estimate=pl.CostEstimate(flops=0, bytes_accessed=4 * all_z.size, transcendentals=0),
    )(all_z, *others, *after)


def added(refs):
    total = refs[0][...].astype(F32)
    for ref in refs[1:]:
        total = total + ref[...].astype(F32)
    return total


def plane_sum_kernel(kept_ref, other_ref, *refs):
    out_ref = refs[-1]
    out_ref[:, :, :COLS_Y] = added([kept_ref, other_ref]).astype(BF16)
    out_ref[:, :, COLS_Y:] = added(refs[:Y]).astype(BF16)


def plane_sum(kept, other, x_parts, after):
    return pl.pallas_call(
        plane_sum_kernel,
        in_specs=[VMEM] * (2 + Y) + [ANY],
        out_specs=VMEM,
        out_shape=jax.ShapeDtypeStruct((Z, SPAN, COLS_Y + COLS_X), BF16),
        compiler_params=PARAMS,
        cost_estimate=pl.CostEstimate(
            flops=8 * kept.size, bytes_accessed=12 * kept.size, transcendentals=0
        ),
    )(kept, other, *x_parts, after)


def y_sum_kernel(own_ref, *refs):
    kept_ref, given_ref = refs[-2:]
    kept_ref[...] = added([own_ref.at[0, 0]] + [ref.at[0] for ref in refs[: Y - 1]])
    given_ref[...] = added([own_ref.at[0, 1]] + [ref.at[1] for ref in refs[: Y - 1]]).astype(BF16)


def y_sum(own, parts, after):
    shape = own.shape[2:]
    return pl.pallas_call(
        y_sum_kernel,
        in_specs=[VMEM] * (1 + len(parts)) + [ANY],
        out_specs=[VMEM] * 2,
        out_shape=[jax.ShapeDtypeStruct(shape, F32), jax.ShapeDtypeStruct(shape, BF16)],
        compiler_params=PARAMS,
        cost_estimate=pl.CostEstimate(flops=own.size, bytes_accessed=3 * own.size, transcendentals=0),
    )(own, *parts, after)


def server_kernel(kept_ref, other_ref, b_ref, out_ref, sums_ref):
    cut = b_ref.shape[2]
    out_ref[:, :cut] = added([kept_ref, other_ref]) / (Z * Y * X)
    out_ref[:, cut:] = added([b_ref.at[k] for k in range(Z)]) / (Z * Y * X)
    rows, cols = out_ref.shape
    sums_ref[...] = in_lanes(jnp.sum(jnp.abs(out_ref[...]).reshape(rows // 8, 8, cols), axis=0))


def server_sum(kept, other, b):
    _, span, cut = b.shape
    return pl.pallas_call(
        server_kernel,
        in_specs=[VMEM] * 3,
        out_specs=[VMEM] * 2,
        out_shape=[jax.ShapeDtypeStruct((span, 2 * cut), F32), jax.ShapeDtypeStruct((8, 128), F32)],
        compiler_params=PARAMS,
        cost_estimate=pl.CostEstimate(flops=2 * b.size, bytes_accessed=5 * b.size, transcendentals=0),
    )(kept, other, b)


def owned_kernel(averaged_ref, sums_ref, other_ref, error_ref, a_ref, b_ref):
    averaged = averaged_ref[...]
    owned = squash(averaged, jnp.sum(sums_ref[...] + other_ref[...], keepdims=True) / (averaged.size * 2))
    error_ref[...] = averaged - owned.astype(F32)
    cut = a_ref.shape[1]
    a_ref[...] = owned[:, :cut]
    b_ref[...] = jnp.broadcast_to(owned[None, :, cut:], b_ref.shape)


def owned_momentum(averaged, sums, other):
    span, cols = averaged.shape
    cut = cols - WIDE_Y - WIDE_X
    return pl.pallas_call(
        owned_kernel,
        in_specs=[VMEM] * 3,
        out_specs=[VMEM] * 3,
        out_shape=[
            jax.ShapeDtypeStruct((span, cols), F32),
            jax.ShapeDtypeStruct((span, cut), BF16),
            pltpu.HBM((Z, span, cols - cut), BF16),
        ],
        compiler_params=PARAMS,
        cost_estimate=pl.CostEstimate(
            flops=8 * averaged.size, bytes_accessed=24 * averaged.size, transcendentals=0
        ),
    )(averaged, sums, other)


def input_grad_kernel(half, where_ref, g_ref, w_ref, own_ref, other_ref):
    step = pl.program_id(0)
    term = lax.dot_general(g_ref[...], w_ref[...], (((1,), (1,)), ((), ())), preferred_element_type=F32)

    @pl.when(step < half)
    def _():
        other_ref[...] = term.astype(BF16)

    @pl.when(step >= half)
    def _():
        own_ref[...] = term


def input_grad(g, weight, first_other):
    tokens, cols = g.shape
    width = weight.shape[0]
    rows = min(512, width // 2)
    half = width // 2 // rows
    return pl.pallas_call(
        functools.partial(input_grad_kernel, half),
        grid_spec=pltpu.PrefetchScalarGridSpec(
            num_scalar_prefetch=1,
            grid=(2 * half,),
            in_specs=[
                pl.BlockSpec((tokens, cols), lambda i, w: (0, 0)),
                pl.BlockSpec((rows, cols), lambda i, w: (lax.rem(w[0] * half + i, 2 * half), 0)),
            ],
            out_specs=[
                pl.BlockSpec((tokens, rows), lambda i, w: (0, jnp.maximum(i - half, 0))),
                pl.BlockSpec((tokens, rows), lambda i, w: (0, jnp.minimum(i, half - 1))),
            ],
        ),
        out_shape=[jax.ShapeDtypeStruct((tokens, width // 2), t) for t in (F32, BF16)],
        compiler_params=PARAMS,
        cost_estimate=pl.CostEstimate(
            flops=2 * tokens * width * cols,
            bytes_accessed=2 * width * cols + 4 * tokens * width,
            transcendentals=0,
        ),
    )(first_other.reshape(1), g, weight)


def copy_all(pairs, sems):
    copies = [pltpu.make_async_copy(*pair, sems.at[k]) for k, pair in enumerate(pairs)]
    for copy in copies:
        copy.start()
    for copy in copies:
        copy.wait()


def rows_of(where_ref, z, dy, dx):
    j = lax.rem(where_ref[1] + dy, Y) * X + lax.rem(where_ref[2] + dx, X)
    return pl.ds(pl.multiple_of((z * Y * X + j) * SPAN, SPAN), SPAN)


def assemble_b_kernel(y_places, x_places, cut, where_ref, *refs):
    out_ref, sems = refs[-2:]
    pairs = []
    for z in range(Z):
        for ref, dy in zip(refs, y_places):
            for dx in range(X):
                rows = rows_of(where_ref, z, dy, dx)
                pairs.append((ref.at[dx, z], out_ref.at[rows, pl.ds(cut, WIDE_Y)]))
        for ref, dx in zip(refs[len(y_places) :], x_places):
            for dy in range(Y):
                rows = rows_of(where_ref, z, dy, dx)
                pairs.append((ref.at[dy, z], out_ref.at[rows, pl.ds(cut + WIDE_Y, WIDE_X)]))
    copy_all(pairs, sems)


def assemble_a_kernel(where_ref, a_ref, _, out_ref, sems, held, held_sems):
    places, cut = X * Y, a_ref.shape[1]
    incoming, outgoing = [], []
    for z in range(Z):
        rows = pl.ds(z * places * SPAN, places * SPAN)
        incoming.append(pltpu.make_async_copy(a_ref.at[rows], held.at[rows], held_sems.at[z]))
        incoming[-1].start()
    for z in range(Z):
        incoming[z].wait()
        for k in range(z * places, (z + 1) * places):
            rows = rows_of(where_ref, z, k % Y, k // Y % X)
            source = held.at[pl.ds(k * SPAN, SPAN)]
            outgoing.append(pltpu.make_async_copy(source, out_ref.at[rows, pl.ds(0, cut)], sems.at[k]))
            outgoing[-1].start()
    for copy in outgoing:
        copy.wait()


def assemble(where, a, y_parts, x_parts, after):
    width, cut = a.shape

    def call(kernel, count, operands, space, more, scratch=()):
        return pl.pallas_call(
            kernel,
            grid_spec=pltpu.PrefetchScalarGridSpec(
                num_scalar_prefetch=1,
                grid=(1,),
                in_specs=[space] * len(operands) + [ANY] * len(more),
                out_specs=ANY,
                scratch_shapes=[pltpu.SemaphoreType.DMA((count,)), *scratch],
            ),
            out_shape=pltpu.HBM((width, cut + WIDE_Y + WIDE_X), BF16),
            input_output_aliases={1 + len(operands): 0} if more else {},
            compiler_params=PARAMS,
            cost_estimate=pl.CostEstimate(flops=0, bytes_accessed=4 * width * cut, transcendentals=0),
        )(where, *operands, *more)

    first = functools.partial(assemble_b_kernel, [0], [0], cut)
    rest = functools.partial(assemble_b_kernel, list(range(1, Y)), list(range(1, X)), cut)
    own = Z * (X + Y)
    out = call(first, own, [y_parts[0], x_parts[0]], VMEM, [])
    scratch = [pltpu.VMEM((width, cut), BF16), pltpu.SemaphoreType.DMA((Z,))]
    a = pltpu.with_memory_space_constraint(a, pltpu.HBM)
    out = call(assemble_a_kernel, Z * Y * X, [a], ANY, [out], scratch)
    return call(rest, 2 * Z * Y * X - own, [*y_parts[1:], *x_parts[1:]], VMEM, [out, *after])


def over_tensor(value):
    return lax.ppermute(value, "tensor", [(0, 1), (1, 0)])


def along(value, axis, steps):
    count = lax.axis_size(axis)
    return lax.ppermute(value, axis, [(i, (i + steps) % count) for i in range(count)])


def exchanged(value, axes):
    return lax.all_to_all(value, axes, split_axis=0, concat_axis=0, tiled=True)


def shards(layer_input, other_grad, head_grad, lengths, proj_weight, old_momentum):
    tensor, my_y, my_x = (lax.axis_index(a).astype(jnp.int32) for a in ("tensor", "y", "x"))
    own, momentum, weight = layer_input[0], old_momentum[0], proj_weight[0]
    width, cols = momentum.shape
    cut = cols // 2
    other = over_tensor(own)

    half = width // 2 // (Y * X * SPAN)
    local_own, sums, used_grad = local_momentum(own, head_grad[0], momentum, tensor * half, lengths)
    local_other, sums = local_momentum(other, used_grad, momentum, (1 - tensor) * half, sums=sums)
    sums = [sums, over_tensor(sums)]

    where = jnp.stack([tensor * half, my_y, my_x])
    by_z, *rest = compress(local_own, local_other, sums, where)
    part_z = lax.psum_scatter(by_z, "z", scatter_dimension=0, tiled=True)
    by_y, by_x = rest[:Y], rest[Y:]
    from_y = [by_y[0]] + [along(by_y[k], "y", k) for k in range(1, Y)]
    from_x = [by_x[0], along(by_x[1], "x", 1)]

    share, share_other = input_grad(used_grad, weight, 1 - tensor)
    err = compression_error(local_own, local_other, sums, where)
    kept, given, *sum_x, share_other, err = first_sums(from_y, from_x, [share_other, err])
    other_x = along(given, "x", 1)
    from_xy = [sum_x[0]] + [along(sum_x[k], "y", k) for k in range(1, Y)]
    term = other_grad[0].astype(F32) + share + over_tensor(share_other).astype(F32)
    rounded = term.astype(BF16)
    sum_plane = plane_sum(kept, other_x, from_xy, rounded[:16, :128])
    nearer = lax.ppermute(rounded, ("section", "x"), [(2, 3), (3, 2)])
    passed = lax.ppermute(nearer, ("section", "x"), [(2, 1), (3, 0)])
    upstream = (term + passed.astype(F32)).astype(BF16)

    arrived_b = exchanged(sum_plane, "z")
    own_a = part_z.reshape(Y, X, SPAN, cut)
    kept_a, given_a = y_sum(own_a, [along(own_a[k], "y", k) for k in range(1, Y)], nearer[:16, :128])
    averaged, magnitudes = server_sum(kept_a, along(given_a, "x", 1), arrived_b)

    server_error, owned_a, owned_b = owned_momentum(averaged, magnitudes, over_tensor(magnitudes))

    ring_a = jnp.concatenate([owned_a] + [along(owned_a, "y", -k) for k in range(1, Y)])
    plane_a = jnp.concatenate([ring_a, along(ring_a, "x", 1)])
    all_a = lax.all_gather(plane_a, "z", axis=0, tiled=True)
    all_z = exchanged(owned_b, "z")
    first_y, first_x = all_z[:, :, :WIDE_Y], all_z[:, :, WIDE_Y:]
    pair_y = gathered(pair_kernel, all_z, [along(first_y, "x", 1)], WIDE_Y, [])
    others = [along(first_x, "y", -k) for k in range(1, Y)]
    ring_x = gathered(ring_kernel, all_z, others, WIDE_X, [pair_y[0, 0, :16, :128]])
    y_parts = [pair_y] + [along(pair_y, "y", -k) for k in range(1, Y)]
    x_parts = [ring_x, along(ring_x, "x", 1)]
    everything = assemble(where, all_a, y_parts, x_parts, [upstream])
    return (upstream[None], everything[None], err[None, None], server_error[None])


def solution(mesh):
    sections, groups, _ = mesh.devices.shape
    fine = Mesh(mesh.devices.reshape(sections, groups, Z, Y, X), ("section", "tensor", "z", "y", "x"))
    dp = ("z", "y", "x")
    placed = (
        P("section", dp, "tensor"),
        P("section", dp, "tensor"),
        P("section", dp, "tensor"),
        P(dp),
        P("section", None, "tensor"),
        P("section", None, "tensor"),
    )
    return jax.shard_map(
        shards,
        mesh=fine,
        in_specs=placed,
        out_specs=(
            P("section", dp, "tensor"),
            P("section", None, "tensor"),
            P("section", dp, None, "tensor"),
            P("section", dp, "tensor"),
        ),
        check_vma=False,
    )
```

time: 223 us -> 206 us (0.924)
  waiting for transfers between devices: 67.1 us -> 59 us
  blocking collectives: 5.67 us -> 0 us
  starting transfers between devices: 65.6 us -> 61.1 us
  Pallas kernels: 49.8 us -> 54 us
    ppermute x24, waiting for transfers between devices: 44.7 us -> 34.4 us  [along(): lax.ppermute(value, axis, [(i, (i + steps) % count) for i in range(count)])]
    psum x2 -> x0, blocking collectives: 5.67 us -> none  [the longest x1 3.08 us: shards(): server_scale = lax.psum(jnp.sum(magnitudes), 'tensor') / (SPAN * cols * 2)]
    all_to_all x2, waiting for transfers between devices: 22.4 us -> 17.3 us  [exchanged(): return lax.all_to_all(value, axes, split_axis=0, concat_axis=0, tiled=True)]
    pallas_call x2 -> x3, Pallas kernels: 8.9 us -> 12.5 us  [call(): pl.pallas_call(kernel, grid_spec=pltpu.PrefetchScalarGridSpec(num_scalar_...]
    ppermute x24, starting transfers between devices: 44.2 us -> 41 us  [along(): lax.ppermute(value, axis, [(i, (i + steps) % count) for i in range(count)])]
    all_gather x1, waiting for transfers between devices: 0.01 us -> 3.05 us  [shards(): all_a = lax.all_gather(plane_a, 'z', axis=0, tiled=True)]
    unnamed x42, local copies, waits for them, and re-layouts: 9.73 us -> 6.88 us
    reduce_scatter x1, waiting for transfers between devices: 0.02 us -> 2.48 us  [shards(): part_z = lax.psum_scatter(by_z, 'z', scatter_dimension=0, tiled=True)]
  transfers between devices with their start and end apart: 32 -> 34, of which waited for: 15 -> 21; matrix products, arithmetic and copies ran while one was open for 3% -> 4% of each run, Pallas kernels for 11% -> 15%
where the time goes in v1:
time: 206 us; the launch traced here: 204 us
  starting transfers between devices  61.1 us (30%)
  waiting for transfers between devices  59 us (29%)
  Pallas kernels  54 us (26%)
  between operations  14.4 us (7%)
  local copies, waits for them, and re-layouts  10 us (5%)
  other arithmetic  5.18 us (3%)
    ppermute x24, starting transfers between devices, along(): lax.ppermute(value, axis, [(i, (i + steps) % count) for i in range(count)])  41 us
    ppermute x24, waiting for transfers between devices, along(): lax.ppermute(value, axis, [(i, (i + steps) % count) for i in range(count)])  34.4 us
    all_to_all x2, waiting for transfers between devices, exchanged(): return lax.all_to_all(value, axes, split_axis=0, concat_axis=0, tiled=True)  17.3 us
    pallas_call x2, Pallas kernels, local_momentum(): pl.pallas_call(kernel, grid_spec=pltpu.PrefetchScalarGridSpec(num_scalar_...  13.4 us
    all_to_all x2, starting transfers between devices, exchanged(): return lax.all_to_all(value, axes, split_axis=0, concat_axis=0, tiled=True)  12.8 us
    pallas_call x3, Pallas kernels, call(): pl.pallas_call(kernel, grid_spec=pltpu.PrefetchScalarGridSpec(num_scalar_...  12.5 us
    pallas_call x1, Pallas kernels, compress(): pl.pallas_call(compress_kernel, grid_spec=pltpu.PrefetchScalarGridSpec(nu...  10.8 us
    pallas_call x1, Pallas kernels, compression_error(): pl.pallas_call(error_kernel, grid_spec=pltpu.PrefetchScalarGridSpec(num_s...  8.19 us
  transfers between devices with their start and end apart: 34, of which 21 were waited for; matrix products, arithmetic and copies ran while one was open for 4% of the time, Pallas kernels for 15%

profile of v1, /device:TPU:4, one launch (start us, length us, event | category | flops | bytes accessed | tf_op | source)
XLA Modules:
  0.0 203.7 jit_solution(6142033175413083108)
XLA Ops:
  8.6 7.1 %shard_map.93 = (bf16[2048,1024]{1,0:T(8,128)(2,1)}, f32[64,128]{1,0:T(8,128)}, bf16[256,1024]{1,0:T(8,128)(2,1)}) custom-call(s32[5]{0:T(128)} %pad_add_fusion.where_ref, bf16[256,2048]{1,0:T(8,128)(2,1)} %bitcast.34, bf16[256,1024]{1,0:T(8,128)(2,1)} %bitcast.35, bf16[4096,1024]{1,0:T(8,128)(2,1)} %bitcast.30), custom_call_target="tpu_custom_call" | custom-call | flops 1073741824 | bytes 8388608 | tf_op jit(solution)/shard_map/pallas_call | solution.py:71
  16.6 6.3 %shard_map.95 = (bf16[2048,1024]{1,0:T(8,128)(2,1)}, f32[64,128]{1,0:T(8,128)}) custom-call(s32[1]{0:T(128)} %bitcast.9.where_ref, bf16[256,2048]{1,0:T(8,128)(2,1)} %copy-done.16, bf16[256,1024]{1,0:T(8,128)(2,1)} %get-tuple-element.33.g_ref, bf16[4096,1024]{1,0:T(8,128)(2,1)} %bitcast.31, ...), custom_call_target="tpu_custom_call", output_to_operand_aliasing={{1}: (4, {})} | custom-call | flops 1073741824 | bytes 8388608 | tf_op jit(solution)/shard_map/pallas_call | solution.py:71
  25.1 10.8 %shard_map.96 = (bf16[4096,512]{1,0:T(8,128)(2,1)}, bf16[2,8,64,256]{3,2,1,0:T(8,128)(2,1)}, bf16[2,8,64,256]{3,2,1,0:T(8,128)(2,1)}, bf16[2,8,64,256]{3,2,1,0:T...) custom-call(s32[3]{0:T(128)} %pad_add_fusion.1.where_ref, ...), custom_call_target="tpu_custom_call" | custom-call | flops 33554432 | bytes 16777216 | tf_op jit(solution)/shard_map/pallas_call | solution.py:167
  37.2 1.6 collective-permute-start.2
  38.8 2.9 %collective-permute-start.3 = (bf16[2,8,64,256]{3,2,1,0:T(8,128)(2,1)}, bf16[2,8,64,256]{3,2,1,0:T(8,128)(2,1)S(1)}, u32[]{:S(2)}, u32[]{:S(2)}) collective-permute-start(bf16[2,8,64,256]{3,2,1,0:T(8,128)(2,1)} %get-tuple-element.41), channel_id=1, source_target_pairs={{0,4},{2,6},{4,0},{6,2},{1,5},{3,7},{5,1},{7,3},{8,12},{10,14},{12... | collective-permute-start | bytes 1572872 | tf_op jit(solution)/shard_map/ppermute | solution.py:475
  43.1 3.4 %copy-done.2 = bf16[1,4096,1024]{2,1,0:T(8,128)(2,1)S(1)} copy-done((bf16[1,4096,1024]{2,1,0:T(8,128)(2,1)S(1)}, bf16[1,4096,1024]{2,1,0:T(8,128)(2,1)}, u32[]{:S(2)}) %copy-start.2) | copy-done | bytes 8388632
  46.5 4.5 %shard_map.94 = (f32[256,2048]{1,0:T(8,128)S(1)}, bf16[256,2048]{1,0:T(8,128)(2,1)S(1)}) custom-call(s32[1]{0:T(128)} %bitcast.1.where_ref, bf16[256,1024]{1,0:T(8,128)(2,1)S(1)} %copy-done.4, bf16[4096,1024]{1,0:T(8,128)(2,1)S(1)} %bitcast.26), custom_call_target="tpu_custom_call" | custom-call | flops 2147483648 | bytes 12582912 | tf_op jit(solution)/shard_map/pallas_call | solution.py:370
  51.0 8.2 %shard_map.97.refs_7_ = bf16[4096,1024]{1,0:T(8,128)(2,1)} custom-call(s32[3]{0:T(128)S(1)} %copy-done.11, bf16[2048,1024]{1,0:T(8,128)(2,1)S(1)} %copy-done, bf16[2048,1024]{1,0:T(8,128)(2,1)S(1)} %copy-done.1, f32[64,128]{1,0:T(8,128)S(1)} %copy-done.8, f32[64,128]{1,0:T(8,128)S(1)} %copy-done.10), custom_call_target="tpu_custom_call" | custom-call | flops 4096 | bytes 4096 | tf_op jit(solution)/shard_map/pallas_call | solution.py:191
  59.2 5.8 %collective-permute-done.3.refs_2_ = bf16[2,8,64,256]{3,2,1,0:T(8,128)(2,1)S(1)} collective-permute-done((bf16[2,8,64,256]{3,2,1,0:T(8,128)(2,1)}, bf16[2,8,64,256]{3,2,1,0:T(8,128)(2,1)S(1)}, u32[]{:S(2)}, u32[]{:S(2)}) %collective-permute-start.3) | collective-permute-done | bytes 524320 | tf_op jit(solution)/shard_map/ppermute | solution.py:475
  67.5 2.6 %collective-permute-start.15 = (bf16[8,64,256]{2,1,0:T(8,128)(2,1)S(1)}, bf16[8,64,256]{2,1,0:T(8,128)(2,1)S(1)}, u32[]{:S(2)}, u32[]{:S(2)}) collective-permute-start(bf16[8,64,256]{2,1,0:T(8,128)(2,1)S(1)} %get-tuple-element.54), channel_id=1, source_target_pairs={{0,4},{2,6},{4,0},{6,2},{1,5},{3,7},{5,1},{7,3},{8,12},{10,14},{12... | collective-permute-start | bytes 786440 | tf_op jit(solution)/shard_map/ppermute | solution.py:475
  70.1 1.6 collective-permute-start.16
  73.2 3.1 %collective-permute-start.7 = (bf16[256,2048]{1,0:T(8,128)(2,1)}, bf16[256,2048]{1,0:T(8,128)(2,1)}, u32[]{:S(2)}, u32[]{:S(2)}) collective-permute-start(bf16[256,2048]{1,0:T(8,128)(2,1)} %fusion.1), channel_id=1, source_target_pairs={{128,129},{129,128},{130,131},{131,130},{132,133},{133,132},{134,1... | collective-permute-start | bytes 3145736 | tf_op jit(solution)/shard_map/ppermute | solution.py:509
  77.0 5.0 %collective-permute-done.15.refs_2_ = bf16[8,64,256]{2,1,0:T(8,128)(2,1)S(1)} collective-permute-done((bf16[8,64,256]{2,1,0:T(8,128)(2,1)S(1)}, bf16[8,64,256]{2,1,0:T(8,128)(2,1)S(1)}, u32[]{:S(2)}, u32[]{:S(2)}) %collective-permute-start.15) | collective-permute-done | bytes 262176 | tf_op jit(solution)/shard_map/ppermute | solution.py:475
  83.4 8.5 %all-to-all-start = ((bf16[8,64,512]{2,1,0:T(8,128)(2,1)}), bf16[8,64,512]{2,1,0:T(8,128)(2,1)S(1)}, u32[]{:S(2)}, u32[]{:S(2)}) async-start(bf16[8,64,512]{2,1,0:T(8,128)(2,1)} %shard_map.100), calls=%async_computation.1 | async-start | bytes 1048576 | tf_op jit(solution)/shard_map/all_to_all | solution.py:479
  91.9 2.5 %reduce-scatter.2.cloned.1.call-done = bf16[512,512]{1,0:T(8,128)(2,1)} async-done(((bf16[4096,512]{1,0:T(8,128)(2,1)}), bf16[512,512]{1,0:T(8,128)(2,1)}) %reduce-scatter.2.cloned.1.call-update) | async-done | bytes 524304 | tf_op jit(solution)/shard_map/reduce_scatter | solution.py:496
  95.4 3.1 %collective-permute-start.10 = (bf16[2,64,512]{2,1,0:T(8,128)(2,1)S(1)}, bf16[2,64,512]{2,1,0:T(8,128)(2,1)S(1)}, u32[]{:S(2)}, u32[]{:S(2)}) collective-permute-start(bf16[2,64,512]{2,1,0:T(8,128)(2,1)S(1)} %bitcast.38), channel_id=1, source_target_pairs={{0,4},{2,6},{4,0},{6,2},{1,5},{3,7},{5,1},{7,3},{8,12},{10,14},{12... | collective-permute-start | bytes 393224 | tf_op jit(solution)/shard_map/ppermute | solution.py:475
  101.2 2.0 collective-permute-done.10.refs_1_
  103.2 2.1 %collective-permute-done.11.refs_2_ = bf16[2,64,512]{2,1,0:T(8,128)(2,1)S(1)} collective-permute-done((bf16[2,64,512]{2,1,0:T(8,128)(2,1)S(1)}, bf16[2,64,512]{2,1,0:T(8,128)(2,1)S(1)}, u32[]{:S(2)}, u32[]{:S(2)}) %collective-permute-start.11) | collective-permute-done | bytes 131104 | tf_op jit(solution)/shard_map/ppermute | solution.py:475
  108.6 2.7 %collective-permute-done.12.other_ref = bf16[64,512]{1,0:T(8,128)(2,1)S(1)} collective-permute-done((bf16[64,512]{1,0:T(8,128)(2,1)S(1)}, bf16[64,512]{1,0:T(8,128)(2,1)S(1)}, u32[]{:S(2)}, u32[]{:S(2)}) %collective-permute-start.12) | collective-permute-done | bytes 65568 | tf_op jit(solution)/shard_map/ppermute | solution.py:475
  114.5 2.8 %collective-permute-start.27 = (bf16[64,512]{1,0:T(8,128)(2,1)S(1)}, bf16[64,512]{1,0:T(8,128)(2,1)S(1)}, u32[]{:S(2)}, u32[]{:S(2)}) collective-permute-start(bf16[64,512]{1,0:T(8,128)(2,1)S(1)} %get-tuple-element.59), channel_id=1, source_target_pairs={{0,4},{2,6},{4,0},{6,2},{1,5},{3,7},{5,1},{7,3},{8,12},{10,14},{12... | collective-permute-start | bytes 196616 | tf_op jit(solution)/shard_map/ppermute | solution.py:475
  122.8 6.4 %collective-permute-done.29 = bf16[256,512]{1,0:T(8,128)(2,1)S(1)} collective-permute-done((bf16[256,512]{1,0:T(8,128)(2,1)S(1)}, bf16[256,512]{1,0:T(8,128)(2,1)S(1)}, u32[]{:S(2)}, u32[]{:S(2)}) %collective-permute-start.29) | collective-permute-done | bytes 262176 | tf_op jit(solution)/shard_map/ppermute | solution.py:475
  130.1 4.3 %all-to-all-start.1 = ((bf16[8,64,512]{2,1,0:T(8,128)(2,1)}), bf16[8,64,512]{2,1,0:T(8,128)(2,1)S(1)}, u32[]{:S(2)}, u32[]{:S(2)}) async-start(bf16[8,64,512]{2,1,0:T(8,128)(2,1)} %get-tuple-element.58), calls=%async_computation.2 | async-start | bytes 1048576 | tf_op jit(solution)/shard_map/all_to_all | solution.py:479
  134.4 3.5 %collective-permute-start.8 = (bf16[256,2048]{1,0:T(8,128)(2,1)}, bf16[256,2048]{1,0:T(8,128)(2,1)}, u32[]{:S(2)}, u32[]{:S(2)}) collective-permute-start(bf16[256,2048]{1,0:T(8,128)(2,1)} %collective-permute-done.7), channel_id=1, source_target_pairs={{128,1},{129,0},{130,3},{131,2},{132,5},{133,4},{134,7},{135,6},{1... | collective-permute-start | bytes 3145736 | tf_op jit(solution)/shard_map/ppermute | solution.py:510
  137.8 17.0 %all-to-all-done.1.all_ref = bf16[8,64,512]{2,1,0:T(8,128)(2,1)S(1)} async-done(((bf16[8,64,512]{2,1,0:T(8,128)(2,1)}), bf16[8,64,512]{2,1,0:T(8,128)(2,1)S(1)}, u32[]{:S(2)}, u32[]{:S(2)}) %all-to-all-start.1) | async-done | bytes 524320 | tf_op jit(solution)/shard_map/all_to_all | solution.py:479
  157.4 2.7 %collective-permute-start.23 = (bf16[8,64,256]{2,1,0:T(8,128)(2,1)S(1)}, bf16[8,64,256]{2,1,0:T(8,128)(2,1)S(1)}, u32[]{:S(2)}, u32[]{:S(2)}) collective-permute-start(bf16[8,64,256]{2,1,0:T(8,128)(2,1)S(1)} %get-tuple-element.62), channel_id=1, source_target_pairs={{0,4},{2,6},{4,0},{6,2},{1,5},{3,7},{5,1},{7,3},{8,12},{10,14},{12... | collective-permute-start | bytes 786440 | tf_op jit(solution)/shard_map/ppermute | solution.py:475
  163.6 4.2 %collective-permute-done.23.refs_1_ = bf16[8,64,256]{2,1,0:T(8,128)(2,1)S(1)} collective-permute-done((bf16[8,64,256]{2,1,0:T(8,128)(2,1)S(1)}, bf16[8,64,256]{2,1,0:T(8,128)(2,1)S(1)}, u32[]{:S(2)}, u32[]{:S(2)}) %collective-permute-start.23) | collective-permute-done | bytes 262176 | tf_op jit(solution)/shard_map/ppermute | solution.py:475
  170.1 9.2 %collective-permute-start.20 = (bf16[2,8,64,256]{3,2,1,0:T(8,128)(2,1)}, bf16[2,8,64,256]{3,2,1,0:T(8,128)(2,1)}, u32[]{:S(2)}, u32[]{:S(2)}) collective-permute-start(bf16[2,8,64,256]{3,2,1,0:T(8,128)(2,1)} %shard_map.103.refs_0_), channel_id=1, source_target_pairs={{0,4},{2,6},{4,0},{6,2},{1,5},{3,7},{5,1},{7,3},{8,12},{10,14},{12... | collective-permute-start | bytes 1572872 | tf_op jit(solution)/shard_map/ppermute | solution.py:475
  179.3 1.9 add_convert_fusion.refs_5_
  181.2 3.5 %shard_map.105._ = bf16[4096,1024]{1,0:T(8,128)(2,1)} custom-call(s32[3]{0:T(128)S(1)} %copy-done.11, bf16[2,8,64,256]{3,2,1,0:T(8,128)(2,1)} %shard_map.103.refs_0_, bf16[4,8,64,256]{3,2,1,0:T(8,128)(2,1)} %shard_map.104.refs_1_), custom_call_target="tpu_custom_call" | custom-call | bytes 8388608 | tf_op jit(solution)/shard_map/pallas_call | solution.py:444
  184.7 3.1 %all-gather.2.cloned.1.call-done.a_ref = bf16[4096,512]{1,0:T(8,128)(2,1)} async-done(((bf16[512,512]{1,0:T(8,128)(2,1)}), bf16[4096,512]{1,0:T(8,128)(2,1)}) %all-gather.2.cloned.1.call-update) | async-done | bytes 4194320 | tf_op jit(solution)/shard_map/all_gather | solution.py:522
  187.8 4.6 %shard_map.106.refs_4_ = bf16[4096,1024]{1,0:T(8,128)(2,1)} custom-call(s32[3]{0:T(128)S(1)} %copy-done.11, bf16[4096,512]{1,0:T(8,128)(2,1)} %all-gather.2.cloned.1.call-done.a_ref, bf16[4096,1024]{1,0:T(8,128)(2,1)} %shard_map.105._), custom_call_target="tpu_custom_call", output_to_operand_aliasing={{}: (2, {})} | custom-call | bytes 8388608 | tf_op jit(solution)/shard_map/pallas_call | solution.py:444
  192.4 4.4 %shard_map.107 = bf16[4096,1024]{1,0:T(8,128)(2,1)} custom-call(s32[3]{0:T(128)S(1)} %copy-done.11, bf16[2,8,64,256]{3,2,1,0:T(8,128)(2,1)} %collective-permute-done.19.refs_0_, bf16[2,8,64,256]{3,2,1,0:T(8,128)(2,1)} %collective-permute-done.20.refs_1_, bf16[2,8,64,256]{3,2,1,0:T(8,128)(2,1)} %collective-permute-done.21.refs_2_, ...), custom_call_target="tpu_custom_call", output_to_operand_aliasing={{}: (5, {})} | custom-call | bytes 8388608 | tf_op jit(solution)/shard_map/pallas_call | solution.py:444
  (106 shorter events, 38.3 us)
Async XLA Ops:
  7.2 87.2 %reduce-scatter.2.cloned.1.call-start = ((), (), s32[]{:S(2)}) async-start(), calls=%async_computation.3 | async-start | bytes 4718592 | tf_op jit(solution)/shard_map/reduce_scatter | solution.py:496
  7.2 8.4 %collective-permute-start = (bf16[256,2048]{1,0:T(8,128)(2,1)}, bf16[256,2048]{1,0:T(8,128)(2,1)S(1)}, u32[]{:S(2)}, u32[]{:S(2)}) collective-permute-start(bf16[256,2048]{1,0:T(8,128)(2,1)} %bitcast.33), channel_id=1, source_target_pairs={{0,64},{64,0},{1,65},{65,1},{2,66},{66,2},{3,67},{67,3},{4,68},{68... | collective-permute-start | bytes 3145736 | tf_op jit(solution)/shard_map/ppermute | solution.py:470
  35.9 29.1 %collective-permute-start.5 = (bf16[4,8,64,256]{3,2,1,0:T(8,128)(2,1)}, bf16[4,8,64,256]{3,2,1,0:T(8,128)(2,1)S(1)}, u32[]{:S(2)}, u32[]{:S(2)}) collective-permute-start(bf16[4,8,64,256]{3,2,1,0:T(8,128)(2,1)} %get-tuple-element.44), channel_id=1, source_target_pairs={{0,1},{1,0},{2,3},{3,2},{4,5},{5,4},{6,7},{7,6},{8,9},{9,8},{10,11... | collective-permute-start | bytes 3145736 | tf_op jit(solution)/shard_map/ppermute | solution.py:475
  37.2 22.0 %collective-permute-start.2 = (bf16[2,8,64,256]{3,2,1,0:T(8,128)(2,1)}, bf16[2,8,64,256]{3,2,1,0:T(8,128)(2,1)S(1)}, u32[]{:S(2)}, u32[]{:S(2)}) collective-permute-start(bf16[2,8,64,256]{3,2,1,0:T(8,128)(2,1)} %get-tuple-element.40), channel_id=1, source_target_pairs={{0,2},{2,4},{4,6},{6,0},{1,3},{3,5},{5,7},{7,1},{8,10},{10,12},{12... | collective-permute-start | bytes 1572872 | tf_op jit(solution)/shard_map/ppermute | solution.py:475
  38.8 26.2 %collective-permute-start.3 = (bf16[2,8,64,256]{3,2,1,0:T(8,128)(2,1)}, bf16[2,8,64,256]{3,2,1,0:T(8,128)(2,1)S(1)}, u32[]{:S(2)}, u32[]{:S(2)}) collective-permute-start(bf16[2,8,64,256]{3,2,1,0:T(8,128)(2,1)} %get-tuple-element.41), channel_id=1, source_target_pairs={{0,4},{2,6},{4,0},{6,2},{1,5},{3,7},{5,1},{7,3},{8,12},{10,14},{12... | collective-permute-start | bytes 1572872 | tf_op jit(solution)/shard_map/ppermute | solution.py:475
  41.7 23.3 %collective-permute-start.4 = (bf16[2,8,64,256]{3,2,1,0:T(8,128)(2,1)S(1)}, bf16[2,8,64,256]{3,2,1,0:T(8,128)(2,1)S(1)}, u32[]{:S(2)}, u32[]{:S(2)}) collective-permute-start(bf16[2,8,64,256]{3,2,1,0:T(8,128)(2,1)S(1)} %copy-done.18), channel_id=1, source_target_pairs={{0,6},{2,0},{4,2},{6,4},{1,7},{3,1},{5,3},{7,5},{8,14},{10,8},{12,... | collective-permute-start | bytes 1572872 | tf_op jit(solution)/shard_map/ppermute | solution.py:475
  65.5 6.2 %collective-permute-start.6 = (bf16[256,2048]{1,0:T(8,128)(2,1)S(1)}, bf16[256,2048]{1,0:T(8,128)(2,1)S(1)}, u32[]{:S(2)}, u32[]{:S(2)}) collective-permute-start(bf16[256,2048]{1,0:T(8,128)(2,1)S(1)} %get-tuple-element.46), channel_id=1, source_target_pairs={{0,64},{64,0},{1,65},{65,1},{2,66},{66,2},{3,67},{67,3},{4,68},{68... | collective-permute-start | bytes 3145736 | tf_op jit(solution)/shard_map/ppermute | solution.py:470
  65.6 11.4 %collective-permute-start.13 = (bf16[8,64,256]{2,1,0:T(8,128)(2,1)S(1)}, bf16[8,64,256]{2,1,0:T(8,128)(2,1)S(1)}, u32[]{:S(2)}, u32[]{:S(2)}) collective-permute-start(bf16[8,64,256]{2,1,0:T(8,128)(2,1)S(1)} %get-tuple-element.51), channel_id=1, source_target_pairs={{0,1},{1,0},{2,3},{3,2},{4,5},{5,4},{6,7},{7,6},{8,9},{9,8},{10,11... | collective-permute-start | bytes 786440 | tf_op jit(solution)/shard_map/ppermute | solution.py:475
  66.6 10.5 %collective-permute-start.14 = (bf16[8,64,256]{2,1,0:T(8,128)(2,1)S(1)}, bf16[8,64,256]{2,1,0:T(8,128)(2,1)S(1)}, u32[]{:S(2)}, u32[]{:S(2)}) collective-permute-start(bf16[8,64,256]{2,1,0:T(8,128)(2,1)S(1)} %get-tuple-element.53), channel_id=1, source_target_pairs={{0,2},{2,4},{4,6},{6,0},{1,3},{3,5},{5,7},{7,1},{8,10},{10,12},{12... | collective-permute-start | bytes 786440 | tf_op jit(solution)/shard_map/ppermute | solution.py:475
  67.5 14.5 %collective-permute-start.15 = (bf16[8,64,256]{2,1,0:T(8,128)(2,1)S(1)}, bf16[8,64,256]{2,1,0:T(8,128)(2,1)S(1)}, u32[]{:S(2)}, u32[]{:S(2)}) collective-permute-start(bf16[8,64,256]{2,1,0:T(8,128)(2,1)S(1)} %get-tuple-element.54), channel_id=1, source_target_pairs={{0,4},{2,6},{4,0},{6,2},{1,5},{3,7},{5,1},{7,3},{8,12},{10,14},{12... | collective-permute-start | bytes 786440 | tf_op jit(solution)/shard_map/ppermute | solution.py:475
  70.1 12.2 %collective-permute-start.16 = (bf16[8,64,256]{2,1,0:T(8,128)(2,1)S(1)}, bf16[8,64,256]{2,1,0:T(8,128)(2,1)S(1)}, u32[]{:S(2)}, u32[]{:S(2)}) collective-permute-start(bf16[8,64,256]{2,1,0:T(8,128)(2,1)S(1)} %get-tuple-element.55), channel_id=1, source_target_pairs={{0,6},{2,0},{4,2},{6,4},{1,7},{3,1},{5,3},{7,5},{8,14},{10,8},{12,... | collective-permute-start | bytes 786440 | tf_op jit(solution)/shard_map/ppermute | solution.py:475
  73.2 27.3 %collective-permute-start.7 = (bf16[256,2048]{1,0:T(8,128)(2,1)}, bf16[256,2048]{1,0:T(8,128)(2,1)}, u32[]{:S(2)}, u32[]{:S(2)}) collective-permute-start(bf16[256,2048]{1,0:T(8,128)(2,1)} %fusion.1), channel_id=1, source_target_pairs={{128,129},{129,128},{130,131},{131,130},{132,133},{133,132},{134,1... | collective-permute-start | bytes 3145736 | tf_op jit(solution)/shard_map/ppermute | solution.py:509
  83.4 25.2 %all-to-all-start = ((bf16[8,64,512]{2,1,0:T(8,128)(2,1)}), bf16[8,64,512]{2,1,0:T(8,128)(2,1)S(1)}, u32[]{:S(2)}, u32[]{:S(2)}) async-start(bf16[8,64,512]{2,1,0:T(8,128)(2,1)} %shard_map.100), calls=%async_computation.1 | async-start | bytes 1048576 | tf_op jit(solution)/shard_map/all_to_all | solution.py:479
  91.8 96.0 %all-gather.2.cloned.1.call-start = ((), (), s32[]{:S(2)}) async-start(), calls=%async_computation.4 | async-start | bytes 4718592 | tf_op jit(solution)/shard_map/all_gather | solution.py:522
  95.4 7.8 %collective-permute-start.10 = (bf16[2,64,512]{2,1,0:T(8,128)(2,1)S(1)}, bf16[2,64,512]{2,1,0:T(8,128)(2,1)S(1)}, u32[]{:S(2)}, u32[]{:S(2)}) collective-permute-start(bf16[2,64,512]{2,1,0:T(8,128)(2,1)S(1)} %bitcast.38), channel_id=1, source_target_pairs={{0,4},{2,6},{4,0},{6,2},{1,5},{3,7},{5,1},{7,3},{8,12},{10,14},{12... | collective-permute-start | bytes 393224 | tf_op jit(solution)/shard_map/ppermute | solution.py:475
  98.5 6.7 %collective-permute-start.11 = (bf16[2,64,512]{2,1,0:T(8,128)(2,1)S(1)}, bf16[2,64,512]{2,1,0:T(8,128)(2,1)S(1)}, u32[]{:S(2)}, u32[]{:S(2)}) collective-permute-start(bf16[2,64,512]{2,1,0:T(8,128)(2,1)S(1)} %bitcast.37), channel_id=1, source_target_pairs={{0,6},{2,0},{4,2},{6,4},{1,7},{3,1},{5,3},{7,5},{8,14},{10,8},{12,... | collective-permute-start | bytes 393224 | tf_op jit(solution)/shard_map/ppermute | solution.py:475
  99.7 6.2 %collective-permute-start.9 = (bf16[2,64,512]{2,1,0:T(8,128)(2,1)S(1)}, bf16[2,64,512]{2,1,0:T(8,128)(2,1)S(1)}, u32[]{:S(2)}, u32[]{:S(2)}) collective-permute-start(bf16[2,64,512]{2,1,0:T(8,128)(2,1)S(1)} %bitcast.36), channel_id=1, source_target_pairs={{0,2},{2,4},{4,6},{6,0},{1,3},{3,5},{5,7},{7,1},{8,10},{10,12},{12... | collective-permute-start | bytes 393224 | tf_op jit(solution)/shard_map/ppermute | solution.py:475
  107.0 4.4 %collective-permute-start.12 = (bf16[64,512]{1,0:T(8,128)(2,1)S(1)}, bf16[64,512]{1,0:T(8,128)(2,1)S(1)}, u32[]{:S(2)}, u32[]{:S(2)}) collective-permute-start(bf16[64,512]{1,0:T(8,128)(2,1)S(1)} %get-tuple-element.49), channel_id=1, source_target_pairs={{0,1},{1,0},{2,3},{3,2},{4,5},{5,4},{6,7},{7,6},{8,9},{9,8},{10,11... | collective-permute-start | bytes 196616 | tf_op jit(solution)/shard_map/ppermute | solution.py:475
  113.8 6.0 %collective-permute-start.28 = (bf16[64,512]{1,0:T(8,128)(2,1)S(1)}, bf16[64,512]{1,0:T(8,128)(2,1)S(1)}, u32[]{:S(2)}, u32[]{:S(2)}) collective-permute-start(bf16[64,512]{1,0:T(8,128)(2,1)S(1)} %get-tuple-element.59), channel_id=1, source_target_pairs={{0,2},{2,4},{4,6},{6,0},{1,3},{3,5},{5,7},{7,1},{8,10},{10,12},{12... | collective-permute-start | bytes 196616 | tf_op jit(solution)/shard_map/ppermute | solution.py:475
  114.5 6.3 %collective-permute-start.27 = (bf16[64,512]{1,0:T(8,128)(2,1)S(1)}, bf16[64,512]{1,0:T(8,128)(2,1)S(1)}, u32[]{:S(2)}, u32[]{:S(2)}) collective-permute-start(bf16[64,512]{1,0:T(8,128)(2,1)S(1)} %get-tuple-element.59), channel_id=1, source_target_pairs={{0,4},{2,6},{4,0},{6,2},{1,5},{3,7},{5,1},{7,3},{8,12},{10,14},{12... | collective-permute-start | bytes 196616 | tf_op jit(solution)/shard_map/ppermute | solution.py:475
  117.3 4.3 %collective-permute-start.26 = (bf16[64,512]{1,0:T(8,128)(2,1)S(1)}, bf16[64,512]{1,0:T(8,128)(2,1)S(1)}, u32[]{:S(2)}, u32[]{:S(2)}) collective-permute-start(bf16[64,512]{1,0:T(8,128)(2,1)S(1)} %get-tuple-element.59), channel_id=1, source_target_pairs={{0,6},{2,0},{4,2},{6,4},{1,7},{3,1},{5,3},{7,5},{8,14},{10,8},{12,... | collective-permute-start | bytes 196616 | tf_op jit(solution)/shard_map/ppermute | solution.py:475
  121.6 7.6 %collective-permute-start.29 = (bf16[256,512]{1,0:T(8,128)(2,1)S(1)}, bf16[256,512]{1,0:T(8,128)(2,1)S(1)}, u32[]{:S(2)}, u32[]{:S(2)}) collective-permute-start(bf16[256,512]{1,0:T(8,128)(2,1)S(1)} %pad_maximum_fusion), channel_id=1, source_target_pairs={{0,1},{1,0},{2,3},{3,2},{4,5},{5,4},{6,7},{7,6},{8,9},{9,8},{10,11... | collective-permute-start | bytes 786440 | tf_op jit(solution)/shard_map/ppermute | solution.py:475
  130.1 24.7 %all-to-all-start.1 = ((bf16[8,64,512]{2,1,0:T(8,128)(2,1)}), bf16[8,64,512]{2,1,0:T(8,128)(2,1)S(1)}, u32[]{:S(2)}, u32[]{:S(2)}) async-start(bf16[8,64,512]{2,1,0:T(8,128)(2,1)} %get-tuple-element.58), calls=%async_computation.2 | async-start | bytes 1048576 | tf_op jit(solution)/shard_map/all_to_all | solution.py:479
  134.4 45.0 %collective-permute-start.8 = (bf16[256,2048]{1,0:T(8,128)(2,1)}, bf16[256,2048]{1,0:T(8,128)(2,1)}, u32[]{:S(2)}, u32[]{:S(2)}) collective-permute-start(bf16[256,2048]{1,0:T(8,128)(2,1)} %collective-permute-done.7), channel_id=1, source_target_pairs={{128,1},{129,0},{130,3},{131,2},{132,5},{133,4},{134,7},{135,6},{1... | collective-permute-start | bytes 3145736 | tf_op jit(solution)/shard_map/ppermute | solution.py:510
  154.9 6.5 %collective-permute-start.18 = (bf16[8,64,256]{2,1,0:T(8,128)(2,1)S(1)}, bf16[8,64,256]{2,1,0:T(8,128)(2,1)S(1)}, u32[]{:S(2)}, u32[]{:S(2)}) collective-permute-start(bf16[8,64,256]{2,1,0:T(8,128)(2,1)S(1)} %get-tuple-element.63), channel_id=1, source_target_pairs={{0,1},{1,0},{2,3},{3,2},{4,5},{5,4},{6,7},{7,6},{8,9},{9,8},{10,11... | collective-permute-start | bytes 786440 | tf_op jit(solution)/shard_map/ppermute | solution.py:475
  156.0 7.6 %collective-permute-start.24 = (bf16[8,64,256]{2,1,0:T(8,128)(2,1)S(1)}, bf16[8,64,256]{2,1,0:T(8,128)(2,1)S(1)}, u32[]{:S(2)}, u32[]{:S(2)}) collective-permute-start(bf16[8,64,256]{2,1,0:T(8,128)(2,1)S(1)} %get-tuple-element.62), channel_id=1, source_target_pairs={{0,2},{2,4},{4,6},{6,0},{1,3},{3,5},{5,7},{7,1},{8,10},{10,12},{12... | collective-permute-start | bytes 786440 | tf_op jit(solution)/shard_map/ppermute | solution.py:475
  157.4 10.4 %collective-permute-start.23 = (bf16[8,64,256]{2,1,0:T(8,128)(2,1)S(1)}, bf16[8,64,256]{2,1,0:T(8,128)(2,1)S(1)}, u32[]{:S(2)}, u32[]{:S(2)}) collective-permute-start(bf16[8,64,256]{2,1,0:T(8,128)(2,1)S(1)} %get-tuple-element.62), channel_id=1, source_target_pairs={{0,4},{2,6},{4,0},{6,2},{1,5},{3,7},{5,1},{7,3},{8,12},{10,14},{12... | collective-permute-start | bytes 786440 | tf_op jit(solution)/shard_map/ppermute | solution.py:475
  160.1 8.1 %collective-permute-start.22 = (bf16[8,64,256]{2,1,0:T(8,128)(2,1)S(1)}, bf16[8,64,256]{2,1,0:T(8,128)(2,1)S(1)}, u32[]{:S(2)}, u32[]{:S(2)}) collective-permute-start(bf16[8,64,256]{2,1,0:T(8,128)(2,1)S(1)} %get-tuple-element.62), channel_id=1, source_target_pairs={{0,6},{2,0},{4,2},{6,4},{1,7},{3,1},{5,3},{7,5},{8,14},{10,8},{12,... | collective-permute-start | bytes 786440 | tf_op jit(solution)/shard_map/ppermute | solution.py:475
  169.3 23.2 %collective-permute-start.25 = (bf16[4,8,64,256]{3,2,1,0:T(8,128)(2,1)}, bf16[4,8,64,256]{3,2,1,0:T(8,128)(2,1)}, u32[]{:S(2)}, u32[]{:S(2)}) collective-permute-start(bf16[4,8,64,256]{3,2,1,0:T(8,128)(2,1)} %shard_map.104.refs_1_), channel_id=1, source_target_pairs={{0,1},{1,0},{2,3},{3,2},{4,5},{5,4},{6,7},{7,6},{8,9},{9,8},{10,11... | collective-permute-start | bytes 3145736 | tf_op jit(solution)/shard_map/ppermute | solution.py:475
  170.1 22.3 %collective-permute-start.21 = (bf16[2,8,64,256]{3,2,1,0:T(8,128)(2,1)}, bf16[2,8,64,256]{3,2,1,0:T(8,128)(2,1)}, u32[]{:S(2)}, u32[]{:S(2)}) collective-permute-start(bf16[2,8,64,256]{3,2,1,0:T(8,128)(2,1)} %shard_map.103.refs_0_), channel_id=1, source_target_pairs={{0,2},{2,4},{4,6},{6,0},{1,3},{3,5},{5,7},{7,1},{8,10},{10,12},{12... | collective-permute-start | bytes 1572872 | tf_op jit(solution)/shard_map/ppermute | solution.py:475
  170.1 22.3 %collective-permute-start.20 = (bf16[2,8,64,256]{3,2,1,0:T(8,128)(2,1)}, bf16[2,8,64,256]{3,2,1,0:T(8,128)(2,1)}, u32[]{:S(2)}, u32[]{:S(2)}) collective-permute-start(bf16[2,8,64,256]{3,2,1,0:T(8,128)(2,1)} %shard_map.103.refs_0_), channel_id=1, source_target_pairs={{0,4},{2,6},{4,0},{6,2},{1,5},{3,7},{5,1},{7,3},{8,12},{10,14},{12... | collective-permute-start | bytes 1572872 | tf_op jit(solution)/shard_map/ppermute | solution.py:475
  179.3 13.1 %collective-permute-start.19 = (bf16[2,8,64,256]{3,2,1,0:T(8,128)(2,1)}, bf16[2,8,64,256]{3,2,1,0:T(8,128)(2,1)}, u32[]{:S(2)}, u32[]{:S(2)}) collective-permute-start(bf16[2,8,64,256]{3,2,1,0:T(8,128)(2,1)} %shard_map.103.refs_0_), channel_id=1, source_target_pairs={{0,6},{2,0},{4,2},{6,4},{1,7},{3,1},{5,3},{7,5},{8,14},{10,8},{12,... | collective-permute-start | bytes 1572872 | tf_op jit(solution)/shard_map/ppermute | solution.py:475
  (21 other events, 141.6 us)
Sparse Core Ops, SparseCore 0:
  36.1 58.2 reduce-scatter.1
  130.2 57.5 all-gather.1

commit v2 on v1

--- a/solution.py
+++ b/solution.py
@@ -18,6 +18,7 @@
 F32, BF16 = jnp.float32, jnp.bfloat16
 PARAMS = pltpu.CompilerParams(vmem_limit_bytes=32 * 1024 * 1024)
 WIDE = pltpu.CompilerParams(vmem_limit_bytes=56 * 1024 * 1024)
+LESS = pltpu.CompilerParams(vmem_limit_bytes=48 * 1024 * 1024)
 ANY = pl.BlockSpec(memory_space=pl.ANY)
 VMEM = pl.BlockSpec(memory_space=pltpu.VMEM)
 
@@ -27,12 +28,14 @@
     return momentum_decay * m.astype(F32) + (1.0 - momentum_decay) * grad
 
 
-def local_part(x_ref, g_ref, m_ref, out_ref, sums_ref):
+def local_part(where_ref, x_ref, g_ref, m_ref, out_ref, sums_ref):
     local = local_block(x_ref[...], g_ref[...], m_ref[...])
     out_ref[...] = local.astype(BF16)
     rows, cols = local.shape
-    per_span = jnp.sum(jnp.abs(local).reshape(rows // SPAN, SPAN, cols), axis=1)
-    sums_ref[...] = in_lanes(per_span)
+    spans = rows // SPAN
+    per_span = jnp.sum(jnp.abs(local).reshape(spans, SPAN, cols), axis=1)
+    at = pl.multiple_of((where_ref[0] + pl.program_id(0)) * spans, spans)
+    sums_ref[pl.ds(at, spans), :] = in_lanes(per_span)
 
 
 def in_lanes(values):
@@ -42,60 +45,60 @@
     return total
 
 
-def own_kernel(seqs, where_ref, x_ref, g_ref, m_ref, out_ref, sums_ref, used_ref):
+def own_kernel(where_ref, lengths_ref, x_ref, g_ref, m_ref, out_ref, sums_ref, used_ref):
     @pl.when(pl.program_id(0) == 0)
     def _():
+        sums_ref[...] = jnp.zeros_like(sums_ref)
+        seqs = lengths_ref.shape[0]
         slots = used_ref.shape[0] // seqs
         for seq in range(seqs):
             rows = slice(seq * slots, (seq + 1) * slots)
             grads = g_ref[rows, :].astype(F32)
             slot = lax.broadcasted_iota(jnp.int32, grads.shape, 0)
-            used_ref[rows, :] = jnp.where(slot < where_ref[1 + seq], grads, 0.0).astype(BF16)
-
-    local_part(x_ref, used_ref, m_ref, out_ref, sums_ref)
+            used_ref[rows, :] = jnp.where(slot < lengths_ref[seq], grads, 0.0).astype(BF16)
+
+    local_part(where_ref, x_ref, used_ref, m_ref, out_ref, sums_ref)
 
 
 def other_kernel(where_ref, x_ref, g_ref, m_ref, all_sums_ref, out_ref, sums_ref):
-    local_part(x_ref, g_ref, m_ref, out_ref, sums_ref)
+    @pl.when(pl.program_id(0) == 0)
+    def _():
+        sums_ref[...] = all_sums_ref[...]
+
+    local_part(where_ref, x_ref, g_ref, m_ref, out_ref, sums_ref)
 
 
 def local_momentum(x, g, m, first, lengths=None, sums=None):
     tokens, feats = x.shape
     width, cols = m.shape
     rows = Y * X * SPAN
-    where, kernel, more, used = first.reshape(1), other_kernel, [sums], []
+    scalars, kernel, more, used = [first.reshape(1)], other_kernel, [sums], []
     if lengths is not None:
-        where = jnp.concatenate([where, lengths])
-        kernel = functools.partial(own_kernel, lengths.shape[0])
-        more, used = [], [pl.BlockSpec((tokens, cols), lambda i, w: (0, 0))]
+        scalars, kernel, more = [*scalars, lengths], own_kernel, []
+        used = [pl.BlockSpec((tokens, cols), lambda i, *w: (0, 0))]
     return pl.pallas_call(
         kernel,
         grid_spec=pltpu.PrefetchScalarGridSpec(
-            num_scalar_prefetch=1,
+            num_scalar_prefetch=len(scalars),
             grid=(feats // rows,),
             in_specs=[
-                pl.BlockSpec((tokens, rows), lambda i, w: (0, i)),
-                pl.BlockSpec((tokens, cols), lambda i, w: (0, 0)),
-                pl.BlockSpec((rows, cols), lambda i, w: (w[0] + i, 0)),
+                pl.BlockSpec((tokens, rows), lambda i, *w: (0, i)),
+                pl.BlockSpec((tokens, cols), lambda i, *w: (0, 0)),
+                pl.BlockSpec((rows, cols), lambda i, *w: (w[0][0] + i, 0)),
             ]
-            + [ANY] * len(more),
-            out_specs=[
-                pl.BlockSpec((rows, cols), lambda i, w: (i, 0)),
-                pl.BlockSpec((rows // SPAN, 128), lambda i, w: (w[0] + i, 0)),
-            ]
-            + used,
+            + [VMEM] * len(more),
+            out_specs=[pl.BlockSpec((rows, cols), lambda i, *w: (i, 0)), VMEM] + used,
         ),
         out_shape=[
             pltpu.HBM((feats, cols), BF16),
             jax.ShapeDtypeStruct((width // SPAN, 128), F32),
         ]
         + [jax.ShapeDtypeStruct((tokens, cols), BF16)] * len(used),
-        input_output_aliases={4: 1} if more else {},
         compiler_params=WIDE,
         cost_estimate=pl.CostEstimate(
             flops=2 * tokens * feats * cols, bytes_accessed=4 * feats * cols, transcendentals=0
         ),
-    )(where, x, g, m, *more)
+    )(*scalars, x, g, m, *more)
 
 
 def squash(local, scale):
@@ -116,13 +119,14 @@
 def compress_kernel(where_ref, own_ref, other_ref, s_ref, t_ref, z_ref, *outs):
     my_y, my_x = where_ref[1], where_ref[2]
     cut = z_ref.shape[1]
+    z = lax.rem(where_ref[0] + pl.program_id(0), Z)
 
     def run(local_ref):
         for k in range(Y * X):
             dy, dx = k // X, k % X
             j = lax.rem(my_y + dy, Y) * X + lax.rem(my_x + dx, X)
             rows = pl.ds(pl.multiple_of(j * SPAN, SPAN), SPAN)
-            scale = scale_of(s_ref, t_ref, pl.ds(j, 1), SPAN * local_ref.shape[1] * 2)
+            scale = scale_of(s_ref, t_ref, pl.ds(z * Y * X + j, 1), SPAN * local_ref.shape[1] * 2)
             packed = squash(local_ref[rows, :].astype(F32), scale)
             z_ref[k * SPAN : (k + 1) * SPAN] = packed[:, :cut]
             outs[dy][dx, 0] = packed[:, cut : cut + COLS_Y]
@@ -132,11 +136,14 @@
 
 
 def error_kernel(where_ref, own_ref, other_ref, s_ref, t_ref, err_ref):
+    z = lax.rem(where_ref[0] + pl.program_id(0), Z)
+
     def run(local_ref):
         for j in range(Y * X):
             rows = pl.ds(j * SPAN, SPAN)
             local = local_ref[rows, :].astype(F32)
-            packed = squash(local, scale_of(s_ref, t_ref, pl.ds(j, 1), SPAN * local.shape[1] * 2))
+            scale = scale_of(s_ref, t_ref, pl.ds(z * Y * X + j, 1), SPAN * local.shape[1] * 2)
+            packed = squash(local, scale)
             err_ref[rows, :] = (local - packed.astype(F32)).astype(BF16)
 
     halves(run, own_ref, other_ref)
@@ -153,8 +160,8 @@
     in_specs = [
         pl.BlockSpec((rows, cols), lambda i, w: (jnp.minimum(i, half - 1), 0)),
         pl.BlockSpec((rows, cols), lambda i, w: (jnp.maximum(i - half, 0), 0)),
-        pl.BlockSpec((rows // SPAN, 128), lambda i, w: (whole(i, w), 0)),
-        pl.BlockSpec((rows // SPAN, 128), lambda i, w: (whole(i, w), 0)),
+        VMEM,
+        VMEM,
     ]
     return (2 * half,), in_specs, whole
 
@@ -177,7 +184,7 @@
         out_shape=[pltpu.HBM((width, cut), BF16)]
         + [pltpu.HBM((X, Z, SPAN, COLS_Y), BF16)] * Y
         + [pltpu.HBM((Y, Z, SPAN, COLS_X), BF16)] * X,
-        compiler_params=WIDE,
+        compiler_params=LESS,
         cost_estimate=pl.CostEstimate(
             flops=8 * width * cols, bytes_accessed=4 * width * cols, transcendentals=0
         ),
@@ -285,12 +292,12 @@
 
 def y_sum_kernel(own_ref, *refs):
     kept_ref, given_ref = refs[-2:]
-    kept_ref[...] = added([own_ref.at[0, 0]] + [ref.at[0] for ref in refs[: Y - 1]])
-    given_ref[...] = added([own_ref.at[0, 1]] + [ref.at[1] for ref in refs[: Y - 1]]).astype(BF16)
+    kept_ref[...] = added([own_ref.at[0]] + [ref.at[0] for ref in refs[: Y - 1]])
+    given_ref[...] = added([own_ref.at[1]] + [ref.at[1] for ref in refs[: Y - 1]]).astype(BF16)
 
 
 def y_sum(own, parts, after):
-    shape = own.shape[2:]
+    shape = own.shape[1:]
     return pl.pallas_call(
         y_sum_kernel,
         in_specs=[VMEM] * (1 + len(parts)) + [ANY],
@@ -429,7 +436,7 @@
     for z in range(Z):
         incoming[z].wait()
         for k in range(z * places, (z + 1) * places):
-            rows = rows_of(where_ref, z, k % Y, k // Y % X)
+            rows = rows_of(where_ref, z, k // X % Y, k % X)
             source = held.at[pl.ds(k * SPAN, SPAN)]
             outgoing.append(pltpu.make_async_copy(source, out_ref.at[rows, pl.ds(0, cut)], sems.at[k]))
             outgoing[-1].start()
@@ -512,13 +519,13 @@
 
     arrived_b = exchanged(sum_plane, "z")
     own_a = part_z.reshape(Y, X, SPAN, cut)
-    kept_a, given_a = y_sum(own_a, [along(own_a[k], "y", k) for k in range(1, Y)], nearer[:16, :128])
+    kept_a, given_a = y_sum(own_a[0], [along(own_a[k], "y", k) for k in range(1, Y)], nearer[:16, :128])
     averaged, magnitudes = server_sum(kept_a, along(given_a, "x", 1), arrived_b)
 
     server_error, owned_a, owned_b = owned_momentum(averaged, magnitudes, over_tensor(magnitudes))
 
-    ring_a = jnp.concatenate([owned_a] + [along(owned_a, "y", -k) for k in range(1, Y)])
-    plane_a = jnp.concatenate([ring_a, along(ring_a, "x", 1)])
+    pair_a = jnp.concatenate([owned_a, along(owned_a, "x", 1)])
+    plane_a = jnp.concatenate([pair_a] + [along(pair_a, "y", -k) for k in range(1, Y)])
     all_a = lax.all_gather(plane_a, "z", axis=0, tiled=True)
     all_z = exchanged(owned_b, "z")
     first_y, first_x = all_z[:, :, :WIDE_Y], all_z[:, :, WIDE_Y:]

time: 206 us -> 203 us (0.985)
  waiting for transfers between devices: 59 us -> 66.5 us
  starting transfers between devices: 61.1 us -> 53.9 us
    ppermute x24, starting transfers between devices: 41 us -> 33.5 us  [along(): lax.ppermute(value, axis, [(i, (i + steps) % count) for i in range(count)])]
    all_gather x1, waiting for transfers between devices: 3.05 us -> 8.98 us  [shards(): all_a = lax.all_gather(plane_a, 'z', axis=0, tiled=True)]
    unnamed x42 -> x37, local copies, waits for them, and re-layouts: 6.88 us -> 5.98 us
  transfers between devices with their start and end apart: 34 -> 34, of which waited for: 21 -> 20; matrix products, arithmetic and copies ran while one was open for 4% -> 3% of each run, Pallas kernels for 15% -> 16%
where the time goes in v2:
time: 203 us; the launch traced here: 200 us
  waiting for transfers between devices  66.5 us (33%)
  starting transfers between devices  53.9 us (27%)
  Pallas kernels  52.9 us (26%)
  between operations  14.4 us (7%)
  local copies, waits for them, and re-layouts  9.23 us (5%)
  other arithmetic  3.45 us (2%)
    ppermute x24, waiting for transfers between devices, along(): lax.ppermute(value, axis, [(i, (i + steps) % count) for i in range(count)])  34.1 us
    ppermute x24, starting transfers between devices, along(): lax.ppermute(value, axis, [(i, (i + steps) % count) for i in range(count)])  33.5 us
    all_to_all x2, waiting for transfers between devices, exchanged(): return lax.all_to_all(value, axes, split_axis=0, concat_axis=0, tiled=True)  18.8 us
    pallas_call x2, Pallas kernels, local_momentum(): pl.pallas_call(kernel, grid_spec=pltpu.PrefetchScalarGridSpec(num_scalar_...  13.6 us
    all_to_all x2, starting transfers between devices, exchanged(): return lax.all_to_all(value, axes, split_axis=0, concat_axis=0, tiled=True)  12.8 us
    pallas_call x3, Pallas kernels, call(): pl.pallas_call(kernel, grid_spec=pltpu.PrefetchScalarGridSpec(num_scalar_...  12.5 us
    pallas_call x1, Pallas kernels, compress(): pl.pallas_call(compress_kernel, grid_spec=pltpu.PrefetchScalarGridSpec(nu...  9.59 us
    all_gather x1, waiting for transfers between devices, shards(): all_a = lax.all_gather(plane_a, 'z', axis=0, tiled=True)  8.98 us
  transfers between devices with their start and end apart: 34, of which 20 were waited for; matrix products, arithmetic and copies ran while one was open for 3% of the time, Pallas kernels for 16%

profile of v2, /device:TPU:4, one launch (start us, length us, event | category | flops | bytes accessed | tf_op | source)
XLA Modules:
  0.0 200.3 jit_solution(16227699199408537169)
XLA Ops:
  7.3 7.1 %shard_map.93 = (bf16[2048,1024]{1,0:T(8,128)(2,1)}, f32[64,128]{1,0:T(8,128)}, bf16[256,1024]{1,0:T(8,128)(2,1)}) custom-call(s32[1]{0:T(128)} %bitcast.2.where_ref, s32[4]{0:T(128)} %lengths_ref.1, bf16[256,2048]{1,0:T(8,128)(2,1)} %bitcast.34, bf16[256,1024]{1,0:T(8,128)(2,1)} %bitcast.35, bf16[4096,1024]{1,0:T(8,128)(2,1)} %bitcast.30), custom_call_target="tpu_custom_call" | custom-call | flops 1073741824 | bytes 8388608 | tf_op jit(solution)/shard_map/pallas_call | solution.py:79
  15.4 6.5 %shard_map.95 = (bf16[2048,1024]{1,0:T(8,128)(2,1)}, f32[64,128]{1,0:T(8,128)}) custom-call(s32[1]{0:T(128)} %bitcast.9.where_ref, bf16[256,2048]{1,0:T(8,128)(2,1)} %copy-done.14, bf16[256,1024]{1,0:T(8,128)(2,1)} %get-tuple-element.33.g_ref, bf16[4096,1024]{1,0:T(8,128)(2,1)} %bitcast.31, f32[64,128]{1,0:T(8,128)} %get-tuple-element.36.all_sums_ref), custom_call_target="tpu_custom_call" | custom-call | flops 1073741824 | bytes 8388608 | tf_op jit(solution)/shard_map/pallas_call | solution.py:79
  24.2 9.6 %shard_map.96 = (bf16[4096,512]{1,0:T(8,128)(2,1)}, bf16[2,8,64,256]{3,2,1,0:T(8,128)(2,1)}, bf16[2,8,64,256]{3,2,1,0:T(8,128)(2,1)}, bf16[2,8,64,256]{3,2,1,0:T...) custom-call(s32[3]{0:T(128)S(1)} %pad_add_fusion.where_ref, ...), custom_call_target="tpu_custom_call" | custom-call | flops 33554432 | bytes 16777216 | tf_op jit(solution)/shard_map/pallas_call | solution.py:174
  36.7 2.9 %collective-permute-start.3 = (bf16[2,8,64,256]{3,2,1,0:T(8,128)(2,1)}, bf16[2,8,64,256]{3,2,1,0:T(8,128)(2,1)S(1)}, u32[]{:S(2)}, u32[]{:S(2)}) collective-permute-start(bf16[2,8,64,256]{3,2,1,0:T(8,128)(2,1)} %get-tuple-element.41), channel_id=1, source_target_pairs={{0,4},{2,6},{4,0},{6,2},{1,5},{3,7},{5,1},{7,3},{8,12},{10,14},{12... | collective-permute-start | bytes 1572872 | tf_op jit(solution)/shard_map/ppermute | solution.py:482
  40.9 3.4 %copy-done.3 = bf16[1,4096,1024]{2,1,0:T(8,128)(2,1)S(1)} copy-done((bf16[1,4096,1024]{2,1,0:T(8,128)(2,1)S(1)}, bf16[1,4096,1024]{2,1,0:T(8,128)(2,1)}, u32[]{:S(2)}) %copy-start.3) | copy-done | bytes 8388632
  44.3 4.5 %shard_map.94 = (f32[256,2048]{1,0:T(8,128)S(1)}, bf16[256,2048]{1,0:T(8,128)(2,1)S(1)}) custom-call(s32[1]{0:T(128)} %bitcast.1.where_ref, bf16[256,1024]{1,0:T(8,128)(2,1)S(1)} %copy-done.5, bf16[4096,1024]{1,0:T(8,128)(2,1)S(1)} %bitcast.26), custom_call_target="tpu_custom_call" | custom-call | flops 2147483648 | bytes 12582912 | tf_op jit(solution)/shard_map/pallas_call | solution.py:377
  48.8 8.2 %shard_map.97.refs_7_ = bf16[4096,1024]{1,0:T(8,128)(2,1)} custom-call(s32[3]{0:T(128)S(1)} %pad_add_fusion.where_ref, bf16[2048,1024]{1,0:T(8,128)(2,1)S(1)} %copy-done.1, bf16[2048,1024]{1,0:T(8,128)(2,1)S(1)} %copy-done.2, f32[64,128]{1,0:T(8,128)S(1)} %copy-done.9, f32[64,128]{1,0:T(8,128)S(1)} %collective-permute-done.1.t_ref), custom_call_target="tpu_custom_call" | custom-call | flops 4096 | bytes 4096 | tf_op jit(solution)/shard_map/pallas_call | solution.py:198
  57.0 5.8 %collective-permute-done.3.refs_2_ = bf16[2,8,64,256]{3,2,1,0:T(8,128)(2,1)S(1)} collective-permute-done((bf16[2,8,64,256]{3,2,1,0:T(8,128)(2,1)}, bf16[2,8,64,256]{3,2,1,0:T(8,128)(2,1)S(1)}, u32[]{:S(2)}, u32[]{:S(2)}) %collective-permute-start.3) | collective-permute-done | bytes 524320 | tf_op jit(solution)/shard_map/ppermute | solution.py:482
  65.3 2.6 %collective-permute-start.15 = (bf16[8,64,256]{2,1,0:T(8,128)(2,1)S(1)}, bf16[8,64,256]{2,1,0:T(8,128)(2,1)S(1)}, u32[]{:S(2)}, u32[]{:S(2)}) collective-permute-start(bf16[8,64,256]{2,1,0:T(8,128)(2,1)S(1)} %get-tuple-element.54), channel_id=1, source_target_pairs={{0,4},{2,6},{4,0},{6,2},{1,5},{3,7},{5,1},{7,3},{8,12},{10,14},{12... | collective-permute-start | bytes 786440 | tf_op jit(solution)/shard_map/ppermute | solution.py:482
  71.1 3.1 %collective-permute-start.7 = (bf16[256,2048]{1,0:T(8,128)(2,1)}, bf16[256,2048]{1,0:T(8,128)(2,1)}, u32[]{:S(2)}, u32[]{:S(2)}) collective-permute-start(bf16[256,2048]{1,0:T(8,128)(2,1)} %fusion.1), channel_id=1, source_target_pairs={{128,129},{129,128},{130,131},{131,130},{132,133},{133,132},{134,1... | collective-permute-start | bytes 3145736 | tf_op jit(solution)/shard_map/ppermute | solution.py:516
  74.9 5.0 %collective-permute-done.15.refs_2_ = bf16[8,64,256]{2,1,0:T(8,128)(2,1)S(1)} collective-permute-done((bf16[8,64,256]{2,1,0:T(8,128)(2,1)S(1)}, bf16[8,64,256]{2,1,0:T(8,128)(2,1)S(1)}, u32[]{:S(2)}, u32[]{:S(2)}) %collective-permute-start.15) | collective-permute-done | bytes 262176 | tf_op jit(solution)/shard_map/ppermute | solution.py:482
  81.2 8.5 %all-to-all-start = ((bf16[8,64,512]{2,1,0:T(8,128)(2,1)}), bf16[8,64,512]{2,1,0:T(8,128)(2,1)S(1)}, u32[]{:S(2)}, u32[]{:S(2)}) async-start(bf16[8,64,512]{2,1,0:T(8,128)(2,1)} %shard_map.100), calls=%async_computation.1 | async-start | bytes 1048576 | tf_op jit(solution)/shard_map/all_to_all | solution.py:486
  89.7 2.5 %reduce-scatter.2.cloned.1.call-done = bf16[512,512]{1,0:T(8,128)(2,1)} async-done(((bf16[4096,512]{1,0:T(8,128)(2,1)}), bf16[512,512]{1,0:T(8,128)(2,1)}) %reduce-scatter.2.cloned.1.call-update) | async-done | bytes 524304 | tf_op jit(solution)/shard_map/reduce_scatter | solution.py:503
  93.3 3.1 %collective-permute-start.10 = (bf16[2,64,512]{2,1,0:T(8,128)(2,1)S(1)}, bf16[2,64,512]{2,1,0:T(8,128)(2,1)S(1)}, u32[]{:S(2)}, u32[]{:S(2)}) collective-permute-start(bf16[2,64,512]{2,1,0:T(8,128)(2,1)S(1)} %bitcast.38), channel_id=1, source_target_pairs={{0,4},{2,6},{4,0},{6,2},{1,5},{3,7},{5,1},{7,3},{8,12},{10,14},{12... | collective-permute-start | bytes 393224 | tf_op jit(solution)/shard_map/ppermute | solution.py:482
  99.1 2.0 %collective-permute-done.10.refs_1_ = bf16[2,64,512]{2,1,0:T(8,128)(2,1)S(1)} collective-permute-done((bf16[2,64,512]{2,1,0:T(8,128)(2,1)S(1)}, bf16[2,64,512]{2,1,0:T(8,128)(2,1)S(1)}, u32[]{:S(2)}, u32[]{:S(2)}) %collective-permute-start.10) | collective-permute-done | bytes 131104 | tf_op jit(solution)/shard_map/ppermute | solution.py:482
  101.2 1.9 collective-permute-done.11.refs_2_
  111.8 3.1 %collective-permute-done.26 = bf16[64,512]{1,0:T(8,128)(2,1)S(1)} collective-permute-done((bf16[64,512]{1,0:T(8,128)(2,1)S(1)}, bf16[64,512]{1,0:T(8,128)(2,1)S(1)}, u32[]{:S(2)}, u32[]{:S(2)}) %collective-permute-start.26) | collective-permute-done | bytes 65568 | tf_op jit(solution)/shard_map/ppermute | solution.py:482
  114.9 2.1 %collective-permute-start.27 = (bf16[128,512]{1,0:T(8,128)(2,1)S(1)}, bf16[128,512]{1,0:T(8,128)(2,1)S(1)}, u32[]{:S(2)}, u32[]{:S(2)}) collective-permute-start(bf16[128,512]{1,0:T(8,128)(2,1)S(1)} %get-tuple-element.68), channel_id=1, source_target_pairs={{0,6},{2,0},{4,2},{6,4},{1,7},{3,1},{5,3},{7,5},{8,14},{10,8},{12,... | collective-permute-start | bytes 393224 | tf_op jit(solution)/shard_map/ppermute | solution.py:482
  118.7 3.1 %collective-permute-done.27 = bf16[128,512]{1,0:T(8,128)(2,1)S(1)} collective-permute-done((bf16[128,512]{1,0:T(8,128)(2,1)S(1)}, bf16[128,512]{1,0:T(8,128)(2,1)S(1)}, u32[]{:S(2)}, u32[]{:S(2)}) %collective-permute-start.27) | collective-permute-done | bytes 131104 | tf_op jit(solution)/shard_map/ppermute | solution.py:482
  121.8 2.3 %collective-permute-done.28 = bf16[128,512]{1,0:T(8,128)(2,1)S(1)} collective-permute-done((bf16[128,512]{1,0:T(8,128)(2,1)S(1)}, bf16[128,512]{1,0:T(8,128)(2,1)S(1)}, u32[]{:S(2)}, u32[]{:S(2)}) %collective-permute-start.28) | collective-permute-done | bytes 131104 | tf_op jit(solution)/shard_map/ppermute | solution.py:482
  126.3 4.4 %all-to-all-start.1 = ((bf16[8,64,512]{2,1,0:T(8,128)(2,1)}), bf16[8,64,512]{2,1,0:T(8,128)(2,1)S(1)}, u32[]{:S(2)}, u32[]{:S(2)}) async-start(bf16[8,64,512]{2,1,0:T(8,128)(2,1)} %get-tuple-element.58), calls=%async_computation.2 | async-start | bytes 1048576 | tf_op jit(solution)/shard_map/all_to_all | solution.py:486
  130.6 3.6 %collective-permute-start.8 = (bf16[256,2048]{1,0:T(8,128)(2,1)}, bf16[256,2048]{1,0:T(8,128)(2,1)}, u32[]{:S(2)}, u32[]{:S(2)}) collective-permute-start(bf16[256,2048]{1,0:T(8,128)(2,1)} %collective-permute-done.7), channel_id=1, source_target_pairs={{128,1},{129,0},{130,3},{131,2},{132,5},{133,4},{134,7},{135,6},{1... | collective-permute-start | bytes 3145736 | tf_op jit(solution)/shard_map/ppermute | solution.py:517
  134.2 17.5 %all-to-all-done.1.all_ref = bf16[8,64,512]{2,1,0:T(8,128)(2,1)S(1)} async-done(((bf16[8,64,512]{2,1,0:T(8,128)(2,1)}), bf16[8,64,512]{2,1,0:T(8,128)(2,1)S(1)}, u32[]{:S(2)}, u32[]{:S(2)}) %all-to-all-start.1) | async-done | bytes 524320 | tf_op jit(solution)/shard_map/all_to_all | solution.py:486
  153.4 2.9 %collective-permute-start.22 = (bf16[8,64,256]{2,1,0:T(8,128)(2,1)S(1)}, bf16[8,64,256]{2,1,0:T(8,128)(2,1)S(1)}, u32[]{:S(2)}, u32[]{:S(2)}) collective-permute-start(bf16[8,64,256]{2,1,0:T(8,128)(2,1)S(1)} %get-tuple-element.62), channel_id=1, source_target_pairs={{0,6},{2,0},{4,2},{6,4},{1,7},{3,1},{5,3},{7,5},{8,14},{10,8},{12,... | collective-permute-start | bytes 786440 | tf_op jit(solution)/shard_map/ppermute | solution.py:482
  156.4 1.8 collective-permute-done.18.swapped_ref
  159.7 4.3 %collective-permute-done.24.refs_2_ = bf16[8,64,256]{2,1,0:T(8,128)(2,1)S(1)} collective-permute-done((bf16[8,64,256]{2,1,0:T(8,128)(2,1)S(1)}, bf16[8,64,256]{2,1,0:T(8,128)(2,1)S(1)}, u32[]{:S(2)}, u32[]{:S(2)}) %collective-permute-start.24) | collective-permute-done | bytes 262176 | tf_op jit(solution)/shard_map/ppermute | solution.py:482
  166.4 3.7 %collective-permute-start.20 = (bf16[2,8,64,256]{3,2,1,0:T(8,128)(2,1)}, bf16[2,8,64,256]{3,2,1,0:T(8,128)(2,1)}, u32[]{:S(2)}, u32[]{:S(2)}) collective-permute-start(bf16[2,8,64,256]{3,2,1,0:T(8,128)(2,1)} %shard_map.103.refs_0_), channel_id=1, source_target_pairs={{0,4},{2,6},{4,0},{6,2},{1,5},{3,7},{5,1},{7,3},{8,12},{10,14},{12... | collective-permute-start | bytes 1572872 | tf_op jit(solution)/shard_map/ppermute | solution.py:482
  170.1 1.9 add_convert_fusion.refs_5_
  172.0 3.5 %shard_map.105._ = bf16[4096,1024]{1,0:T(8,128)(2,1)} custom-call(s32[3]{0:T(128)S(1)} %pad_add_fusion.where_ref, bf16[2,8,64,256]{3,2,1,0:T(8,128)(2,1)} %shard_map.103.refs_0_, bf16[4,8,64,256]{3,2,1,0:T(8,128)(2,1)} %shard_map.104.refs_1_), custom_call_target="tpu_custom_call" | custom-call | bytes 8388608 | tf_op jit(solution)/shard_map/pallas_call | solution.py:451
  175.4 9.0 %all-gather.2.cloned.1.call-done.a_ref = bf16[4096,512]{1,0:T(8,128)(2,1)} async-done(((bf16[512,512]{1,0:T(8,128)(2,1)}), bf16[4096,512]{1,0:T(8,128)(2,1)}) %all-gather.2.cloned.1.call-update) | async-done | bytes 4194320 | tf_op jit(solution)/shard_map/all_gather | solution.py:529
  184.4 4.6 %shard_map.106.refs_4_ = bf16[4096,1024]{1,0:T(8,128)(2,1)} custom-call(s32[3]{0:T(128)S(1)} %pad_add_fusion.where_ref, bf16[4096,512]{1,0:T(8,128)(2,1)} %all-gather.2.cloned.1.call-done.a_ref, bf16[4096,1024]{1,0:T(8,128)(2,1)} %shard_map.105._), custom_call_target="tpu_custom_call", output_to_operand_aliasing={{}: (2, {})} | custom-call | bytes 8388608 | tf_op jit(solution)/shard_map/pallas_call | solution.py:451
  189.1 4.4 %shard_map.107 = bf16[4096,1024]{1,0:T(8,128)(2,1)} custom-call(s32[3]{0:T(128)S(1)} %pad_add_fusion.where_ref, bf16[2,8,64,256]{3,2,1,0:T(8,128)(2,1)} %collective-permute-done.19.refs_0_, bf16[2,8,64,256]{3,2,1,0:T(8,128)(2,1)} %collective-permute-done.20.refs_1_, ...), custom_call_target="tpu_custom_call", output_to_operand_aliasing={{}: (5, {})} | custom-call | bytes 8388608 | tf_op jit(solution)/shard_map/pallas_call | solution.py:451
  (100 shorter events, 37.4 us)
Async XLA Ops:
  7.2 85.0 %reduce-scatter.2.cloned.1.call-start = ((), (), s32[]{:S(2)}) async-start(), calls=%async_computation.3 | async-start | bytes 4718592 | tf_op jit(solution)/shard_map/reduce_scatter | solution.py:503
  7.2 7.2 %collective-permute-start = (bf16[256,2048]{1,0:T(8,128)(2,1)}, bf16[256,2048]{1,0:T(8,128)(2,1)S(1)}, u32[]{:S(2)}, u32[]{:S(2)}) collective-permute-start(bf16[256,2048]{1,0:T(8,128)(2,1)} %bitcast.33), channel_id=1, source_target_pairs={{0,64},{64,0},{1,65},{65,1},{2,66},{66,2},{3,67},{67,3},{4,68},{68... | collective-permute-start | bytes 3145736 | tf_op jit(solution)/shard_map/ppermute | solution.py:477
  33.8 29.0 %collective-permute-start.5 = (bf16[4,8,64,256]{3,2,1,0:T(8,128)(2,1)}, bf16[4,8,64,256]{3,2,1,0:T(8,128)(2,1)S(1)}, u32[]{:S(2)}, u32[]{:S(2)}) collective-permute-start(bf16[4,8,64,256]{3,2,1,0:T(8,128)(2,1)} %get-tuple-element.44), channel_id=1, source_target_pairs={{0,1},{1,0},{2,3},{3,2},{4,5},{5,4},{6,7},{7,6},{8,9},{9,8},{10,11... | collective-permute-start | bytes 3145736 | tf_op jit(solution)/shard_map/ppermute | solution.py:482
  35.1 21.9 %collective-permute-start.2 = (bf16[2,8,64,256]{3,2,1,0:T(8,128)(2,1)}, bf16[2,8,64,256]{3,2,1,0:T(8,128)(2,1)S(1)}, u32[]{:S(2)}, u32[]{:S(2)}) collective-permute-start(bf16[2,8,64,256]{3,2,1,0:T(8,128)(2,1)} %get-tuple-element.40), channel_id=1, source_target_pairs={{0,2},{2,4},{4,6},{6,0},{1,3},{3,5},{5,7},{7,1},{8,10},{10,12},{12... | collective-permute-start | bytes 1572872 | tf_op jit(solution)/shard_map/ppermute | solution.py:482
  36.7 26.2 %collective-permute-start.3 = (bf16[2,8,64,256]{3,2,1,0:T(8,128)(2,1)}, bf16[2,8,64,256]{3,2,1,0:T(8,128)(2,1)S(1)}, u32[]{:S(2)}, u32[]{:S(2)}) collective-permute-start(bf16[2,8,64,256]{3,2,1,0:T(8,128)(2,1)} %get-tuple-element.41), channel_id=1, source_target_pairs={{0,4},{2,6},{4,0},{6,2},{1,5},{3,7},{5,1},{7,3},{8,12},{10,14},{12... | collective-permute-start | bytes 1572872 | tf_op jit(solution)/shard_map/ppermute | solution.py:482
  39.6 23.3 %collective-permute-start.4 = (bf16[2,8,64,256]{3,2,1,0:T(8,128)(2,1)S(1)}, bf16[2,8,64,256]{3,2,1,0:T(8,128)(2,1)S(1)}, u32[]{:S(2)}, u32[]{:S(2)}) collective-permute-start(bf16[2,8,64,256]{3,2,1,0:T(8,128)(2,1)S(1)} %copy-done.16), channel_id=1, source_target_pairs={{0,6},{2,0},{4,2},{6,4},{1,7},{3,1},{5,3},{7,5},{8,14},{10,8},{12,... | collective-permute-start | bytes 1572872 | tf_op jit(solution)/shard_map/ppermute | solution.py:482
  63.4 6.2 %collective-permute-start.6 = (bf16[256,2048]{1,0:T(8,128)(2,1)S(1)}, bf16[256,2048]{1,0:T(8,128)(2,1)S(1)}, u32[]{:S(2)}, u32[]{:S(2)}) collective-permute-start(bf16[256,2048]{1,0:T(8,128)(2,1)S(1)} %get-tuple-element.46), channel_id=1, source_target_pairs={{0,64},{64,0},{1,65},{65,1},{2,66},{66,2},{3,67},{67,3},{4,68},{68... | collective-permute-start | bytes 3145736 | tf_op jit(solution)/shard_map/ppermute | solution.py:477
  63.5 11.4 %collective-permute-start.13 = (bf16[8,64,256]{2,1,0:T(8,128)(2,1)S(1)}, bf16[8,64,256]{2,1,0:T(8,128)(2,1)S(1)}, u32[]{:S(2)}, u32[]{:S(2)}) collective-permute-start(bf16[8,64,256]{2,1,0:T(8,128)(2,1)S(1)} %get-tuple-element.51), channel_id=1, source_target_pairs={{0,1},{1,0},{2,3},{3,2},{4,5},{5,4},{6,7},{7,6},{8,9},{9,8},{10,11... | collective-permute-start | bytes 786440 | tf_op jit(solution)/shard_map/ppermute | solution.py:482
  64.4 10.5 %collective-permute-start.14 = (bf16[8,64,256]{2,1,0:T(8,128)(2,1)S(1)}, bf16[8,64,256]{2,1,0:T(8,128)(2,1)S(1)}, u32[]{:S(2)}, u32[]{:S(2)}) collective-permute-start(bf16[8,64,256]{2,1,0:T(8,128)(2,1)S(1)} %get-tuple-element.53), channel_id=1, source_target_pairs={{0,2},{2,4},{4,6},{6,0},{1,3},{3,5},{5,7},{7,1},{8,10},{10,12},{12... | collective-permute-start | bytes 786440 | tf_op jit(solution)/shard_map/ppermute | solution.py:482
  65.3 14.5 %collective-permute-start.15 = (bf16[8,64,256]{2,1,0:T(8,128)(2,1)S(1)}, bf16[8,64,256]{2,1,0:T(8,128)(2,1)S(1)}, u32[]{:S(2)}, u32[]{:S(2)}) collective-permute-start(bf16[8,64,256]{2,1,0:T(8,128)(2,1)S(1)} %get-tuple-element.54), channel_id=1, source_target_pairs={{0,4},{2,6},{4,0},{6,2},{1,5},{3,7},{5,1},{7,3},{8,12},{10,14},{12... | collective-permute-start | bytes 786440 | tf_op jit(solution)/shard_map/ppermute | solution.py:482
  68.0 12.2 %collective-permute-start.16 = (bf16[8,64,256]{2,1,0:T(8,128)(2,1)S(1)}, bf16[8,64,256]{2,1,0:T(8,128)(2,1)S(1)}, u32[]{:S(2)}, u32[]{:S(2)}) collective-permute-start(bf16[8,64,256]{2,1,0:T(8,128)(2,1)S(1)} %get-tuple-element.55), channel_id=1, source_target_pairs={{0,6},{2,0},{4,2},{6,4},{1,7},{3,1},{5,3},{7,5},{8,14},{10,8},{12,... | collective-permute-start | bytes 786440 | tf_op jit(solution)/shard_map/ppermute | solution.py:482
  71.1 27.4 %collective-permute-start.7 = (bf16[256,2048]{1,0:T(8,128)(2,1)}, bf16[256,2048]{1,0:T(8,128)(2,1)}, u32[]{:S(2)}, u32[]{:S(2)}) collective-permute-start(bf16[256,2048]{1,0:T(8,128)(2,1)} %fusion.1), channel_id=1, source_target_pairs={{128,129},{129,128},{130,131},{131,130},{132,133},{133,132},{134,1... | collective-permute-start | bytes 3145736 | tf_op jit(solution)/shard_map/ppermute | solution.py:516
  81.2 25.2 %all-to-all-start = ((bf16[8,64,512]{2,1,0:T(8,128)(2,1)}), bf16[8,64,512]{2,1,0:T(8,128)(2,1)S(1)}, u32[]{:S(2)}, u32[]{:S(2)}) async-start(bf16[8,64,512]{2,1,0:T(8,128)(2,1)} %shard_map.100), calls=%async_computation.1 | async-start | bytes 1048576 | tf_op jit(solution)/shard_map/all_to_all | solution.py:486
  89.6 94.8 %all-gather.2.cloned.1.call-start = ((), (), s32[]{:S(2)}) async-start(), calls=%async_computation.4 | async-start | bytes 4718592 | tf_op jit(solution)/shard_map/all_gather | solution.py:529
  93.3 7.9 %collective-permute-start.10 = (bf16[2,64,512]{2,1,0:T(8,128)(2,1)S(1)}, bf16[2,64,512]{2,1,0:T(8,128)(2,1)S(1)}, u32[]{:S(2)}, u32[]{:S(2)}) collective-permute-start(bf16[2,64,512]{2,1,0:T(8,128)(2,1)S(1)} %bitcast.38), channel_id=1, source_target_pairs={{0,4},{2,6},{4,0},{6,2},{1,5},{3,7},{5,1},{7,3},{8,12},{10,14},{12... | collective-permute-start | bytes 393224 | tf_op jit(solution)/shard_map/ppermute | solution.py:482
  96.4 6.6 %collective-permute-start.11 = (bf16[2,64,512]{2,1,0:T(8,128)(2,1)S(1)}, bf16[2,64,512]{2,1,0:T(8,128)(2,1)S(1)}, u32[]{:S(2)}, u32[]{:S(2)}) collective-permute-start(bf16[2,64,512]{2,1,0:T(8,128)(2,1)S(1)} %bitcast.37), channel_id=1, source_target_pairs={{0,6},{2,0},{4,2},{6,4},{1,7},{3,1},{5,3},{7,5},{8,14},{10,8},{12,... | collective-permute-start | bytes 393224 | tf_op jit(solution)/shard_map/ppermute | solution.py:482
  97.6 6.2 %collective-permute-start.9 = (bf16[2,64,512]{2,1,0:T(8,128)(2,1)S(1)}, bf16[2,64,512]{2,1,0:T(8,128)(2,1)S(1)}, u32[]{:S(2)}, u32[]{:S(2)}) collective-permute-start(bf16[2,64,512]{2,1,0:T(8,128)(2,1)S(1)} %bitcast.36), channel_id=1, source_target_pairs={{0,2},{2,4},{4,6},{6,0},{1,3},{3,5},{5,7},{7,1},{8,10},{10,12},{12... | collective-permute-start | bytes 393224 | tf_op jit(solution)/shard_map/ppermute | solution.py:482
  103.8 4.4 %collective-permute-start.12 = (bf16[64,512]{1,0:T(8,128)(2,1)S(1)}, bf16[64,512]{1,0:T(8,128)(2,1)S(1)}, u32[]{:S(2)}, u32[]{:S(2)}) collective-permute-start(bf16[64,512]{1,0:T(8,128)(2,1)S(1)} %get-tuple-element.49), channel_id=1, source_target_pairs={{0,1},{1,0},{2,3},{3,2},{4,5},{5,4},{6,7},{7,6},{8,9},{9,8},{10,11... | collective-permute-start | bytes 196616 | tf_op jit(solution)/shard_map/ppermute | solution.py:482
  110.6 4.3 %collective-permute-start.26 = (bf16[64,512]{1,0:T(8,128)(2,1)S(1)}, bf16[64,512]{1,0:T(8,128)(2,1)S(1)}, u32[]{:S(2)}, u32[]{:S(2)}) collective-permute-start(bf16[64,512]{1,0:T(8,128)(2,1)S(1)} %get-tuple-element.59), channel_id=1, source_target_pairs={{0,1},{1,0},{2,3},{3,2},{4,5},{5,4},{6,7},{7,6},{8,9},{9,8},{10,11... | collective-permute-start | bytes 196616 | tf_op jit(solution)/shard_map/ppermute | solution.py:482
  114.9 6.9 %collective-permute-start.27 = (bf16[128,512]{1,0:T(8,128)(2,1)S(1)}, bf16[128,512]{1,0:T(8,128)(2,1)S(1)}, u32[]{:S(2)}, u32[]{:S(2)}) collective-permute-start(bf16[128,512]{1,0:T(8,128)(2,1)S(1)} %get-tuple-element.68), channel_id=1, source_target_pairs={{0,6},{2,0},{4,2},{6,4},{1,7},{3,1},{5,3},{7,5},{8,14},{10,8},{12,... | collective-permute-start | bytes 393224 | tf_op jit(solution)/shard_map/ppermute | solution.py:482
  117.0 7.1 %collective-permute-start.28 = (bf16[128,512]{1,0:T(8,128)(2,1)S(1)}, bf16[128,512]{1,0:T(8,128)(2,1)S(1)}, u32[]{:S(2)}, u32[]{:S(2)}) collective-permute-start(bf16[128,512]{1,0:T(8,128)(2,1)S(1)} %get-tuple-element.68), channel_id=1, source_target_pairs={{0,4},{2,6},{4,0},{6,2},{1,5},{3,7},{5,1},{7,3},{8,12},{10,14},{12... | collective-permute-start | bytes 393224 | tf_op jit(solution)/shard_map/ppermute | solution.py:482
  117.8 7.6 %collective-permute-start.29 = (bf16[128,512]{1,0:T(8,128)(2,1)S(1)}, bf16[128,512]{1,0:T(8,128)(2,1)S(1)}, u32[]{:S(2)}, u32[]{:S(2)}) collective-permute-start(bf16[128,512]{1,0:T(8,128)(2,1)S(1)} %get-tuple-element.68), channel_id=1, source_target_pairs={{0,2},{2,4},{4,6},{6,0},{1,3},{3,5},{5,7},{7,1},{8,10},{10,12},{12... | collective-permute-start | bytes 393224 | tf_op jit(solution)/shard_map/ppermute | solution.py:482
  126.3 25.4 %all-to-all-start.1 = ((bf16[8,64,512]{2,1,0:T(8,128)(2,1)}), bf16[8,64,512]{2,1,0:T(8,128)(2,1)S(1)}, u32[]{:S(2)}, u32[]{:S(2)}) async-start(bf16[8,64,512]{2,1,0:T(8,128)(2,1)} %get-tuple-element.58), calls=%async_computation.2 | async-start | bytes 1048576 | tf_op jit(solution)/shard_map/all_to_all | solution.py:486
  130.6 39.4 %collective-permute-start.8 = (bf16[256,2048]{1,0:T(8,128)(2,1)}, bf16[256,2048]{1,0:T(8,128)(2,1)}, u32[]{:S(2)}, u32[]{:S(2)}) collective-permute-start(bf16[256,2048]{1,0:T(8,128)(2,1)} %collective-permute-done.7), channel_id=1, source_target_pairs={{128,1},{129,0},{130,3},{131,2},{132,5},{133,4},{134,7},{135,6},{1... | collective-permute-start | bytes 3145736 | tf_op jit(solution)/shard_map/ppermute | solution.py:517
  151.8 6.5 %collective-permute-start.18 = (bf16[8,64,256]{2,1,0:T(8,128)(2,1)S(1)}, bf16[8,64,256]{2,1,0:T(8,128)(2,1)S(1)}, u32[]{:S(2)}, u32[]{:S(2)}) collective-permute-start(bf16[8,64,256]{2,1,0:T(8,128)(2,1)S(1)} %get-tuple-element.63), channel_id=1, source_target_pairs={{0,1},{1,0},{2,3},{3,2},{4,5},{5,4},{6,7},{7,6},{8,9},{9,8},{10,11... | collective-permute-start | bytes 786440 | tf_op jit(solution)/shard_map/ppermute | solution.py:482
  153.1 10.8 %collective-permute-start.24 = (bf16[8,64,256]{2,1,0:T(8,128)(2,1)S(1)}, bf16[8,64,256]{2,1,0:T(8,128)(2,1)S(1)}, u32[]{:S(2)}, u32[]{:S(2)}) collective-permute-start(bf16[8,64,256]{2,1,0:T(8,128)(2,1)S(1)} %get-tuple-element.62), channel_id=1, source_target_pairs={{0,2},{2,4},{4,6},{6,0},{1,3},{3,5},{5,7},{7,1},{8,10},{10,12},{12... | collective-permute-start | bytes 786440 | tf_op jit(solution)/shard_map/ppermute | solution.py:482
  153.2 10.8 %collective-permute-start.23 = (bf16[8,64,256]{2,1,0:T(8,128)(2,1)S(1)}, bf16[8,64,256]{2,1,0:T(8,128)(2,1)S(1)}, u32[]{:S(2)}, u32[]{:S(2)}) collective-permute-start(bf16[8,64,256]{2,1,0:T(8,128)(2,1)S(1)} %get-tuple-element.62), channel_id=1, source_target_pairs={{0,4},{2,6},{4,0},{6,2},{1,5},{3,7},{5,1},{7,3},{8,12},{10,14},{12... | collective-permute-start | bytes 786440 | tf_op jit(solution)/shard_map/ppermute | solution.py:482
  153.4 11.2 %collective-permute-start.22 = (bf16[8,64,256]{2,1,0:T(8,128)(2,1)S(1)}, bf16[8,64,256]{2,1,0:T(8,128)(2,1)S(1)}, u32[]{:S(2)}, u32[]{:S(2)}) collective-permute-start(bf16[8,64,256]{2,1,0:T(8,128)(2,1)S(1)} %get-tuple-element.62), channel_id=1, source_target_pairs={{0,6},{2,0},{4,2},{6,4},{1,7},{3,1},{5,3},{7,5},{8,14},{10,8},{12,... | collective-permute-start | bytes 786440 | tf_op jit(solution)/shard_map/ppermute | solution.py:482
  165.7 23.4 %collective-permute-start.25 = (bf16[4,8,64,256]{3,2,1,0:T(8,128)(2,1)}, bf16[4,8,64,256]{3,2,1,0:T(8,128)(2,1)}, u32[]{:S(2)}, u32[]{:S(2)}) collective-permute-start(bf16[4,8,64,256]{3,2,1,0:T(8,128)(2,1)} %shard_map.104.refs_1_), channel_id=1, source_target_pairs={{0,1},{1,0},{2,3},{3,2},{4,5},{5,4},{6,7},{7,6},{8,9},{9,8},{10,11... | collective-permute-start | bytes 3145736 | tf_op jit(solution)/shard_map/ppermute | solution.py:482
  166.2 22.8 %collective-permute-start.21 = (bf16[2,8,64,256]{3,2,1,0:T(8,128)(2,1)}, bf16[2,8,64,256]{3,2,1,0:T(8,128)(2,1)}, u32[]{:S(2)}, u32[]{:S(2)}) collective-permute-start(bf16[2,8,64,256]{3,2,1,0:T(8,128)(2,1)} %shard_map.103.refs_0_), channel_id=1, source_target_pairs={{0,2},{2,4},{4,6},{6,0},{1,3},{3,5},{5,7},{7,1},{8,10},{10,12},{12... | collective-permute-start | bytes 1572872 | tf_op jit(solution)/shard_map/ppermute | solution.py:482
  166.4 22.7 %collective-permute-start.20 = (bf16[2,8,64,256]{3,2,1,0:T(8,128)(2,1)}, bf16[2,8,64,256]{3,2,1,0:T(8,128)(2,1)}, u32[]{:S(2)}, u32[]{:S(2)}) collective-permute-start(bf16[2,8,64,256]{3,2,1,0:T(8,128)(2,1)} %shard_map.103.refs_0_), channel_id=1, source_target_pairs={{0,4},{2,6},{4,0},{6,2},{1,5},{3,7},{5,1},{7,3},{8,12},{10,14},{12... | collective-permute-start | bytes 1572872 | tf_op jit(solution)/shard_map/ppermute | solution.py:482
  170.0 19.0 %collective-permute-start.19 = (bf16[2,8,64,256]{3,2,1,0:T(8,128)(2,1)}, bf16[2,8,64,256]{3,2,1,0:T(8,128)(2,1)}, u32[]{:S(2)}, u32[]{:S(2)}) collective-permute-start(bf16[2,8,64,256]{3,2,1,0:T(8,128)(2,1)} %shard_map.103.refs_0_), channel_id=1, source_target_pairs={{0,6},{2,0},{4,2},{6,4},{1,7},{3,1},{5,3},{7,5},{8,14},{10,8},{12,... | collective-permute-start | bytes 1572872 | tf_op jit(solution)/shard_map/ppermute | solution.py:482
  (19 other events, 133.2 us)
Sparse Core Ops, SparseCore 0:
  33.9 58.2 reduce-scatter.1
  126.4 57.9 all-gather.1

commit v3 on v2

--- a/solution.py
+++ b/solution.py
@@ -464,13 +464,19 @@
         )(where, *operands, *more)
 
     first = functools.partial(assemble_b_kernel, [0], [0], cut)
-    rest = functools.partial(assemble_b_kernel, list(range(1, Y)), list(range(1, X)), cut)
+    early = functools.partial(assemble_b_kernel, [Y - 1], [], cut)
+    rest = functools.partial(assemble_b_kernel, list(range(1, Y - 1)), list(range(1, X)), cut)
     own = Z * (X + Y)
     out = call(first, own, [y_parts[0], x_parts[0]], VMEM, [])
+    out = call(early, Z * X, [y_parts[-1]], VMEM, [out])
     scratch = [pltpu.VMEM((width, cut), BF16), pltpu.SemaphoreType.DMA((Z,))]
     a = pltpu.with_memory_space_constraint(a, pltpu.HBM)
     out = call(assemble_a_kernel, Z * Y * X, [a], ANY, [out], scratch)
-    return call(rest, 2 * Z * Y * X - own, [*y_parts[1:], *x_parts[1:]], VMEM, [out, *after])
+    return call(rest, 2 * Z * Y * X - own - Z * X, [*y_parts[1:-1], *x_parts[1:]], VMEM, [out, *after])
+
+
+def in_vmem(value):
+    return pltpu.with_memory_space_constraint(value, pltpu.VMEM)
 
 
 def over_tensor(value):
@@ -495,11 +501,11 @@
 
     half = width // 2 // (Y * X * SPAN)
     local_own, sums, used_grad = local_momentum(own, head_grad[0], momentum, tensor * half, lengths)
-    local_other, sums = local_momentum(other, used_grad, momentum, (1 - tensor) * half, sums=sums)
+    local_other, sums = local_momentum(in_vmem(other), used_grad, momentum, (1 - tensor) * half, sums=sums)
     sums = [sums, over_tensor(sums)]
 
     where = jnp.stack([tensor * half, my_y, my_x])
-    by_z, *rest = compress(local_own, local_other, sums, where)
+    by_z, *rest = compress(local_own, local_other, [in_vmem(part) for part in sums], where)
     part_z = lax.psum_scatter(by_z, "z", scatter_dimension=0, tiled=True)
     by_y, by_x = rest[:Y], rest[Y:]
     from_y = [by_y[0]] + [along(by_y[k], "y", k) for k in range(1, Y)]

time: 203 us -> 207 us (1.020)
  the two profiles are of different devices: /device:TPU:4 before, /device:TPU:2 now
where the time goes in v3:
time: 207 us; the launch traced here: 206 us
  waiting for transfers between devices  78.9 us (38%)
  Pallas kernels  53.6 us (26%)
  starting transfers between devices  47.8 us (23%)
  between operations  14.4 us (7%)
  local copies, waits for them, and re-layouts  8.26 us (4%)
  other arithmetic  3.45 us (2%)
    ppermute x24, waiting for transfers between devices, along(): lax.ppermute(value, axis, [(i, (i + steps) % count) for i in range(count)])  52.2 us
    ppermute x24, starting transfers between devices, along(): lax.ppermute(value, axis, [(i, (i + steps) % count) for i in range(count)])  31.3 us
    all_to_all x2, waiting for transfers between devices, exchanged(): return lax.all_to_all(value, axes, split_axis=0, concat_axis=0, tiled=True)  22 us
    pallas_call x4, Pallas kernels, call(): pl.pallas_call(kernel, grid_spec=pltpu.PrefetchScalarGridSpec(num_scalar_...  13.5 us
    pallas_call x2, Pallas kernels, local_momentum(): pl.pallas_call(kernel, grid_spec=pltpu.PrefetchScalarGridSpec(num_scalar_...  13.3 us
    all_to_all x2, starting transfers between devices, exchanged(): return lax.all_to_all(value, axes, split_axis=0, concat_axis=0, tiled=True)  12.7 us
    pallas_call x1, Pallas kernels, compress(): pl.pallas_call(compress_kernel, grid_spec=pltpu.PrefetchScalarGridSpec(nu...  9.57 us
    pallas_call x1, Pallas kernels, compression_error(): pl.pallas_call(error_kernel, grid_spec=pltpu.PrefetchScalarGridSpec(num_s...  8.19 us
  transfers between devices with their start and end apart: 34, of which 21 were waited for; matrix products, arithmetic and copies ran while one was open for 3% of the time, Pallas kernels for 16%

profile of v3, /device:TPU:2, one launch (start us, length us, event | category | flops | bytes accessed | tf_op | source)
XLA Modules:
  0.0 206.3 jit_solution(3527589925400407192)
XLA Ops:
  7.3 7.1 %shard_map.93 = (bf16[2048,1024]{1,0:T(8,128)(2,1)}, f32[64,128]{1,0:T(8,128)}, bf16[256,1024]{1,0:T(8,128)(2,1)}) custom-call(s32[1]{0:T(128)} %bitcast.2.where_ref, s32[4]{0:T(128)} %lengths_ref.1, bf16[256,2048]{1,0:T(8,128)(2,1)} %bitcast.34, bf16[256,1024]{1,0:T(8,128)(2,1)} %bitcast.35, bf16[4096,1024]{1,0:T(8,128)(2,1)} %bitcast.30), custom_call_target="tpu_custom_call" | custom-call | flops 1073741824 | bytes 8388608 | tf_op jit(solution)/shard_map/pallas_call | solution.py:79
  14.4 6.2 %shard_map.95 = (bf16[2048,1024]{1,0:T(8,128)(2,1)}, f32[64,128]{1,0:T(8,128)}) custom-call(s32[1]{0:T(128)} %bitcast.9.where_ref, bf16[256,2048]{1,0:T(8,128)(2,1)S(1)} %collective-permute-done.x_ref, bf16[256,1024]{1,0:T(8,128)(2,1)} %get-tuple-element.33.g_ref, bf16[4096,1024]{1,0:T(8,128)(2,1)} %bitcast.31, f32[64,128]{1,0:T(8,128)} %get-tuple-element.36.all_sums_ref), custom_call_target="tpu_custom_call" | custom-call | flops 1073741824 | bytes 8388608 | tf_op jit(solution)/shard_map/pallas_call | solution.py:79
  23.0 9.6 %shard_map.96 = (bf16[4096,512]{1,0:T(8,128)(2,1)}, bf16[2,8,64,256]{3,2,1,0:T(8,128)(2,1)}, bf16[2,8,64,256]{3,2,1,0:T(8,128)(2,1)}, bf16[2,8,64,256]{3,2,1,0:T...) custom-call(s32[3]{0:T(128)S(1)} %pad_add_fusion.where_ref, ...), custom_call_target="tpu_custom_call" | custom-call | flops 33554432 | bytes 16777216 | tf_op jit(solution)/shard_map/pallas_call | solution.py:174
  32.6 2.4 %collective-permute-start.5 = (bf16[4,8,64,256]{3,2,1,0:T(8,128)(2,1)}, bf16[4,8,64,256]{3,2,1,0:T(8,128)(2,1)S(1)}, u32[]{:S(2)}, u32[]{:S(2)}) collective-permute-start(bf16[4,8,64,256]{3,2,1,0:T(8,128)(2,1)} %get-tuple-element.44), channel_id=1, source_target_pairs={{0,1},{1,0},{2,3},{3,2},{4,5},{5,4},{6,7},{7,6},{8,9},{9,8},{10,11... | collective-permute-start | bytes 3145736 | tf_op jit(solution)/shard_map/ppermute | solution.py:488
  34.9 2.7 %collective-permute-start.3 = (bf16[2,8,64,256]{3,2,1,0:T(8,128)(2,1)}, bf16[2,8,64,256]{3,2,1,0:T(8,128)(2,1)S(1)}, u32[]{:S(2)}, u32[]{:S(2)}) collective-permute-start(bf16[2,8,64,256]{3,2,1,0:T(8,128)(2,1)} %get-tuple-element.41), channel_id=1, source_target_pairs={{0,4},{2,6},{4,0},{6,2},{1,5},{3,7},{5,1},{7,3},{8,12},{10,14},{12... | collective-permute-start | bytes 1572872 | tf_op jit(solution)/shard_map/ppermute | solution.py:488
  39.0 3.4 %copy-done.3 = bf16[1,4096,1024]{2,1,0:T(8,128)(2,1)S(1)} copy-done((bf16[1,4096,1024]{2,1,0:T(8,128)(2,1)S(1)}, bf16[1,4096,1024]{2,1,0:T(8,128)(2,1)}, u32[]{:S(2)}) %copy-start.3) | copy-done | bytes 8388632
  42.4 4.4 %shard_map.94 = (f32[256,2048]{1,0:T(8,128)S(1)}, bf16[256,2048]{1,0:T(8,128)(2,1)S(1)}) custom-call(s32[1]{0:T(128)} %bitcast.1.where_ref, bf16[256,1024]{1,0:T(8,128)(2,1)S(1)} %copy-done.5, bf16[4096,1024]{1,0:T(8,128)(2,1)S(1)} %bitcast.26), custom_call_target="tpu_custom_call" | custom-call | flops 2147483648 | bytes 12582912 | tf_op jit(solution)/shard_map/pallas_call | solution.py:377
  46.9 8.2 %shard_map.97.refs_7_ = bf16[4096,1024]{1,0:T(8,128)(2,1)} custom-call(s32[3]{0:T(128)S(1)} %pad_add_fusion.where_ref, bf16[2048,1024]{1,0:T(8,128)(2,1)S(1)} %copy-done.1, bf16[2048,1024]{1,0:T(8,128)(2,1)S(1)} %copy-done.2, f32[64,128]{1,0:T(8,128)S(1)} %copy-done.9, f32[64,128]{1,0:T(8,128)S(1)} %collective-permute-done.1.t_ref), custom_call_target="tpu_custom_call" | custom-call | flops 4096 | bytes 4096 | tf_op jit(solution)/shard_map/pallas_call | solution.py:198
  55.1 6.4 %collective-permute-done.2.refs_1_ = bf16[2,8,64,256]{3,2,1,0:T(8,128)(2,1)S(1)} collective-permute-done((bf16[2,8,64,256]{3,2,1,0:T(8,128)(2,1)}, bf16[2,8,64,256]{3,2,1,0:T(8,128)(2,1)S(1)}, u32[]{:S(2)}, u32[]{:S(2)}) %collective-permute-start.2) | collective-permute-done | bytes 524320 | tf_op jit(solution)/shard_map/ppermute | solution.py:488
  64.7 2.6 %collective-permute-start.15 = (bf16[8,64,256]{2,1,0:T(8,128)(2,1)S(1)}, bf16[8,64,256]{2,1,0:T(8,128)(2,1)S(1)}, u32[]{:S(2)}, u32[]{:S(2)}) collective-permute-start(bf16[8,64,256]{2,1,0:T(8,128)(2,1)S(1)} %get-tuple-element.54), channel_id=1, source_target_pairs={{0,4},{2,6},{4,0},{6,2},{1,5},{3,7},{5,1},{7,3},{8,12},{10,14},{12... | collective-permute-start | bytes 786440 | tf_op jit(solution)/shard_map/ppermute | solution.py:488
  72.8 6.4 %collective-permute-done.15.refs_2_ = bf16[8,64,256]{2,1,0:T(8,128)(2,1)S(1)} collective-permute-done((bf16[8,64,256]{2,1,0:T(8,128)(2,1)S(1)}, bf16[8,64,256]{2,1,0:T(8,128)(2,1)S(1)}, u32[]{:S(2)}, u32[]{:S(2)}) %collective-permute-start.15) | collective-permute-done | bytes 262176 | tf_op jit(solution)/shard_map/ppermute | solution.py:488
  80.2 8.3 %all-to-all-start = ((bf16[8,64,512]{2,1,0:T(8,128)(2,1)}), bf16[8,64,512]{2,1,0:T(8,128)(2,1)S(1)}, u32[]{:S(2)}, u32[]{:S(2)}) async-start(bf16[8,64,512]{2,1,0:T(8,128)(2,1)} %shard_map.100), calls=%async_computation.1 | async-start | bytes 1048576 | tf_op jit(solution)/shard_map/all_to_all | solution.py:492
  88.5 2.5 %reduce-scatter.2.cloned.1.call-done = bf16[512,512]{1,0:T(8,128)(2,1)} async-done(((bf16[4096,512]{1,0:T(8,128)(2,1)}), bf16[512,512]{1,0:T(8,128)(2,1)}) %reduce-scatter.2.cloned.1.call-update) | async-done | bytes 524304 | tf_op jit(solution)/shard_map/reduce_scatter | solution.py:509
  92.1 3.1 %collective-permute-start.10 = (bf16[2,64,512]{2,1,0:T(8,128)(2,1)S(1)}, bf16[2,64,512]{2,1,0:T(8,128)(2,1)S(1)}, u32[]{:S(2)}, u32[]{:S(2)}) collective-permute-start(bf16[2,64,512]{2,1,0:T(8,128)(2,1)S(1)} %bitcast.38), channel_id=1, source_target_pairs={{0,4},{2,6},{4,0},{6,2},{1,5},{3,7},{5,1},{7,3},{8,12},{10,14},{12... | collective-permute-start | bytes 393224 | tf_op jit(solution)/shard_map/ppermute | solution.py:488
  97.9 2.1 %collective-permute-done.10.refs_1_ = bf16[2,64,512]{2,1,0:T(8,128)(2,1)S(1)} collective-permute-done((bf16[2,64,512]{2,1,0:T(8,128)(2,1)S(1)}, bf16[2,64,512]{2,1,0:T(8,128)(2,1)S(1)}, u32[]{:S(2)}, u32[]{:S(2)}) %collective-permute-start.10) | collective-permute-done | bytes 131104 | tf_op jit(solution)/shard_map/ppermute | solution.py:488
  100.0 1.9 collective-permute-done.11.refs_2_
  103.3 1.9 all-to-all-done.b_ref
  110.0 3.7 %collective-permute-done.25 = bf16[64,512]{1,0:T(8,128)(2,1)S(1)} collective-permute-done((bf16[64,512]{1,0:T(8,128)(2,1)S(1)}, bf16[64,512]{1,0:T(8,128)(2,1)S(1)}, u32[]{:S(2)}, u32[]{:S(2)}) %collective-permute-start.25) | collective-permute-done | bytes 65568 | tf_op jit(solution)/shard_map/ppermute | solution.py:488
  113.7 2.1 %collective-permute-start.26 = (bf16[128,512]{1,0:T(8,128)(2,1)S(1)}, bf16[128,512]{1,0:T(8,128)(2,1)S(1)}, u32[]{:S(2)}, u32[]{:S(2)}) collective-permute-start(bf16[128,512]{1,0:T(8,128)(2,1)S(1)} %get-tuple-element.68), channel_id=1, source_target_pairs={{0,6},{2,0},{4,2},{6,4},{1,7},{3,1},{5,3},{7,5},{8,14},{10,8},{12,... | collective-permute-start | bytes 393224 | tf_op jit(solution)/shard_map/ppermute | solution.py:488
  117.5 3.1 %collective-permute-done.26 = bf16[128,512]{1,0:T(8,128)(2,1)S(1)} collective-permute-done((bf16[128,512]{1,0:T(8,128)(2,1)S(1)}, bf16[128,512]{1,0:T(8,128)(2,1)S(1)}, u32[]{:S(2)}, u32[]{:S(2)}) %collective-permute-start.26) | collective-permute-done | bytes 131104 | tf_op jit(solution)/shard_map/ppermute | solution.py:488
  120.6 2.3 %collective-permute-done.27 = bf16[128,512]{1,0:T(8,128)(2,1)S(1)} collective-permute-done((bf16[128,512]{1,0:T(8,128)(2,1)S(1)}, bf16[128,512]{1,0:T(8,128)(2,1)S(1)}, u32[]{:S(2)}, u32[]{:S(2)}) %collective-permute-start.27) | collective-permute-done | bytes 131104 | tf_op jit(solution)/shard_map/ppermute | solution.py:488
  125.1 4.5 %all-to-all-start.1 = ((bf16[8,64,512]{2,1,0:T(8,128)(2,1)}), bf16[8,64,512]{2,1,0:T(8,128)(2,1)S(1)}, u32[]{:S(2)}, u32[]{:S(2)}) async-start(bf16[8,64,512]{2,1,0:T(8,128)(2,1)} %get-tuple-element.58), calls=%async_computation.2 | async-start | bytes 1048576 | tf_op jit(solution)/shard_map/all_to_all | solution.py:492
  130.8 20.0 %all-to-all-done.1.all_ref = bf16[8,64,512]{2,1,0:T(8,128)(2,1)S(1)} async-done(((bf16[8,64,512]{2,1,0:T(8,128)(2,1)}), bf16[8,64,512]{2,1,0:T(8,128)(2,1)S(1)}, u32[]{:S(2)}, u32[]{:S(2)}) %all-to-all-start.1) | async-done | bytes 524320 | tf_op jit(solution)/shard_map/all_to_all | solution.py:492
  151.7 2.9 %collective-permute-start.21 = (bf16[8,64,256]{2,1,0:T(8,128)(2,1)S(1)}, bf16[8,64,256]{2,1,0:T(8,128)(2,1)S(1)}, u32[]{:S(2)}, u32[]{:S(2)}) collective-permute-start(bf16[8,64,256]{2,1,0:T(8,128)(2,1)S(1)} %get-tuple-element.62), channel_id=1, source_target_pairs={{0,6},{2,0},{4,2},{6,4},{1,7},{3,1},{5,3},{7,5},{8,14},{10,8},{12,... | collective-permute-start | bytes 786440 | tf_op jit(solution)/shard_map/ppermute | solution.py:488
  154.6 2.8 %collective-permute-done.18.swapped_ref = bf16[8,64,256]{2,1,0:T(8,128)(2,1)S(1)} collective-permute-done((bf16[8,64,256]{2,1,0:T(8,128)(2,1)S(1)}, bf16[8,64,256]{2,1,0:T(8,128)(2,1)S(1)}, u32[]{:S(2)}, u32[]{:S(2)}) %collective-permute-start.18) | collective-permute-done | bytes 262176 | tf_op jit(solution)/shard_map/ppermute | solution.py:488
  158.9 3.6 %collective-permute-done.23.refs_2_ = bf16[8,64,256]{2,1,0:T(8,128)(2,1)S(1)} collective-permute-done((bf16[8,64,256]{2,1,0:T(8,128)(2,1)S(1)}, bf16[8,64,256]{2,1,0:T(8,128)(2,1)S(1)}, u32[]{:S(2)}, u32[]{:S(2)}) %collective-permute-start.23) | collective-permute-done | bytes 262176 | tf_op jit(solution)/shard_map/ppermute | solution.py:488
  166.0 3.6 %collective-permute-start.20 = (bf16[2,8,64,256]{3,2,1,0:T(8,128)(2,1)}, bf16[2,8,64,256]{3,2,1,0:T(8,128)(2,1)}, u32[]{:S(2)}, u32[]{:S(2)}) collective-permute-start(bf16[2,8,64,256]{3,2,1,0:T(8,128)(2,1)} %shard_map.103.refs_0_), channel_id=1, source_target_pairs={{0,4},{2,6},{4,0},{6,2},{1,5},{3,7},{5,1},{7,3},{8,12},{10,14},{12... | collective-permute-start | bytes 1572872 | tf_op jit(solution)/shard_map/ppermute | solution.py:488
  169.6 1.9 add_convert_fusion.refs_4_
  171.5 3.5 %shard_map.105.refs_1_ = bf16[4096,1024]{1,0:T(8,128)(2,1)} custom-call(s32[3]{0:T(128)S(1)} %pad_add_fusion.where_ref, bf16[2,8,64,256]{3,2,1,0:T(8,128)(2,1)} %shard_map.103.refs_0_, bf16[4,8,64,256]{3,2,1,0:T(8,128)(2,1)} %shard_map.104.refs_1_), custom_call_target="tpu_custom_call" | custom-call | bytes 8388608 | tf_op jit(solution)/shard_map/pallas_call | solution.py:451
  175.0 14.3 %collective-permute-done.29.refs_0_ = bf16[2,8,64,256]{3,2,1,0:T(8,128)(2,1)S(1)} collective-permute-done((bf16[2,8,64,256]{3,2,1,0:T(8,128)(2,1)}, bf16[2,8,64,256]{3,2,1,0:T(8,128)(2,1)S(1)}, u32[]{:S(2)}, u32[]{:S(2)}) %collective-permute-start.29) | collective-permute-done | bytes 524320 | tf_op jit(solution)/shard_map/ppermute | solution.py:488
  190.9 4.6 %shard_map.107.refs_3_ = bf16[4096,1024]{1,0:T(8,128)(2,1)} custom-call(s32[3]{0:T(128)S(1)} %pad_add_fusion.where_ref, bf16[4096,512]{1,0:T(8,128)(2,1)} %all-gather.2.cloned.1.call-done.a_ref, bf16[4096,1024]{1,0:T(8,128)(2,1)} %shard_map.106._), custom_call_target="tpu_custom_call", output_to_operand_aliasing={{}: (2, {})} | custom-call | bytes 8388608 | tf_op jit(solution)/shard_map/pallas_call | solution.py:451
  195.5 3.9 %shard_map.108 = bf16[4096,1024]{1,0:T(8,128)(2,1)} custom-call(s32[3]{0:T(128)S(1)} %pad_add_fusion.where_ref, bf16[2,8,64,256]{3,2,1,0:T(8,128)(2,1)} %collective-permute-done.19.refs_0_, bf16[2,8,64,256]{3,2,1,0:T(8,128)(2,1)} %collective-permute-done.20.refs_1_, ...), custom_call_target="tpu_custom_call", output_to_operand_aliasing={{}: (4, {})} | custom-call | bytes 8388608 | tf_op jit(solution)/shard_map/pallas_call | solution.py:451
  (99 shorter events, 36.0 us)
Async XLA Ops:
  7.2 83.8 %reduce-scatter.2.cloned.1.call-start = ((), (), s32[]{:S(2)}) async-start(), calls=%async_computation.3 | async-start | bytes 4718592 | tf_op jit(solution)/shard_map/reduce_scatter | solution.py:509
  7.2 7.2 %collective-permute-start = (bf16[256,2048]{1,0:T(8,128)(2,1)}, bf16[256,2048]{1,0:T(8,128)(2,1)S(1)}, u32[]{:S(2)}, u32[]{:S(2)}) collective-permute-start(bf16[256,2048]{1,0:T(8,128)(2,1)} %bitcast.33), channel_id=1, source_target_pairs={{0,64},{64,0},{1,65},{65,1},{2,66},{66,2},{3,67},{67,3},{4,68},{68... | collective-permute-start | bytes 3145736 | tf_op jit(solution)/shard_map/ppermute | solution.py:483
  32.6 29.5 %collective-permute-start.5 = (bf16[4,8,64,256]{3,2,1,0:T(8,128)(2,1)}, bf16[4,8,64,256]{3,2,1,0:T(8,128)(2,1)S(1)}, u32[]{:S(2)}, u32[]{:S(2)}) collective-permute-start(bf16[4,8,64,256]{3,2,1,0:T(8,128)(2,1)} %get-tuple-element.44), channel_id=1, source_target_pairs={{0,1},{1,0},{2,3},{3,2},{4,5},{5,4},{6,7},{7,6},{8,9},{9,8},{10,11... | collective-permute-start | bytes 3145736 | tf_op jit(solution)/shard_map/ppermute | solution.py:488
  34.9 26.5 %collective-permute-start.2 = (bf16[2,8,64,256]{3,2,1,0:T(8,128)(2,1)}, bf16[2,8,64,256]{3,2,1,0:T(8,128)(2,1)S(1)}, u32[]{:S(2)}, u32[]{:S(2)}) collective-permute-start(bf16[2,8,64,256]{3,2,1,0:T(8,128)(2,1)} %get-tuple-element.40), channel_id=1, source_target_pairs={{0,2},{2,4},{4,6},{6,0},{1,3},{3,5},{5,7},{7,1},{8,10},{10,12},{12... | collective-permute-start | bytes 1572872 | tf_op jit(solution)/shard_map/ppermute | solution.py:488
  34.9 26.5 %collective-permute-start.3 = (bf16[2,8,64,256]{3,2,1,0:T(8,128)(2,1)}, bf16[2,8,64,256]{3,2,1,0:T(8,128)(2,1)S(1)}, u32[]{:S(2)}, u32[]{:S(2)}) collective-permute-start(bf16[2,8,64,256]{3,2,1,0:T(8,128)(2,1)} %get-tuple-element.41), channel_id=1, source_target_pairs={{0,4},{2,6},{4,0},{6,2},{1,5},{3,7},{5,1},{7,3},{8,12},{10,14},{12... | collective-permute-start | bytes 1572872 | tf_op jit(solution)/shard_map/ppermute | solution.py:488
  37.7 24.4 %collective-permute-start.4 = (bf16[2,8,64,256]{3,2,1,0:T(8,128)(2,1)S(1)}, bf16[2,8,64,256]{3,2,1,0:T(8,128)(2,1)S(1)}, u32[]{:S(2)}, u32[]{:S(2)}) collective-permute-start(bf16[2,8,64,256]{3,2,1,0:T(8,128)(2,1)S(1)} %copy-done.15), channel_id=1, source_target_pairs={{0,6},{2,0},{4,2},{6,4},{1,7},{3,1},{5,3},{7,5},{8,14},{10,8},{12,... | collective-permute-start | bytes 1572872 | tf_op jit(solution)/shard_map/ppermute | solution.py:488
  62.6 5.8 %collective-permute-start.6 = (bf16[256,2048]{1,0:T(8,128)(2,1)S(1)}, bf16[256,2048]{1,0:T(8,128)(2,1)S(1)}, u32[]{:S(2)}, u32[]{:S(2)}) collective-permute-start(bf16[256,2048]{1,0:T(8,128)(2,1)S(1)} %get-tuple-element.46), channel_id=1, source_target_pairs={{0,64},{64,0},{1,65},{65,1},{2,66},{66,2},{3,67},{67,3},{4,68},{68... | collective-permute-start | bytes 3145736 | tf_op jit(solution)/shard_map/ppermute | solution.py:483
  62.7 9.5 %collective-permute-start.13 = (bf16[8,64,256]{2,1,0:T(8,128)(2,1)S(1)}, bf16[8,64,256]{2,1,0:T(8,128)(2,1)S(1)}, u32[]{:S(2)}, u32[]{:S(2)}) collective-permute-start(bf16[8,64,256]{2,1,0:T(8,128)(2,1)S(1)} %get-tuple-element.51), channel_id=1, source_target_pairs={{0,1},{1,0},{2,3},{3,2},{4,5},{5,4},{6,7},{7,6},{8,9},{9,8},{10,11... | collective-permute-start | bytes 786440 | tf_op jit(solution)/shard_map/ppermute | solution.py:488
  63.2 9.6 %collective-permute-start.14 = (bf16[8,64,256]{2,1,0:T(8,128)(2,1)S(1)}, bf16[8,64,256]{2,1,0:T(8,128)(2,1)S(1)}, u32[]{:S(2)}, u32[]{:S(2)}) collective-permute-start(bf16[8,64,256]{2,1,0:T(8,128)(2,1)S(1)} %get-tuple-element.53), channel_id=1, source_target_pairs={{0,2},{2,4},{4,6},{6,0},{1,3},{3,5},{5,7},{7,1},{8,10},{10,12},{12... | collective-permute-start | bytes 786440 | tf_op jit(solution)/shard_map/ppermute | solution.py:488
  64.7 14.5 %collective-permute-start.15 = (bf16[8,64,256]{2,1,0:T(8,128)(2,1)S(1)}, bf16[8,64,256]{2,1,0:T(8,128)(2,1)S(1)}, u32[]{:S(2)}, u32[]{:S(2)}) collective-permute-start(bf16[8,64,256]{2,1,0:T(8,128)(2,1)S(1)} %get-tuple-element.54), channel_id=1, source_target_pairs={{0,4},{2,6},{4,0},{6,2},{1,5},{3,7},{5,1},{7,3},{8,12},{10,14},{12... | collective-permute-start | bytes 786440 | tf_op jit(solution)/shard_map/ppermute | solution.py:488
  67.3 11.9 %collective-permute-start.16 = (bf16[8,64,256]{2,1,0:T(8,128)(2,1)S(1)}, bf16[8,64,256]{2,1,0:T(8,128)(2,1)S(1)}, u32[]{:S(2)}, u32[]{:S(2)}) collective-permute-start(bf16[8,64,256]{2,1,0:T(8,128)(2,1)S(1)} %get-tuple-element.55), channel_id=1, source_target_pairs={{0,6},{2,0},{4,2},{6,4},{1,7},{3,1},{5,3},{7,5},{8,14},{10,8},{12,... | collective-permute-start | bytes 786440 | tf_op jit(solution)/shard_map/ppermute | solution.py:488
  69.9 27.4 %collective-permute-start.7 = (bf16[256,2048]{1,0:T(8,128)(2,1)}, bf16[256,2048]{1,0:T(8,128)(2,1)}, u32[]{:S(2)}, u32[]{:S(2)}) collective-permute-start(bf16[256,2048]{1,0:T(8,128)(2,1)} %fusion.1), channel_id=1, source_target_pairs={{128,129},{129,128},{130,131},{131,130},{132,133},{133,132},{134,1... | collective-permute-start | bytes 3145736 | tf_op jit(solution)/shard_map/ppermute | solution.py:522
  80.2 25.0 %all-to-all-start = ((bf16[8,64,512]{2,1,0:T(8,128)(2,1)}), bf16[8,64,512]{2,1,0:T(8,128)(2,1)S(1)}, u32[]{:S(2)}, u32[]{:S(2)}) async-start(bf16[8,64,512]{2,1,0:T(8,128)(2,1)} %shard_map.100), calls=%async_computation.1 | async-start | bytes 1048576 | tf_op jit(solution)/shard_map/all_to_all | solution.py:492
  88.4 102.4 %all-gather.2.cloned.1.call-start = ((), (), s32[]{:S(2)}) async-start(), calls=%async_computation.4 | async-start | bytes 4718592 | tf_op jit(solution)/shard_map/all_gather | solution.py:535
  92.1 7.9 %collective-permute-start.10 = (bf16[2,64,512]{2,1,0:T(8,128)(2,1)S(1)}, bf16[2,64,512]{2,1,0:T(8,128)(2,1)S(1)}, u32[]{:S(2)}, u32[]{:S(2)}) collective-permute-start(bf16[2,64,512]{2,1,0:T(8,128)(2,1)S(1)} %bitcast.38), channel_id=1, source_target_pairs={{0,4},{2,6},{4,0},{6,2},{1,5},{3,7},{5,1},{7,3},{8,12},{10,14},{12... | collective-permute-start | bytes 393224 | tf_op jit(solution)/shard_map/ppermute | solution.py:488
  95.2 6.7 %collective-permute-start.11 = (bf16[2,64,512]{2,1,0:T(8,128)(2,1)S(1)}, bf16[2,64,512]{2,1,0:T(8,128)(2,1)S(1)}, u32[]{:S(2)}, u32[]{:S(2)}) collective-permute-start(bf16[2,64,512]{2,1,0:T(8,128)(2,1)S(1)} %bitcast.37), channel_id=1, source_target_pairs={{0,6},{2,0},{4,2},{6,4},{1,7},{3,1},{5,3},{7,5},{8,14},{10,8},{12,... | collective-permute-start | bytes 393224 | tf_op jit(solution)/shard_map/ppermute | solution.py:488
  96.4 6.2 %collective-permute-start.9 = (bf16[2,64,512]{2,1,0:T(8,128)(2,1)S(1)}, bf16[2,64,512]{2,1,0:T(8,128)(2,1)S(1)}, u32[]{:S(2)}, u32[]{:S(2)}) collective-permute-start(bf16[2,64,512]{2,1,0:T(8,128)(2,1)S(1)} %bitcast.36), channel_id=1, source_target_pairs={{0,2},{2,4},{4,6},{6,0},{1,3},{3,5},{5,7},{7,1},{8,10},{10,12},{12... | collective-permute-start | bytes 393224 | tf_op jit(solution)/shard_map/ppermute | solution.py:488
  102.6 4.4 %collective-permute-start.12 = (bf16[64,512]{1,0:T(8,128)(2,1)S(1)}, bf16[64,512]{1,0:T(8,128)(2,1)S(1)}, u32[]{:S(2)}, u32[]{:S(2)}) collective-permute-start(bf16[64,512]{1,0:T(8,128)(2,1)S(1)} %get-tuple-element.49), channel_id=1, source_target_pairs={{0,1},{1,0},{2,3},{3,2},{4,5},{5,4},{6,7},{7,6},{8,9},{9,8},{10,11... | collective-permute-start | bytes 196616 | tf_op jit(solution)/shard_map/ppermute | solution.py:488
  109.4 4.3 %collective-permute-start.25 = (bf16[64,512]{1,0:T(8,128)(2,1)S(1)}, bf16[64,512]{1,0:T(8,128)(2,1)S(1)}, u32[]{:S(2)}, u32[]{:S(2)}) collective-permute-start(bf16[64,512]{1,0:T(8,128)(2,1)S(1)} %get-tuple-element.59), channel_id=1, source_target_pairs={{0,1},{1,0},{2,3},{3,2},{4,5},{5,4},{6,7},{7,6},{8,9},{9,8},{10,11... | collective-permute-start | bytes 196616 | tf_op jit(solution)/shard_map/ppermute | solution.py:488
  113.7 6.9 %collective-permute-start.26 = (bf16[128,512]{1,0:T(8,128)(2,1)S(1)}, bf16[128,512]{1,0:T(8,128)(2,1)S(1)}, u32[]{:S(2)}, u32[]{:S(2)}) collective-permute-start(bf16[128,512]{1,0:T(8,128)(2,1)S(1)} %get-tuple-element.68), channel_id=1, source_target_pairs={{0,6},{2,0},{4,2},{6,4},{1,7},{3,1},{5,3},{7,5},{8,14},{10,8},{12,... | collective-permute-start | bytes 393224 | tf_op jit(solution)/shard_map/ppermute | solution.py:488
  115.8 7.1 %collective-permute-start.27 = (bf16[128,512]{1,0:T(8,128)(2,1)S(1)}, bf16[128,512]{1,0:T(8,128)(2,1)S(1)}, u32[]{:S(2)}, u32[]{:S(2)}) collective-permute-start(bf16[128,512]{1,0:T(8,128)(2,1)S(1)} %get-tuple-element.68), channel_id=1, source_target_pairs={{0,4},{2,6},{4,0},{6,2},{1,5},{3,7},{5,1},{7,3},{8,12},{10,14},{12... | collective-permute-start | bytes 393224 | tf_op jit(solution)/shard_map/ppermute | solution.py:488
  116.6 7.6 %collective-permute-start.28 = (bf16[128,512]{1,0:T(8,128)(2,1)S(1)}, bf16[128,512]{1,0:T(8,128)(2,1)S(1)}, u32[]{:S(2)}, u32[]{:S(2)}) collective-permute-start(bf16[128,512]{1,0:T(8,128)(2,1)S(1)} %get-tuple-element.68), channel_id=1, source_target_pairs={{0,2},{2,4},{4,6},{6,0},{1,3},{3,5},{5,7},{7,1},{8,10},{10,12},{12... | collective-permute-start | bytes 393224 | tf_op jit(solution)/shard_map/ppermute | solution.py:488
  125.1 25.8 %all-to-all-start.1 = ((bf16[8,64,512]{2,1,0:T(8,128)(2,1)}), bf16[8,64,512]{2,1,0:T(8,128)(2,1)S(1)}, u32[]{:S(2)}, u32[]{:S(2)}) async-start(bf16[8,64,512]{2,1,0:T(8,128)(2,1)} %get-tuple-element.58), calls=%async_computation.2 | async-start | bytes 1048576 | tf_op jit(solution)/shard_map/all_to_all | solution.py:492
  129.6 40.0 %collective-permute-start.8 = (bf16[256,2048]{1,0:T(8,128)(2,1)}, bf16[256,2048]{1,0:T(8,128)(2,1)}, u32[]{:S(2)}, u32[]{:S(2)}) collective-permute-start(bf16[256,2048]{1,0:T(8,128)(2,1)} %collective-permute-done.7), channel_id=1, source_target_pairs={{128,1},{129,0},{130,3},{131,2},{132,5},{133,4},{134,7},{135,6},{1... | collective-permute-start | bytes 3145736 | tf_op jit(solution)/shard_map/ppermute | solution.py:523
  150.9 6.5 %collective-permute-start.18 = (bf16[8,64,256]{2,1,0:T(8,128)(2,1)S(1)}, bf16[8,64,256]{2,1,0:T(8,128)(2,1)S(1)}, u32[]{:S(2)}, u32[]{:S(2)}) collective-permute-start(bf16[8,64,256]{2,1,0:T(8,128)(2,1)S(1)} %get-tuple-element.63), channel_id=1, source_target_pairs={{0,1},{1,0},{2,3},{3,2},{4,5},{5,4},{6,7},{7,6},{8,9},{9,8},{10,11... | collective-permute-start | bytes 786440 | tf_op jit(solution)/shard_map/ppermute | solution.py:488
  151.4 11.1 %collective-permute-start.23 = (bf16[8,64,256]{2,1,0:T(8,128)(2,1)S(1)}, bf16[8,64,256]{2,1,0:T(8,128)(2,1)S(1)}, u32[]{:S(2)}, u32[]{:S(2)}) collective-permute-start(bf16[8,64,256]{2,1,0:T(8,128)(2,1)S(1)} %get-tuple-element.62), channel_id=1, source_target_pairs={{0,2},{2,4},{4,6},{6,0},{1,3},{3,5},{5,7},{7,1},{8,10},{10,12},{12... | collective-permute-start | bytes 786440 | tf_op jit(solution)/shard_map/ppermute | solution.py:488
  151.4 11.1 %collective-permute-start.22 = (bf16[8,64,256]{2,1,0:T(8,128)(2,1)S(1)}, bf16[8,64,256]{2,1,0:T(8,128)(2,1)S(1)}, u32[]{:S(2)}, u32[]{:S(2)}) collective-permute-start(bf16[8,64,256]{2,1,0:T(8,128)(2,1)S(1)} %get-tuple-element.62), channel_id=1, source_target_pairs={{0,4},{2,6},{4,0},{6,2},{1,5},{3,7},{5,1},{7,3},{8,12},{10,14},{12... | collective-permute-start | bytes 786440 | tf_op jit(solution)/shard_map/ppermute | solution.py:488
  151.7 11.4 %collective-permute-start.21 = (bf16[8,64,256]{2,1,0:T(8,128)(2,1)S(1)}, bf16[8,64,256]{2,1,0:T(8,128)(2,1)S(1)}, u32[]{:S(2)}, u32[]{:S(2)}) collective-permute-start(bf16[8,64,256]{2,1,0:T(8,128)(2,1)S(1)} %get-tuple-element.62), channel_id=1, source_target_pairs={{0,6},{2,0},{4,2},{6,4},{1,7},{3,1},{5,3},{7,5},{8,14},{10,8},{12,... | collective-permute-start | bytes 786440 | tf_op jit(solution)/shard_map/ppermute | solution.py:488
  164.2 31.3 %collective-permute-start.24 = (bf16[4,8,64,256]{3,2,1,0:T(8,128)(2,1)}, bf16[4,8,64,256]{3,2,1,0:T(8,128)(2,1)}, u32[]{:S(2)}, u32[]{:S(2)}) collective-permute-start(bf16[4,8,64,256]{3,2,1,0:T(8,128)(2,1)} %shard_map.104.refs_1_), channel_id=1, source_target_pairs={{0,1},{1,0},{2,3},{3,2},{4,5},{5,4},{6,7},{7,6},{8,9},{9,8},{10,11... | collective-permute-start | bytes 3145736 | tf_op jit(solution)/shard_map/ppermute | solution.py:488
  165.8 23.5 %collective-permute-start.29 = (bf16[2,8,64,256]{3,2,1,0:T(8,128)(2,1)}, bf16[2,8,64,256]{3,2,1,0:T(8,128)(2,1)S(1)}, u32[]{:S(2)}, u32[]{:S(2)}) collective-permute-start(bf16[2,8,64,256]{3,2,1,0:T(8,128)(2,1)} %shard_map.103.refs_0_), channel_id=1, source_target_pairs={{0,2},{2,4},{4,6},{6,0},{1,3},{3,5},{5,7},{7,1},{8,10},{10,12},{12... | collective-permute-start | bytes 1572872 | tf_op jit(solution)/shard_map/ppermute | solution.py:488
  166.0 29.5 %collective-permute-start.20 = (bf16[2,8,64,256]{3,2,1,0:T(8,128)(2,1)}, bf16[2,8,64,256]{3,2,1,0:T(8,128)(2,1)}, u32[]{:S(2)}, u32[]{:S(2)}) collective-permute-start(bf16[2,8,64,256]{3,2,1,0:T(8,128)(2,1)} %shard_map.103.refs_0_), channel_id=1, source_target_pairs={{0,4},{2,6},{4,0},{6,2},{1,5},{3,7},{5,1},{7,3},{8,12},{10,14},{12... | collective-permute-start | bytes 1572872 | tf_op jit(solution)/shard_map/ppermute | solution.py:488
  169.6 25.9 %collective-permute-start.19 = (bf16[2,8,64,256]{3,2,1,0:T(8,128)(2,1)}, bf16[2,8,64,256]{3,2,1,0:T(8,128)(2,1)}, u32[]{:S(2)}, u32[]{:S(2)}) collective-permute-start(bf16[2,8,64,256]{3,2,1,0:T(8,128)(2,1)} %shard_map.103.refs_0_), channel_id=1, source_target_pairs={{0,6},{2,0},{4,2},{6,4},{1,7},{3,1},{5,3},{7,5},{8,14},{10,8},{12,... | collective-permute-start | bytes 1572872 | tf_op jit(solution)/shard_map/ppermute | solution.py:488
  (18 other events, 140.1 us)
Sparse Core Ops, SparseCore 0:
  32.7 58.2 reduce-scatter.1
  125.2 58.2 all-gather.1
